TPU v7x, 256 devices: a whole 4x4x8 slice. The times are simulated.
256 devices in a mesh: dp: 32 (over z_hi, y, core), ctr: 8 (over z_lo, x).
Axes of the slice: x: 4, y: 4, z: 8 (z_hi: 4, z_lo: 2; z = z_hi * 2 + z_lo), core: 2. Of those that a mesh axis runs over, the one named last changes fastest.
Arguments:
- points: bfloat16 [65536, 128], P(('dp', 'ctr')), may hold values from -6 to 6
- adjoint_rows: bfloat16 [65536, 32], P(('dp', 'ctr')), may hold values from -8 to 8
- centers: bfloat16 [32768, 128], P(('dp', 'ctr')), may hold values from -6 to 6
- solution_rows: bfloat16 [32768, 32], P(('dp', 'ctr')), may hold values from -8 to 8
- center_left: bfloat16 [32768, 32], P(('dp', 'ctr')), may hold values from -8 to 8
- center_right: bfloat16 [32768, 32], P(('dp', 'ctr')), may hold values from -8 to 8
- lengthscale: float32 [128], replicated, may hold values from 6 to 24
Outputs:
- grad_centers: float32 [32768, 128], P(('dp', 'ctr'))
- grad_scale: float32 [128], replicated
All inputs are finite; a program needn't handle non-finite values.
Results may differ from a plain program's by a relative error of at most 0.0047.
Values may be sent and summed in bfloat16 or wider, within the bound.
No kernel may reach another device: no remote copies, remote signals or barrier semaphores. Data moves between devices by JAX's collectives and lax.ppermute only.
A program may use at most 64 MiB of HBM per device.

v0:
```python
import math

import jax
import jax.numpy as jnp
from jax import lax
from jax.sharding import PartitionSpec as P


def gauss(left, left_sq, right, right_sq):
    cross = jnp.dot(left, right.T, preferred_element_type=jnp.float32)
    return jnp.exp(-0.5 * (left_sq[:, None] + right_sq[None, :] - 2.0 * cross))


def local(points, adjoint_rows, centers, solution_rows, center_left, center_right, lengthscale):
    scaled_x = (points.astype(jnp.float32) / lengthscale).astype(jnp.bfloat16)
    scaled_c = (centers.astype(jnp.float32) / lengthscale).astype(jnp.bfloat16)
    block_c, block_u, block_a = (
        lax.all_gather(scaled_c, "dp", axis=0, tiled=True),
        lax.all_gather(solution_rows, "dp", axis=0, tiled=True),
        lax.all_gather(center_left, "dp", axis=0, tiled=True),
    )
    partner_c, partner_b = (
        lax.all_gather(scaled_c, "ctr", axis=0, tiled=True),
        lax.all_gather(center_right, "ctr", axis=0, tiled=True),
    )
    block_f = block_c.astype(jnp.float32)
    block_sq = jnp.sum(block_f * block_f, 1)
    partner_f = partner_c.astype(jnp.float32)
    partner_sq = jnp.sum(partner_f * partner_f, 1)
    width = block_c.shape[1]
    block_rows = block_c.shape[0]
    sub_rows = math.gcd(block_rows, 256)
    sub_count = block_rows // sub_rows
    g_acc = jnp.zeros((block_rows, width), jnp.float32)
    col_acc = jnp.zeros((block_rows,), jnp.float32)
    ell_acc = jnp.zeros((width,), jnp.float32)
    xpiece = lax.all_gather(scaled_x, "ctr", axis=0, tiled=True)
    vpiece = lax.all_gather(adjoint_rows, "ctr", axis=0, tiled=True)
    xpiece_f = xpiece.astype(jnp.float32)
    xpiece_sq = xpiece_f * xpiece_f
    xnorms = jnp.sum(xpiece_sq, 1)

    def center_step(ell_run, item):
        cpart, upart, csq_part, gpart, colpart = item
        kern = gauss(xpiece, xnorms, cpart, csq_part)
        weight = kern * jnp.dot(vpiece, upart.T, preferred_element_type=jnp.float32)
        rounded = weight.astype(jnp.bfloat16)
        gpart = gpart + jnp.dot(rounded.T, xpiece, preferred_element_type=jnp.float32)
        colpart = colpart + jnp.sum(weight, 0)
        ell_run = ell_run + jnp.sum(jnp.sum(weight, 1)[:, None] * xpiece_sq, 0)
        return (ell_run, (gpart, colpart))

    ell_acc, (g_new, col_new) = lax.scan(
        center_step,
        ell_acc,
        (
            block_c.reshape(sub_count, sub_rows, width),
            block_u.reshape(sub_count, sub_rows, -1),
            block_sq.reshape(sub_count, sub_rows),
            g_acc.reshape(sub_count, sub_rows, width),
            col_acc.reshape(sub_count, sub_rows),
        ),
    )
    data_g, data_col, ell_acc = (
        g_new.reshape(block_rows, width),
        col_new.reshape(block_rows),
        ell_acc,
    )

    def pair_step(carry, item):
        col_g, col_q = carry
        cpart, apart, csq_part = item
        kern = gauss(cpart, csq_part, partner_c, partner_sq)
        weight = kern * jnp.dot(apart, partner_b.T, preferred_element_type=jnp.float32)
        rounded = weight.astype(jnp.bfloat16)
        row_g = jnp.dot(rounded, partner_c, preferred_element_type=jnp.float32)
        row_q = jnp.sum(weight, 1)
        col_g = col_g + jnp.dot(rounded.T, cpart, preferred_element_type=jnp.float32)
        col_q = col_q + jnp.sum(weight, 0)
        return ((col_g, col_q), (row_g, row_q))

    partner_rows = partner_c.shape[0]
    pair_init = (
        jnp.zeros((partner_rows, width), jnp.float32),
        jnp.zeros((partner_rows,), jnp.float32),
    )
    (col_g, col_q), (row_g, row_q) = lax.scan(
        pair_step,
        pair_init,
        (
            block_c.reshape(sub_count, sub_rows, width),
            block_a.reshape(sub_count, sub_rows, -1),
            block_sq.reshape(sub_count, sub_rows),
        ),
    )
    row_g = row_g.reshape(block_rows, width)
    row_q = row_q.reshape(block_rows)
    block_q = data_col + row_q
    block_term = (data_g + row_g - block_q[:, None] * block_f) / lengthscale
    partner_term = (col_g - col_q[:, None] * partner_f) / lengthscale
    scale_part = (
        ell_acc
        + jnp.sum(block_q[:, None] * block_f * block_f, 0)
        - 2.0 * jnp.sum(block_f * (data_g + row_g), 0)
    )
    scale_part = scale_part + jnp.sum(col_q[:, None] * partner_f * partner_f, 0)
    own_rows = centers.shape[0]
    block_full = lax.psum(block_term, "dp")
    block_own = lax.dynamic_slice_in_dim(block_full, lax.axis_index("dp") * own_rows, own_rows, 0)
    partner_full = lax.psum(partner_term, "ctr")
    partner_own = lax.dynamic_slice_in_dim(
        partner_full, lax.axis_index("ctr") * own_rows, own_rows, 0
    )
    scale_total = lax.psum(scale_part, ("dp", "ctr"))
    return (block_own + partner_own, scale_total / lengthscale)


def solution(mesh):
    in_specs = (
        P(("dp", "ctr"), None),
        P(("dp", "ctr"), None),
        P(("dp", "ctr"), None),
        P(("dp", "ctr"), None),
        P(("dp", "ctr"), None),
        P(("dp", "ctr"), None),
        P(),
    )
    out_specs = (P(("dp", "ctr"), None), P())
    return jax.shard_map(local, mesh=mesh, in_specs=in_specs, out_specs=out_specs, check_vma=False)
```

profile of v0, /device:TPU:1, one launch (start us, length us, event | category | flops | bytes accessed | tf_op | source)
XLA Modules:
  0.0 679.3 jit_solution(3950751126253922817)
XLA Ops:
  7.2 1.4 divide_convert_fusion.1
  8.7 50.0 %all_gather.26 = bf16[4096,32]{0,1:T(8,128)(2,1)S(1)} all-gather(bf16[128,32]{0,1:T(8,128)(2,1)} %param.15), channel_id=1, replica_groups=mesh['dp'=32,'ctr'=8] {'dp'}, dimensions={0}, use_global_device_ids=true | all-gather | bytes 270336 | tf_op jit(solution)/shard_map/all_gather | solution.py:20
  60.9 40.1 %all_gather.23 = bf16[4096,32]{0,1:T(8,128)(2,1)S(1)} all-gather(bf16[128,32]{0,1:T(8,128)(2,1)} %param.14), channel_id=1, replica_groups=mesh['dp'=32,'ctr'=8] {'dp'}, dimensions={0}, use_global_device_ids=true | all-gather | bytes 270336 | tf_op jit(solution)/shard_map/all_gather | solution.py:19
  102.5 24.0 %all_gather.27 = bf16[1024,32]{1,0:T(8,128)(2,1)} all-gather(bf16[128,32]{1,0:T(8,128)(2,1)S(1)} %copy.12), channel_id=1, replica_groups=mesh['dp'=32,'ctr'=8] {'ctr'}, dimensions={0}, use_global_device_ids=true | all-gather | bytes 73728 | tf_op jit(solution)/shard_map/all_gather | solution.py:24
  126.5 23.2 %all_gather.24 = bf16[2048,32]{1,0:T(8,128)(2,1)S(1)} all-gather(bf16[256,32]{1,0:T(8,128)(2,1)S(1)} %copy.10), channel_id=1, replica_groups=mesh['dp'=32,'ctr'=8] {'ctr'}, dimensions={0}, use_global_device_ids=true | all-gather | bytes 147456 | tf_op jit(solution)/shard_map/all_gather | solution.py:38
  149.7 22.4 %all_gather.25 = bf16[1024,128]{1,0:T(8,128)(2,1)S(1)} all-gather(bf16[128,128]{1,0:T(8,128)(2,1)S(1)} %copy-done), channel_id=1, replica_groups=mesh['dp'=32,'ctr'=8] {'ctr'}, dimensions={0}, use_global_device_ids=true | all-gather | bytes 294912 | tf_op jit(solution)/shard_map/all_gather | solution.py:23
  172.4 23.2 %all_gather.21 = bf16[2048,128]{1,0:T(8,128)(2,1)S(1)} all-gather(bf16[256,128]{1,0:T(8,128)(2,1)S(1)} %divide_convert_fusion), channel_id=1, replica_groups=mesh['dp'=32,'ctr'=8] {'ctr'}, dimensions={0}, use_global_device_ids=true | all-gather | bytes 589824 | tf_op jit(solution)/shard_map/all_gather | solution.py:37
  196.0 1.8 fusion.31
  197.9 1.5 broadcast.33.clone
  199.4 78.5 %while.33 = (s32[]{:T(128)}, f32[1024,128]{1,0:T(8,128)S(1)}, f32[1024]{0:T(1024)S(1)}, f32[16,256,128]{2,1,0:T(8,128)}, f32[16,256]{1,0:T(8,128)S(1)}, /*index=...) while((s32[]{:T(128)}, f32[1024,128]{1,0:T(8,128)S(1)}, ...), condition=%wide.region_11.12_spmd.clone, body=%wide.region_8.11_spmd.clone.sunk | while | flops 220463872 | bytes 5859496 | solution.py:87
  200.6 1.4 fusion.86
  205.5 1.4 fusion.86
  210.4 1.4 fusion.86
  215.3 1.4 fusion.86
  225.1 1.4 fusion.86
  230.1 1.4 fusion.86
  235.0 1.4 fusion.86
  239.9 1.4 fusion.86
  244.8 1.4 fusion.86
  249.7 1.4 fusion.86
  254.6 1.4 fusion.86
  259.5 1.4 fusion.86
  264.4 1.4 fusion.86
  269.3 1.4 fusion.86
  274.2 1.4 fusion.86
  279.0 1.6 broadcast.33.clone.1
  280.6 68.8 %while.32 = (s32[]{:T(128)}, f32[128]{0:T(128)S(1)}, f32[16,256,128]{2,1,0:T(8,128)}, f32[16,256]{1,0:T(8,128)S(1)}, f32[2048]{0:T(1024)S(1)}, /*index=5*/f32[16...) while((s32[]{:T(128)}, f32[128]{0:T(128)S(1)}, ...), condition=%wide.region_6.7_spmd.clone, body=%wide.region_2.6_spmd.clone.sunk | while | flops 306706304 | bytes 8814755 | solution.py:53
  280.6 1.4 fusion.74
  282.0 1.4 fusion.75
  284.9 1.4 fusion.74
  286.3 1.4 fusion.75
  289.2 1.4 fusion.74
  290.6 1.4 fusion.75
  293.5 1.4 fusion.74
  294.9 1.4 fusion.75
  297.8 1.4 fusion.74
  299.2 1.4 fusion.75
  302.1 1.4 fusion.74
  303.5 1.4 fusion.75
  306.4 1.4 fusion.74
  307.8 1.4 fusion.75
  310.7 1.4 fusion.74
  312.1 1.4 fusion.75
  315.0 1.4 fusion.74
  316.4 1.4 fusion.75
  319.3 1.4 fusion.74
  320.7 1.4 fusion.75
  323.6 1.4 fusion.74
  325.0 1.4 fusion.75
  327.9 1.4 fusion.74
  329.3 1.4 fusion.75
  332.2 1.4 fusion.74
  333.6 1.4 fusion.75
  336.5 1.4 fusion.74
  337.9 1.4 fusion.75
  340.8 1.4 fusion.74
  342.2 1.4 fusion.75
  345.1 1.4 fusion.74
  346.5 1.4 fusion.75
  349.4 2.5 add.85
  351.9 2.8 fusion.32
  354.8 97.6 %psum.23 = f32[128]{0:T(128)S(1)} all-reduce(f32[128]{0:T(128)S(1)} %subtract_add_fusion), channel_id=1, replica_groups=mesh['dp'=32,'ctr'=8] {'dp','ctr'}, use_global_device_ids=true, to_apply=%region_17.18 | all-reduce | flops 128 | bytes 1024 | tf_op jit(solution)/shard_map/psum | solution.py:114
  452.9 218.4 %all-reduce.3.cloned.1.call-done = f32[4096,128]{1,0:T(8,128)} async-done(((f32[4096,128]{1,0:T(8,128)}), f32[4096,128]{1,0:T(8,128)}) %all-reduce.3.cloned.1.call-update) | async-done | bytes 2097168 | tf_op jit(solution)/shard_map/psum | solution.py:108
  671.3 1.5 dynamic-slice_add_fusion
  (211 shorter events, 86.7 us)
Async XLA Ops:
  7.2 95.2 %copy-start.2 = (bf16[256,32]{0,1:T(8,128)(2,1)S(1)}, bf16[256,32]{0,1:T(8,128)(2,1)}, u32[]{:S(2)}) copy-start(bf16[256,32]{0,1:T(8,128)(2,1)} %param.12) | copy-start | bytes 49156
  7.2 188.8 %all-gather.2.cloned.1.call-start = ((), (), s32[]{:S(2)}) async-start(), calls=%async_computation | async-start | bytes 1081344 | tf_op jit(solution)/shard_map/all_gather | solution.py:18
  8.6 141.1 %copy-start = (bf16[128,128]{1,0:T(8,128)(2,1)S(1)}, bf16[128,128]{1,0:T(8,128)(2,1)}, u32[]{:S(2)}) copy-start(bf16[128,128]{1,0:T(8,128)(2,1)} %divide_convert_fusion.1) | copy-start | bytes 98308
  8.6 444.3 %all-reduce.5.cloned.1.call-start = ((), (), s32[]{:S(2)}) async-start(), calls=%async_computation.2 | async-start | bytes 1048576 | tf_op jit(solution)/shard_map/psum | solution.py:110
  58.7 113.6 %copy-start.1 = (bf16[256,128]{1,0:T(8,128)(2,1)S(1)}, bf16[256,128]{1,0:T(8,128)(2,1)}, u32[]{:S(2)}) copy-start(bf16[256,128]{1,0:T(8,128)(2,1)} %param.11) | copy-start | bytes 196612
  58.7 113.7 %copy-start.3 = (f32[128]{0:T(128)S(1)}, f32[128]{0:T(128)}, u32[]{:S(2)}) copy-start(f32[128]{0:T(128)} %param.17) | copy-start | bytes 1540
  279.0 392.3 %all-reduce.3.cloned.1.call-start = ((), (), s32[]{:S(2)}) async-start(), calls=%async_computation.1 | async-start | bytes 4194304 | tf_op jit(solution)/shard_map/psum | solution.py:108
Sparse Core Ops, SparseCore 0:
  11.1 56.3 all-gather.1
  279.1 93.3 all-reduce.4
  375.3 295.9 all-reduce.2
where the time goes:
time: 683 us; the launch traced here: 679 us
  blocking collectives  281 us (41%)
  waiting for transfers between devices  218 us (32%)
  matrix products  139 us (20%)
  other arithmetic  18.1 us (3%)
  between operations  13.9 us (2%)
  local copies, waits for them, and re-layouts  7.84 us (1%)
    psum x1, waiting for transfers between devices, local(): block_full = lax.psum(block_term, 'dp')  218 us
    psum x1, blocking collectives, local(): scale_total = lax.psum(scale_part, ('dp', 'ctr'))  97.6 us
    all_gather x1, blocking collectives, local(): lax.all_gather(center_left, 'dp', axis=0, tiled=True)  50 us
    dot_general x32, matrix products, gauss(): cross = jnp.dot(left, right.T, preferred_element_type=jnp.float32)  41.9 us
    all_gather x1, blocking collectives, local(): lax.all_gather(solution_rows, 'dp', axis=0, tiled=True)  40.1 us
    all_gather x1, blocking collectives, local(): lax.all_gather(center_right, 'ctr', axis=0, tiled=True)  24 us
    all_gather x1, blocking collectives, local(): vpiece = lax.all_gather(adjoint_rows, 'ctr', axis=0, tiled=True)  23.2 us
    all_gather x1, blocking collectives, local(): xpiece = lax.all_gather(scaled_x, 'ctr', axis=0, tiled=True)  23.2 us
  transfers between devices with their start and end apart: 3, of which 1 were waited for; matrix products, arithmetic and copies ran while one was open for 12% of the time, Pallas kernels for 0%

commit v1 on v0

v1 whole, which is shorter than its diff:
```python
import functools

import jax
import jax.numpy as jnp
from jax import lax
from jax.experimental import pallas as pl
from jax.experimental.pallas import tpu as pltpu
from jax.sharding import Mesh, PartitionSpec as P

BF = jnp.bfloat16
F32 = jnp.float32
AXES = ("zh", "y", "core", "zl", "x")
SIZES = (4, 4, 2, 2, 4)
CENTER_AXES = ("zl", "x")
PARTNER_AXES = ("zh", "y")
D = 128
R = 32
PTS = 256
CTR = 128
CROWS = CTR + 3 * R
PROWS = PTS + CTR + 4 * R
TROWS = CTR + 8


def dot_nt(a, b):
    return lax.dot_general(a, b, (((1,), (1,)), ((), ())), preferred_element_type=F32)


def dot_nn(a, b):
    return lax.dot_general(a, b, (((1,), (0,)), ((), ())), preferred_element_type=F32)


def prep_kernel(x_ref, v_ref, c_ref, s_ref, l_ref, r_ref, ls_ref, pp_ref, cp_ref, pbuf, cbuf, sem, *, np_, nc):
    ls = ls_ref[...]
    pbuf[0:PTS, :] = (x_ref[...].astype(F32) / ls).astype(BF)
    c = (c_ref[...].astype(F32) / ls).astype(BF)
    pbuf[PTS : PTS + CTR, :] = c
    cbuf[0:CTR, :] = c
    base = PTS + CTR
    vt = v_ref[...].astype(F32).T.astype(BF)
    pbuf[base : base + R, :] = vt[:, 0:CTR]
    pbuf[base + R : base + 2 * R, :] = vt[:, CTR : 2 * CTR]
    lt = l_ref[...].astype(F32).T.astype(BF)
    rt = r_ref[...].astype(F32).T.astype(BF)
    pbuf[base + 2 * R : base + 3 * R, :] = rt
    pbuf[base + 3 * R : base + 4 * R, :] = lt
    cbuf[CTR : CTR + R, :] = s_ref[...].astype(F32).T.astype(BF)
    cbuf[CTR + R : CTR + 2 * R, :] = lt
    cbuf[CTR + 2 * R : CTR + 3 * R, :] = rt
    copies = [pltpu.make_async_copy(cbuf, cp_ref.at[i], sem.at[i]) for i in range(nc)]
    copies += [pltpu.make_async_copy(pbuf, pp_ref.at[i], sem.at[nc + i]) for i in range(np_)]
    for cp in copies:
        cp.start()
    for cp in copies:
        cp.wait()


def tail_columns(f, swap):
    n = f.shape[0]
    ff = f.astype(F32)
    h = -0.5 * jnp.sum(ff * ff, axis=1, keepdims=True)
    a = h.astype(BF).astype(F32)
    rest = h - a
    b = rest.astype(BF).astype(F32)
    c = rest - b
    lane = lax.broadcasted_iota(jnp.int32, (n, 128), 1)
    o, one = (3, 0) if swap else (0, 3)
    t = jnp.where((lane >= one) & (lane < one + 3), 1.0, 0.0)
    t = jnp.where(lane == o + 2, c, t)
    t = jnp.where(lane == o + 1, b, t)
    t = jnp.where(lane == o, a, t)
    return t.astype(BF)


def main_kernel(own_ref, oth_ref, pp_ref, ls_ref, t_ref, ca, us, ul, gd, gp, qa, ell):
    nc = own_ref.shape[0]
    npeer = pp_ref.shape[0]
    m = 2 * nc * CTR
    lane = lax.broadcasted_iota(jnp.int32, (CTR, 128), 1)
    for j in range(2 * nc):
        ref, k = (own_ref, j) if j < nc else (oth_ref, j - nc)
        rows = slice(j * CTR, (j + 1) * CTR)
        c = ref[k, 0:CTR, :]
        ca[rows, 0:D] = c
        ca[rows, D : 2 * D] = tail_columns(c, False)
        ut = jnp.concatenate([ref[k, CTR:CROWS, :], jnp.zeros((R, 128), BF)], 0)
        u = ut.astype(F32).T
        us[rows, :] = jnp.where(lane < R, u, 0.0).astype(BF)
        ul[rows, :] = jnp.where((lane >= R) & (lane < 3 * R), u, 0.0).astype(BF)
    gd[...] = jnp.zeros_like(gd)
    gp[...] = jnp.zeros_like(gp)
    qa[...] = jnp.zeros_like(qa)
    ell[...] = jnp.zeros_like(ell)

    def sweep(x, vt, u_ref, g_ref):
        n = x.shape[0]
        xt = jnp.concatenate([x, tail_columns(x, True)], 1)
        kern = jnp.exp(dot_nt(ca[...], xt))
        w = kern * dot_nn(u_ref[...], vt)
        g_ref[...] += dot_nn(w.astype(BF), x)
        s = w[:, 0:128]
        for k in range(1, n // 128):
            s = s + w[:, k * 128 : (k + 1) * 128]
        qa[...] += s
        return w

    def step(a, carry):
        ia, ib = 2 * a, 2 * a + 1
        base = PTS + CTR
        x = jnp.concatenate([pp_ref[ia, 0:PTS, :], pp_ref[ib, 0:PTS, :]], 0)
        vt = jnp.concatenate(
            [pp_ref[i, base + k * R : base + (k + 1) * R, :] for i in (ia, ib) for k in (0, 1)], 1
        )
        vt = jnp.concatenate([vt, jnp.zeros((3 * R, 2 * PTS), BF)], 0)
        w = sweep(x, vt, us, gd)
        rowsum = jnp.sum(w.reshape(m // 8, 8, 2 * PTS), axis=0)
        r1 = rowsum.astype(BF)
        rest = rowsum - r1.astype(F32)
        r2 = rest.astype(BF)
        r3 = (rest - r2.astype(F32)).astype(BF)
        xf = x.astype(F32)
        xsq = xf * xf
        xh = xsq.astype(BF)
        xl = (xsq - xh.astype(F32)).astype(BF)
        ell[...] += dot_nn(
            jnp.concatenate([r1, r2, r3, jnp.zeros_like(r1)], 0), jnp.concatenate([xh, xl], 1)
        )
        c = jnp.concatenate([pp_ref[ia, PTS:base, :], pp_ref[ib, PTS:base, :]], 0)
        z = jnp.zeros((R, 2 * CTR), BF)
        vc = jnp.concatenate([pp_ref[ia, base + 2 * R : PROWS, :], pp_ref[ib, base + 2 * R : PROWS, :]], 1)
        sweep(c, jnp.concatenate([z, vc, z], 0), ul, gp)
        return carry

    lax.fori_loop(0, npeer // 2, step, 0)

    e = ell[...]
    e = e[:, 0:128] + e[:, 128:256]
    scale = e[0:8] + e[8:16] + e[16:24]
    ls = ls_ref[...]
    for j in range(2 * nc):
        rows = slice(j * CTR, (j + 1) * CTR)
        c = ca[rows, 0:D].astype(F32)
        q = jnp.sum(qa[rows, :], axis=1, keepdims=True)
        g1 = gd[rows, :]
        g = g1 + gp[rows, :]
        qc = q * c
        t_ref[j // nc, j % nc, 0:CTR, :] = (g - qc) / ls
        part = c * (qc - (g + g1))
        scale = scale + jnp.sum(part.reshape(CTR // 8, 8, D), axis=0)
    for j in range(2 * nc):
        t_ref[j // nc, j % nc, CTR:TROWS, :] = scale


def local(points, adjoint_rows, centers, solution_rows, center_left, center_right, lengthscale):
    size = dict(zip(AXES, SIZES))
    nc = size["zl"] * size["x"]
    npeer = size["zh"] * size["y"]
    ls = lengthscale.reshape(1, D)
    vm = pl.BlockSpec(memory_space=pltpu.VMEM)
    hbm = pl.BlockSpec(memory_space=pl.ANY)
    pp, cp = pl.pallas_call(
        functools.partial(prep_kernel, np_=npeer, nc=nc),
        out_shape=[
            jax.ShapeDtypeStruct((npeer, PROWS, D), BF),
            jax.ShapeDtypeStruct((nc, CROWS, D), BF),
        ],
        in_specs=[vm] * 7,
        out_specs=[hbm, hbm],
        scratch_shapes=[
            pltpu.VMEM((PROWS, D), BF),
            pltpu.VMEM((CROWS, D), BF),
            pltpu.SemaphoreType.DMA((npeer + nc,)),
        ],
        name="prep",
    )(points, adjoint_rows, centers, solution_rows, center_left, center_right, ls)
    own = lax.all_to_all(cp, CENTER_AXES, 0, 0, tiled=True)
    oth = lax.ppermute(own, "core", [(0, 1), (1, 0)])
    partners = lax.all_to_all(pp, PARTNER_AXES, 0, 0, tiled=True)
    m = 2 * nc * CTR
    terms = pl.pallas_call(
        main_kernel,
        out_shape=jax.ShapeDtypeStruct((2, nc, TROWS, D), F32),
        in_specs=[vm] * 4,
        out_specs=vm,
        scratch_shapes=[
            pltpu.VMEM((m, 2 * D), BF),
            pltpu.VMEM((m, D), BF),
            pltpu.VMEM((m, D), BF),
            pltpu.VMEM((m, D), F32),
            pltpu.VMEM((m, D), F32),
            pltpu.VMEM((m, D), F32),
            pltpu.VMEM((32, 2 * D), F32),
        ],
        compiler_params=pltpu.CompilerParams(vmem_limit_bytes=48 * 2**20),
        name="pairs",
    )(own, oth, partners, ls)
    both = terms[0] + lax.ppermute(terms[1], "core", [(0, 1), (1, 0)])
    parts = lax.all_to_all(both, CENTER_AXES, 0, 0, tiled=True)
    total = jnp.sum(parts, 0)
    grad_centers = total[0:CTR]
    tiny = jnp.broadcast_to(total[CTR:TROWS][None], (npeer, 8, D))
    scale = jnp.sum(lax.all_to_all(tiny, PARTNER_AXES, 0, 0, tiled=True), (0, 1))
    return grad_centers, scale / lengthscale


def solution(mesh):
    grid = Mesh(mesh.devices.reshape(SIZES), AXES)
    rows = P(AXES, None)
    return jax.shard_map(
        local,
        mesh=grid,
        in_specs=(rows,) * 6 + (P(),),
        out_specs=(rows, P()),
        check_vma=False,
    )
```

time: 683 us -> 143 us (0.21)
  blocking collectives: 281 us -> 37.6 us
  waiting for transfers between devices: 218 us -> 46 us
  matrix products: 139 us -> 0 us
  Pallas kernels: 0 us -> 27.2 us
  starting transfers between devices: 0.12 us -> 23.1 us
  other arithmetic: 18.1 us -> 0.64 us
  between operations: 13.9 us -> 0.69 us
    psum x2 -> x0, waiting for transfers between devices: 218 us -> none  [the longest x1 218 us: local(): block_full = lax.psum(block_term, 'dp')]
    all_gather x6 -> x0, blocking collectives: 183 us -> none  [the longest x1 50 us: local(): lax.all_gather(center_left, 'dp', axis=0, tiled=True)]
    dot_general x112 -> x0, matrix products: 139 us -> none  [the longest x32 41.9 us: gauss(): cross = jnp.dot(left, right.T, preferred_element_type=jnp.float32)]
    psum x1 -> x0, blocking collectives: 97.6 us -> none  [local(): scale_total = lax.psum(scale_part, ('dp', 'ctr'))]
    all_to_all x0 -> x2, waiting for transfers between devices: none -> 42.9 us  [the longest x1 34.6 us: local(): partners = lax.all_to_all(pp, PARTNER_AXES, 0, 0, tiled=True)]
    all_to_all x0 -> x2, blocking collectives: none -> 37.6 us  [the longest x1 23.4 us: local(): parts = lax.all_to_all(both, CENTER_AXES, 0, 0, tiled=True)]
    pallas_call x0 -> x2, Pallas kernels: none -> 27.2 us  [the longest x1 24.5 us: local(): pl.pallas_call(main_kernel, out_shape=jax.ShapeDtypeStruct((2, nc, TROWS,...]
    all_to_all x0 -> x2, starting transfers between devices: none -> 14.1 us  [the longest x1 10.2 us: local(): partners = lax.all_to_all(pp, PARTNER_AXES, 0, 0, tiled=True)]
  transfers between devices with their start and end apart: 3 -> 4, of which waited for: 1 -> 4; matrix products, arithmetic and copies ran while one was open for 12% -> 0% of each run, Pallas kernels for 0% -> 0%
where the time goes in v1:
time: 143 us; the launch traced here: 142 us
  waiting for transfers between devices  46 us (32%)
  blocking collectives  37.6 us (26%)
  Pallas kernels  27.2 us (19%)
  starting transfers between devices  23.1 us (16%)
  local copies, waits for them, and re-layouts  6.96 us (5%)
    all_to_all x1, waiting for transfers between devices, local(): partners = lax.all_to_all(pp, PARTNER_AXES, 0, 0, tiled=True)  34.6 us
    pallas_call x1, Pallas kernels, local(): pl.pallas_call(main_kernel, out_shape=jax.ShapeDtypeStruct((2, nc, TROWS,...  24.5 us
    all_to_all x1, blocking collectives, local(): parts = lax.all_to_all(both, CENTER_AXES, 0, 0, tiled=True)  23.4 us
    all_to_all x1, blocking collectives, local(): own = lax.all_to_all(cp, CENTER_AXES, 0, 0, tiled=True)  14.2 us
    all_to_all x1, starting transfers between devices, local(): partners = lax.all_to_all(pp, PARTNER_AXES, 0, 0, tiled=True)  10.2 us
    all_to_all x1, waiting for transfers between devices, local(): lax.all_to_all(tiny, PARTNER_AXES, 0, 0, tiled=True)  8.3 us
    ppermute x1, starting transfers between devices, local(): both = terms[0] + lax.ppermute(terms[1], 'core', [(0, 1), (1, 0)])  6.32 us
    unnamed x6, local copies, waits for them, and re-layouts  5.67 us
  transfers between devices with their start and end apart: 4, of which 4 were waited for; matrix products, arithmetic and copies ran while one was open for 0% of the time, Pallas kernels for 0%

profile of v1, /device:TPU:1, one launch (start us, length us, event | category | flops | bytes accessed | tf_op | source)
XLA Modules:
  0.0 142.2 jit_solution(3150158967832810263)
XLA Ops:
  0.6 1.4 copy.14.s_ref
  2.0 1.4 copy.15.l_ref
  3.4 1.4 copy.16.r_ref
  4.8 1.4 %copy.13.v_ref = bf16[256,32]{1,0:T(8,128)(2,1)} copy(bf16[256,32]{0,1:T(8,128)(2,1)} %param.8) | data formatting | bytes 32768 | tf_op args[1]
  6.3 2.7 %prep.1 = (bf16[16,512,128]{2,1,0:T(8,128)(2,1)}, bf16[8,224,128]{2,1,0:T(8,128)(2,1)}) custom-call(bf16[256,128]{1,0:T(8,128)(2,1)} %x_ref.1, bf16[256,32]{1,0:T(8,128)(2,1)} %copy.13.v_ref, bf16[128,128]{1,0:T(8,128)(2,1)} %c_ref.1, bf16[128,32]{1,0:T(8,128)(2,1)} %copy.14.s_ref, bf16[128,32]{1,0:T(8,128)(2,1)} %copy.15.l_ref, ...), custom_call_target="tpu_custom_call" | custom-call | tf_op jit(solution)/shard_map/prep/pallas_call | solution.py:161
  9.0 14.2 %all_to_all.20.own_ref = bf16[8,224,128]{2,1,0:T(8,128)(2,1)S(1)} all-to-all(bf16[8,224,128]{2,1,0:T(8,128)(2,1)} %get-tuple-element.4), channel_id=1, replica_groups=mesh['zh'=4,'y'=4,'core'=2,'zl'=2,'x'=4] {'zl','x'}, dimensions={0} | all-to-all | bytes 917504 | tf_op jit(solution)/shard_map/all_to_all | solution.py:176
  23.2 0.0 copy-start
  23.2 10.2 %all-to-all-start.1 = ((bf16[16,512,128]{2,1,0:T(8,128)(2,1)}), bf16[16,512,128]{2,1,0:T(8,128)(2,1)S(1)}, u32[]{:S(2)}, u32[]{:S(2)}) async-start(bf16[16,512,128]{2,1,0:T(8,128)(2,1)} %get-tuple-element.5), calls=%async_computation.1 | async-start | bytes 4194304 | tf_op jit(solution)/shard_map/all_to_all | solution.py:178
  33.4 2.7 %collective-permute-start = (bf16[8,224,128]{2,1,0:T(8,128)(2,1)S(1)}, bf16[8,224,128]{2,1,0:T(8,128)(2,1)S(1)}, u32[]{:S(2)}, u32[]{:S(2)}) collective-permute-start(bf16[8,224,128]{2,1,0:T(8,128)(2,1)S(1)} %all_to_all.20.own_ref), channel_id=1, source_target_pairs={{0,8},{8,0},{1,9},{9,1},{2,10},{10,2},{3,11},{11,3},{4,12},{12,4},... | collective-permute-start | bytes 1376264 | tf_op jit(solution)/shard_map/ppermute | solution.py:177
  36.1 1.4 %collective-permute-done.oth_ref = bf16[8,224,128]{2,1,0:T(8,128)(2,1)S(1)} collective-permute-done((bf16[8,224,128]{2,1,0:T(8,128)(2,1)S(1)}, bf16[8,224,128]{2,1,0:T(8,128)(2,1)S(1)}, u32[]{:S(2)}, u32[]{:S(2)}) %collective-permute-start) | collective-permute-done | bytes 458784 | tf_op jit(solution)/shard_map/ppermute | solution.py:177
  37.6 34.6 %all-to-all-done.1.pp_ref = bf16[16,512,128]{2,1,0:T(8,128)(2,1)S(1)} async-done(((bf16[16,512,128]{2,1,0:T(8,128)(2,1)}), bf16[16,512,128]{2,1,0:T(8,128)(2,1)S(1)}, u32[]{:S(2)}, u32[]{:S(2)}) %all-to-all-start.1) | async-done | bytes 2097184 | tf_op jit(solution)/shard_map/all_to_all | solution.py:178
  72.2 0.0 copy-done
  72.2 24.5 %pairs.1 = f32[2,8,136,128]{3,2,1,0:T(8,128)S(1)} custom-call(bf16[8,224,128]{2,1,0:T(8,128)(2,1)S(1)} %all_to_all.20.own_ref, bf16[8,224,128]{2,1,0:T(8,128)(2,1)S(1)} %collective-permute-done.oth_ref, bf16[16,512,128]{2,1,0:T(8,128)(2,1)S(1)} %all-to-all-done.1.pp_ref, f32[1,128]{1,0:T(1,128)S(1)} %bitcast.8), custom_call_target="tpu_custom_call" | custom-call | tf_op jit(solution)/shard_map/pairs/pallas_call | solution.py:180
  96.7 6.3 %collective-permute-start.1 = (f32[8,136,128]{2,1,0:T(8,128)S(1)}, f32[8,136,128]{2,1,0:T(8,128)S(1)}, u32[]{:S(2)}, u32[]{:S(2)}) collective-permute-start(f32[8,136,128]{2,1,0:T(8,128)S(1)} %slice_bitcast_fusion), channel_id=1, source_target_pairs={{0,8},{8,0},{1,9},{9,1},{2,10},{10,2},{3,11},{11,3},{4,12},{12,4},... | collective-permute-start | bytes 1671176 | tf_op jit(solution)/shard_map/ppermute | solution.py:197
  103.0 1.6 %collective-permute-done.1 = f32[8,136,128]{2,1,0:T(8,128)S(1)} collective-permute-done((f32[8,136,128]{2,1,0:T(8,128)S(1)}, f32[8,136,128]{2,1,0:T(8,128)S(1)}, u32[]{:S(2)}, u32[]{:S(2)}) %collective-permute-start.1) | collective-permute-done | bytes 557088 | tf_op jit(solution)/shard_map/ppermute | solution.py:197
  104.6 0.1 fusion
  104.7 23.4 %all_to_all.21 = f32[8,136,128]{2,1,0:T(8,128)S(1)} all-to-all(f32[8,136,128]{2,1,0:T(8,128)S(1)} %fusion), channel_id=1, replica_groups=mesh['zh'=4,'y'=4,'core'=2,'zl'=2,'x'=4] {'zl','x'}, dimensions={0} | all-to-all | bytes 1114112 | tf_op jit(solution)/shard_map/all_to_all | solution.py:198
  128.2 0.6 broadcast_in_dim.2
  128.8 3.9 %all-to-all-start.3 = ((f32[16,8,128]{2,1,0:T(8,128)}), f32[16,8,128]{2,1,0:T(8,128)S(1)}, u32[]{:S(2)}, u32[]{:S(2)}) async-start(f32[16,8,128]{2,1,0:T(8,128)} %broadcast_in_dim.2), calls=%async_computation.3 | async-start | bytes 131072 | tf_op jit(solution)/shard_map/all_to_all | solution.py:202
  132.7 0.6 slice.18
  133.3 8.3 %all-to-all-done.3 = f32[16,8,128]{2,1,0:T(8,128)S(1)} async-done(((f32[16,8,128]{2,1,0:T(8,128)}), f32[16,8,128]{2,1,0:T(8,128)S(1)}, u32[]{:S(2)}, u32[]{:S(2)}) %all-to-all-start.3) | async-done | bytes 65568 | tf_op jit(solution)/shard_map/all_to_all | solution.py:202
  141.7 0.5 div.3
  (4 shorter events, 0.1 us)
Async XLA Ops:
  23.2 49.0 %copy-start = (f32[128]{0:T(128)S(1)}, f32[128]{0:T(128)}, u32[]{:S(2)}) copy-start(f32[128]{0:T(128)} %param.13) | copy-start | bytes 1540
  23.2 49.0 %all-to-all-start.1 = ((bf16[16,512,128]{2,1,0:T(8,128)(2,1)}), bf16[16,512,128]{2,1,0:T(8,128)(2,1)S(1)}, u32[]{:S(2)}, u32[]{:S(2)}) async-start(bf16[16,512,128]{2,1,0:T(8,128)(2,1)} %get-tuple-element.5), calls=%async_computation.1 | async-start | bytes 4194304 | tf_op jit(solution)/shard_map/all_to_all | solution.py:178
  33.4 4.2 %collective-permute-start = (bf16[8,224,128]{2,1,0:T(8,128)(2,1)S(1)}, bf16[8,224,128]{2,1,0:T(8,128)(2,1)S(1)}, u32[]{:S(2)}, u32[]{:S(2)}) collective-permute-start(bf16[8,224,128]{2,1,0:T(8,128)(2,1)S(1)} %all_to_all.20.own_ref), channel_id=1, source_target_pairs={{0,8},{8,0},{1,9},{9,1},{2,10},{10,2},{3,11},{11,3},{4,12},{12,4},... | collective-permute-start | bytes 1376264 | tf_op jit(solution)/shard_map/ppermute | solution.py:177
  96.7 7.9 %collective-permute-start.1 = (f32[8,136,128]{2,1,0:T(8,128)S(1)}, f32[8,136,128]{2,1,0:T(8,128)S(1)}, u32[]{:S(2)}, u32[]{:S(2)}) collective-permute-start(f32[8,136,128]{2,1,0:T(8,128)S(1)} %slice_bitcast_fusion), channel_id=1, source_target_pairs={{0,8},{8,0},{1,9},{9,1},{2,10},{10,2},{3,11},{11,3},{4,12},{12,4},... | collective-permute-start | bytes 1671176 | tf_op jit(solution)/shard_map/ppermute | solution.py:197
  128.8 12.9 %all-to-all-start.3 = ((f32[16,8,128]{2,1,0:T(8,128)}), f32[16,8,128]{2,1,0:T(8,128)S(1)}, u32[]{:S(2)}, u32[]{:S(2)}) async-start(f32[16,8,128]{2,1,0:T(8,128)} %broadcast_in_dim.2), calls=%async_computation.3 | async-start | bytes 131072 | tf_op jit(solution)/shard_map/all_to_all | solution.py:202

commit v2 on v1

v2 whole, which is shorter than its diff:
```python
import functools

import jax
import jax.numpy as jnp
from jax import lax
from jax.experimental import pallas as pl
from jax.experimental.pallas import tpu as pltpu
from jax.sharding import Mesh, PartitionSpec as P

BF = jnp.bfloat16
F32 = jnp.float32
AXES = ("zh", "y", "core", "zl", "x")
SIZES = (4, 4, 2, 2, 4)
CENTER_AXES = ("zh", "zl")
BLOCK_AXES = ("zh", "zl", "core")
PLANE_AXES = ("y", "core", "x")
SCALE_AXES = ("y", "x", "core")
D = 128
R = 32
PTS = 256
CTR = 128
CROWS = CTR + 3 * R
BASE = PTS + CTR
PROWS = BASE + 4 * R
TAIL = 16
NZ = 8
NB = 2 * NZ
NSIDE = 4
M = NB * CTR
VM = pl.BlockSpec(memory_space=pltpu.VMEM)
SM = pl.BlockSpec(memory_space=pltpu.SMEM)
PARAMS = pltpu.CompilerParams(vmem_limit_bytes=44 * 2**20)


def dot_nn(a, b):
    return lax.dot_general(a, b, (((1,), (0,)), ((), ())), preferred_element_type=F32)


def fold(v):
    return jnp.sum(v.reshape(v.shape[0] // 8, 8, v.shape[1]), axis=0)


def prep_kernel(x_ref, v_ref, c_ref, s_ref, l_ref, r_ref, ls_ref, pp_ref, cb_ref):
    ls = ls_ref[...]
    x = (x_ref[...].astype(F32) / ls).astype(BF)
    c = (c_ref[...].astype(F32) / ls).astype(BF)
    lt, rt = l_ref[...], r_ref[...]
    pp_ref[...] = jnp.concatenate([x, c, v_ref[:, 0:CTR], v_ref[:, CTR:PTS], rt, lt], 0)
    cb_ref[...] = jnp.concatenate([c, s_ref[...], lt, rt], 0)


def set_centers(cen_ref, ca, hc, us, ul):
    lane = lax.broadcasted_iota(jnp.int32, (CTR, 128), 1)
    for j in range(NB):
        rows = slice(j * CTR, (j + 1) * CTR)
        c = cen_ref[j, 0:CTR, :]
        cf = c.astype(F32)
        ca[rows, :] = c
        hc[rows, :] = jnp.broadcast_to(0.5 * jnp.sum(cf * cf, axis=1, keepdims=True), (CTR, 128))
        ut = jnp.concatenate([cen_ref[j, CTR:CROWS, :], jnp.zeros((R, 128), BF)], 0)
        u = ut.astype(F32).T
        us[rows, :] = jnp.where(lane < R, u, 0.0).astype(BF)
        ul[rows, :] = jnp.where((lane >= R) & (lane < 3 * R), u, 0.0).astype(BF)


def turn(rows, xt, hx, slot, at):
    t = rows.astype(F32).T
    cols = slice(at * 128, (at + 1) * 128)
    xt[slot, :, cols] = t.astype(BF)
    hx[slot, :, cols] = jnp.broadcast_to(0.5 * jnp.sum(t * t, axis=0, keepdims=True), (8, 128))


def sweep(x, xt, hx, vt, ca, hc, u_ref, g, qa):
    n = x.shape[0]
    cross = dot_nn(ca[...], xt)
    prod = dot_nn(u_ref[...], vt)
    h = hc[...]
    parts = []
    for k in range(n // 128):
        cols = slice(k * 128, (k + 1) * 128)
        parts.append(jnp.exp((cross[:, cols] - h) - hx[:, cols]) * prod[:, cols])
    w = jnp.concatenate(parts, 1)
    g[...] += dot_nn(w.astype(BF), x)
    s = parts[0]
    for p in parts[1:]:
        s = s + p
    qa[...] += s
    return w


def add_pairs(blocks, count, ca, hc, us, ul, g, qa, ell, xt, hx, ct, hy):
    g[...] = jnp.zeros_like(g)
    qa[...] = jnp.zeros_like(qa)
    ell[...] = jnp.zeros_like(ell)
    steps = count // NSIDE

    def turn_points(a, slot):
        for k in range(NSIDE):
            turn(blocks[NSIDE * a + k, 0:128, :], xt, hx, slot, 2 * k)
            turn(blocks[NSIDE * a + k, 128:PTS, :], xt, hx, slot, 2 * k + 1)

    def turn_centers(a, slot):
        for k in range(NSIDE):
            turn(blocks[NSIDE * a + k, PTS:BASE, :], ct, hy, slot, k)

    def points_step(a, carry):
        ids = [NSIDE * a + k for k in range(NSIDE)]
        slot = lax.rem(a, 2)
        x = jnp.concatenate([blocks[i, 0:PTS, :] for i in ids], 0)
        vt = jnp.concatenate(
            [blocks[i, BASE + k * R : BASE + (k + 1) * R, :] for i in ids for k in (0, 1)], 1
        )
        vt = jnp.concatenate([vt, jnp.zeros((3 * R, NSIDE * PTS), BF)], 0)
        w = sweep(x, xt[slot], hx[slot, 0:1, :], vt, ca, hc, us, g, qa)
        if steps > 1:
            turn_points(lax.min(a + 1, steps - 1), 1 - slot)
        rowsum = fold(w)
        r1 = rowsum.astype(BF)
        rest = rowsum - r1.astype(F32)
        r2 = rest.astype(BF)
        r3 = (rest - r2.astype(F32)).astype(BF)
        xf = x.astype(F32)
        xsq = xf * xf
        xh = xsq.astype(BF)
        xl = (xsq - xh.astype(F32)).astype(BF)
        ell[...] += dot_nn(
            jnp.concatenate([r1, r2, r3, jnp.zeros_like(r1)], 0), jnp.concatenate([xh, xl], 1)
        )
        return carry

    def centers_step(a, carry):
        ids = [NSIDE * a + k for k in range(NSIDE)]
        slot = lax.rem(a, 2)
        c = jnp.concatenate([blocks[i, PTS:BASE, :] for i in ids], 0)
        z = jnp.zeros((R, NSIDE * CTR), BF)
        vc = jnp.concatenate([blocks[i, BASE + 2 * R : PROWS, :] for i in ids], 1)
        sweep(c, ct[slot], hy[slot, 0:1, :], jnp.concatenate([z, vc, z], 0), ca, hc, ul, g, qa)
        if steps > 1:
            turn_centers(lax.min(a + 1, steps - 1), 1 - slot)
        return carry

    turn_points(0, 0)
    lax.fori_loop(0, steps, points_step, 0)
    e = ell[...]
    e = e[:, 0:128] + e[:, 128:256]
    scale = e[0:8] + e[8:16] + e[16:24]
    for j in range(NB):
        rows = slice(j * CTR, (j + 1) * CTR)
        scale = scale - fold(ca[rows, :].astype(F32) * g[rows, :])
    turn_centers(0, 0)
    lax.fori_loop(0, steps, centers_step, 0)
    return scale


def block_terms(j, ca, g, qa):
    rows = slice(j * CTR, (j + 1) * CTR)
    c = ca[rows, :].astype(F32)
    q = jnp.sum(qa[rows, :], axis=1, keepdims=True)
    t = g[rows, :] - q * c
    return t, fold(c * t)


def first_kernel(cen_ref, a_ref, b_ref, c_ref, d_ref, ca, hc, us, ul, t_ref, s_ref, g, qa, ell, xt, hx, ct, hy, blocks):
    set_centers(cen_ref, ca, hc, us, ul)
    for k, ref in enumerate((a_ref, b_ref, c_ref, d_ref)):
        blocks[k] = ref[...]
    scale = add_pairs(blocks, NSIDE, ca, hc, us, ul, g, qa, ell, xt, hx, ct, hy)
    for j in range(NB):
        t, s = block_terms(j, ca, g, qa)
        t_ref[j] = t
        scale = scale - s
    s_ref[...] = scale


def last_kernel(me_ref, ca, hc, us, ul, t0, s0, ls_ref, a_ref, b_ref, c_ref, t_ref, s_ref, g, qa, ell, xt, hx, ct, hy, blocks):
    for k, ref in enumerate((a_ref, b_ref, c_ref)):
        for i in range(NSIDE):
            blocks[NSIDE * k + i] = ref[i]
    scale = s0[...] + add_pairs(blocks, 3 * NSIDE, ca, hc, us, ul, g, qa, ell, xt, hx, ct, hy)
    ls = ls_ref[...]
    me = me_ref[0]
    for j in range(NB):
        t, s = block_terms(j, ca, g, qa)
        h = me if j % 2 == 0 else 1 - me
        t_ref[h, j // 2] = (t0[j] + t) / ls
        scale = scale - s
    s_ref[...] = scale


def plane_shift(value, by, swap):
    perm = []
    for y in range(4):
        for core in range(2):
            for x in range(4):
                along_x = (core == 0) != swap
                ty, tx = (y, (x + by) % 4) if along_x else ((y + by) % 4, x)
                perm.append(((y * 2 + core) * 4 + x, (ty * 2 + core) * 4 + tx))
    return lax.ppermute(value, PLANE_AXES, perm)


def pieces(s):
    a = s.astype(BF)
    rest = s - a.astype(F32)
    b = rest.astype(BF)
    c = (rest - b.astype(F32)).astype(BF)
    return jnp.concatenate([jnp.stack([a, b, c]), jnp.zeros((TAIL - 3, D), BF)], 0)


def cost(peers):
    rows = peers * BASE
    return pl.CostEstimate(flops=2 * rows * M * 288, bytes_accessed=2**22, transcendentals=rows * M)


def local(points, adjoint_rows, centers, solution_rows, center_left, center_right, lengthscale):
    ls = lengthscale.reshape(1, D)
    shape = jax.ShapeDtypeStruct
    pp, cb = pl.pallas_call(
        prep_kernel,
        out_shape=[shape((PROWS, D), BF), shape((CROWS, D), BF)],
        in_specs=[VM] * 7,
        out_specs=[VM] * 2,
        name="prep",
    )(points, adjoint_rows.T, centers, solution_rows.T, center_left.T, center_right.T, ls)
    side = [pp] + [plane_shift(pp, by, False) for by in (1, 3, 2)]
    line = jnp.stack(side)
    rest = [plane_shift(line, by, True) for by in (1, 3, 2)]
    cen = lax.all_gather(cb, BLOCK_AXES, axis=0, tiled=False)
    work = [
        pltpu.VMEM((M, D), F32),
        pltpu.VMEM((M, D), F32),
        pltpu.VMEM((32, 2 * D), F32),
        pltpu.VMEM((2, D, NSIDE * PTS), BF),
        pltpu.VMEM((2, 8, NSIDE * PTS), F32),
        pltpu.VMEM((2, D, NSIDE * CTR), BF),
        pltpu.VMEM((2, 8, NSIDE * CTR), F32),
    ]
    state = pl.pallas_call(
        first_kernel,
        out_shape=[
            shape((M, D), BF),
            shape((M, D), F32),
            shape((M, D), BF),
            shape((M, D), BF),
            shape((NB, CTR, D), F32),
            shape((8, D), F32),
        ],
        in_specs=[VM] * 5,
        out_specs=[VM] * 6,
        scratch_shapes=work + [pltpu.VMEM((NSIDE, PROWS, D), BF)],
        compiler_params=PARAMS,
        cost_estimate=cost(NSIDE),
        name="pairs_first",
    )(cen, *side)
    me = lax.axis_index("core").astype(jnp.int32).reshape(1)
    terms, scale = pl.pallas_call(
        last_kernel,
        out_shape=[shape((2, NZ, CTR, D), F32), shape((8, D), F32)],
        in_specs=[SM] + [VM] * 10,
        out_specs=[VM] * 2,
        scratch_shapes=work + [pltpu.VMEM((3 * NSIDE, PROWS, D), BF)],
        compiler_params=PARAMS,
        cost_estimate=cost(3 * NSIDE),
        name="pairs_last",
    )(me, *state, ls, *rest)
    swapped = lax.ppermute(terms[1], "core", [(0, 1), (1, 0)])
    tiny = jnp.broadcast_to(scale[None], (32, 8, D))
    scale = jnp.sum(lax.all_to_all(tiny, SCALE_AXES, 0, 0, tiled=True), (0, 1))
    mine = (terms[0] + swapped).astype(BF)
    chunk = jnp.concatenate([mine, jnp.broadcast_to(pieces(scale)[None], (NZ, TAIL, D))], 1)
    parts = jnp.sum(lax.all_to_all(chunk, CENTER_AXES, 0, 0, tiled=True).astype(F32), 0)
    return parts[0:CTR], jnp.sum(parts[CTR:], 0) / lengthscale


def solution(mesh):
    grid = Mesh(mesh.devices.reshape(SIZES), AXES)
    rows = P(AXES, None)
    return jax.shard_map(
        local,
        mesh=grid,
        in_specs=(rows,) * 6 + (P(),),
        out_specs=(rows, P()),
        check_vma=False,
    )
```

time: 143 us -> 96.5 us (0.67)
  waiting for transfers between devices: 46 us -> 11.1 us
  starting transfers between devices: 23.1 us -> 14.2 us
  local copies, waits for them, and re-layouts: 6.96 us -> 2.08 us
  blocking collectives: 37.6 us -> 41 us
  Pallas kernels: 27.2 us -> 25.3 us
    all_to_all x2 -> x1, waiting for transfers between devices: 42.9 us -> 7.26 us  [local(): scale = jnp.sum(lax.all_to_all(tiny, SCALE_AXES, 0, 0, tiled=True), (0, 1))]
    all_gather x0 -> x1, blocking collectives: none -> 25.8 us  [local(): cen = lax.all_gather(cb, BLOCK_AXES, axis=0, tiled=False)]
    all_to_all x2 -> x1, blocking collectives: 37.6 us -> 15.2 us  [local(): lax.all_to_all(chunk, CENTER_AXES, 0, 0, tiled=True).astype(F32)]
    all_to_all x2 -> x1, starting transfers between devices: 14.1 us -> 4.39 us  [local(): scale = jnp.sum(lax.all_to_all(tiny, SCALE_AXES, 0, 0, tiled=True), (0, 1))]
    unnamed x6, local copies, waits for them, and re-layouts: 5.67 us -> 0.66 us
    pallas_call x2 -> x3, Pallas kernels: 27.2 us -> 25.3 us  [the longest x1 17.5 us: local(): pl.pallas_call(last_kernel, out_shape=[shape((2, NZ, CTR, D), F32), shape...]
    ppermute x2 -> x7, waiting for transfers between devices: 3.03 us -> 3.82 us  [the longest x6 3.81 us: plane_shift(): return lax.ppermute(value, PLANE_AXES, perm)]
    ppermute x2 -> x7, starting transfers between devices: 9.06 us -> 9.82 us  [the longest x6 9.5 us: plane_shift(): return lax.ppermute(value, PLANE_AXES, perm)]
  transfers between devices with their start and end apart: 4 -> 8, of which waited for: 4 -> 3; matrix products, arithmetic and copies ran while one was open for 0% -> 0% of each run, Pallas kernels for 0% -> 7%
where the time goes in v2:
time: 96.5 us; the launch traced here: 96.2 us
  blocking collectives  41 us (42%)
  Pallas kernels  25.3 us (26%)
  starting transfers between devices  14.2 us (15%)
  waiting for transfers between devices  11.1 us (12%)
  local copies, waits for them, and re-layouts  2.08 us (2%)
  other arithmetic  1.79 us (2%)
    all_gather x1, blocking collectives, local(): cen = lax.all_gather(cb, BLOCK_AXES, axis=0, tiled=False)  25.8 us
    pallas_call x1, Pallas kernels, local(): pl.pallas_call(last_kernel, out_shape=[shape((2, NZ, CTR, D), F32), shape...  17.5 us
    all_to_all x1, blocking collectives, local(): lax.all_to_all(chunk, CENTER_AXES, 0, 0, tiled=True).astype(F32)  15.2 us
    ppermute x6, starting transfers between devices, plane_shift(): return lax.ppermute(value, PLANE_AXES, perm)  9.5 us
    all_to_all x1, waiting for transfers between devices, local(): scale = jnp.sum(lax.all_to_all(tiny, SCALE_AXES, 0, 0, tiled=True), (0, 1))  7.26 us
    pallas_call x1, Pallas kernels, local(): pl.pallas_call(first_kernel, out_shape=[shape((M, D), BF), shape((M, D),...  6.26 us
    all_to_all x1, starting transfers between devices, local(): scale = jnp.sum(lax.all_to_all(tiny, SCALE_AXES, 0, 0, tiled=True), (0, 1))  4.39 us
    ppermute x6, waiting for transfers between devices, plane_shift(): return lax.ppermute(value, PLANE_AXES, perm)  3.81 us
  transfers between devices with their start and end apart: 8, of which 3 were waited for; matrix products, arithmetic and copies ran while one was open for 0% of the time, Pallas kernels for 7%

profile of v2, /device:TPU:1, one launch (start us, length us, event | category | flops | bytes accessed | tf_op | source)
XLA Modules:
  0.0 96.2 jit_solution(7744935307306440539)
XLA Ops:
  0.6 1.6 %prep.1 = (bf16[512,128]{1,0:T(8,128)(2,1)}, bf16[224,128]{1,0:T(8,128)(2,1)}) custom-call(bf16[256,128]{1,0:T(8,128)(2,1)} %x_ref.1, bf16[32,256]{1,0:T(8,128)(2,1)} %bitcast.37, bf16[128,128]{1,0:T(8,128)(2,1)} %c_ref.1, bf16[32,128]{1,0:T(8,128)(2,1)} %bitcast.38, bf16[32,128]{1,0:T(8,128)(2,1)} %bitcast.39, bf16[32,128]{1,0:T(8,128)(2,1)} %bitcast.40, ...), custom_call_target="tpu_custom_call" | custom-call | tf_op jit(solution)/shard_map/prep/pallas_call | solution.py:217
  2.2 2.1 %collective-permute-start = (bf16[512,128]{1,0:T(8,128)(2,1)}, bf16[512,128]{1,0:T(8,128)(2,1)S(1)}, u32[]{:S(2)}, u32[]{:S(2)}) collective-permute-start(bf16[512,128]{1,0:T(8,128)(2,1)} %get-tuple-element.13.a_ref), channel_id=1, source_target_pairs={{0,1},{1,2},{2,3},{3,0},{8,24},{9,25},{10,26},{11,27},{16,17},{17,... | collective-permute-start | bytes 393224 | tf_op jit(solution)/shard_map/ppermute | solution.py:198
  4.3 1.4 %collective-permute-start.1 = (bf16[512,128]{1,0:T(8,128)(2,1)}, bf16[512,128]{1,0:T(8,128)(2,1)S(1)}, u32[]{:S(2)}, u32[]{:S(2)}) collective-permute-start(bf16[512,128]{1,0:T(8,128)(2,1)} %get-tuple-element.13.a_ref), channel_id=1, source_target_pairs={{0,3},{1,0},{2,1},{3,2},{8,56},{9,57},{10,58},{11,59},{16,19},{17,... | collective-permute-start | bytes 393224 | tf_op jit(solution)/shard_map/ppermute | solution.py:198
  5.8 1.6 %collective-permute-start.2 = (bf16[512,128]{1,0:T(8,128)(2,1)}, bf16[512,128]{1,0:T(8,128)(2,1)S(1)}, u32[]{:S(2)}, u32[]{:S(2)}) collective-permute-start(bf16[512,128]{1,0:T(8,128)(2,1)} %get-tuple-element.13.a_ref), channel_id=1, source_target_pairs={{0,2},{1,3},{2,0},{3,1},{8,40},{9,41},{10,42},{11,43},{16,18},{17,... | collective-permute-start | bytes 393224 | tf_op jit(solution)/shard_map/ppermute | solution.py:198
  7.4 0.1 pad.5.clone
  7.5 0.8 collective-permute-done.b_ref
  8.3 0.0 collective-permute-done.1.c_ref
  8.4 2.9 %collective-permute-done.2.d_ref = bf16[512,128]{1,0:T(8,128)(2,1)S(1)} collective-permute-done((bf16[512,128]{1,0:T(8,128)(2,1)}, bf16[512,128]{1,0:T(8,128)(2,1)S(1)}, u32[]{:S(2)}, u32[]{:S(2)}) %collective-permute-start.2) | collective-permute-done | bytes 131104 | tf_op jit(solution)/shard_map/ppermute | solution.py:198
  11.3 0.0 copy-start.2
  11.3 1.0 %pad_maximum_fusion = bf16[4,512,128]{2,1,0:T(8,128)(2,1)S(1)} fusion(bf16[1,512,128]{2,1,0:T(8,128)(2,1)S(1)} %bitcast.34, bf16[1,512,128]{2,1,0:T(8,128)(2,1)S(1)} %bitcast.33, bf16[1,512,128]{2,1,0:T(8,128)(2,1)S(1)} %bitcast.32, bf16[1,512,128]{2,1,0:T(8,128)(2,1)} %bitcast.31), kind=kLoop, calls=%fused_computation.1 | loop fusion | flops 786432 | bytes 1048576 | tf_op jit(solution)/shard_map/stack | solution.py:225
  12.3 1.3 %collective-permute-start.3 = (bf16[4,512,128]{2,1,0:T(8,128)(2,1)S(1)}, bf16[4,512,128]{2,1,0:T(8,128)(2,1)S(1)}, u32[]{:S(2)}, u32[]{:S(2)}) collective-permute-start(bf16[4,512,128]{2,1,0:T(8,128)(2,1)S(1)} %pad_maximum_fusion), channel_id=1, source_target_pairs={{0,16},{1,17},{2,18},{3,19},{8,9},{9,10},{10,11},{11,8},{16,32},{1... | collective-permute-start | bytes 1572872 | tf_op jit(solution)/shard_map/ppermute | solution.py:198
  13.6 1.7 %collective-permute-start.4 = (bf16[4,512,128]{2,1,0:T(8,128)(2,1)S(1)}, bf16[4,512,128]{2,1,0:T(8,128)(2,1)S(1)}, u32[]{:S(2)}, u32[]{:S(2)}) collective-permute-start(bf16[4,512,128]{2,1,0:T(8,128)(2,1)S(1)} %pad_maximum_fusion), channel_id=1, source_target_pairs={{0,48},{1,49},{2,50},{3,51},{8,11},{9,8},{10,9},{11,10},{16,0},{17... | collective-permute-start | bytes 1572872 | tf_op jit(solution)/shard_map/ppermute | solution.py:198
  15.2 1.3 %collective-permute-start.5 = (bf16[4,512,128]{2,1,0:T(8,128)(2,1)S(1)}, bf16[4,512,128]{2,1,0:T(8,128)(2,1)S(1)}, u32[]{:S(2)}, u32[]{:S(2)}) collective-permute-start(bf16[4,512,128]{2,1,0:T(8,128)(2,1)S(1)} %pad_maximum_fusion), channel_id=1, source_target_pairs={{0,32},{1,33},{2,34},{3,35},{8,10},{9,11},{10,8},{11,9},{16,48},{1... | collective-permute-start | bytes 1572872 | tf_op jit(solution)/shard_map/ppermute | solution.py:198
  16.6 0.0 copy-done.2
  16.6 0.0 copy-start
  16.6 25.8 %all-gather = bf16[3584,128]{1,0:T(8,128)(2,1)S(1)} all-gather(bf16[224,128]{1,0:T(8,128)(2,1)S(1)} %copy-done.2), channel_id=2, replica_groups=mesh['zh'=4,'y'=4,'core'=2,'zl'=2,'x'=4] {'zh','zl','core'}, dimensions={0}, use_global_device_ids=true | all-gather | bytes 974848 | tf_op jit(solution)/shard_map/all_gather | solution.py:227
  42.4 0.0 copy-done
  42.4 6.3 %pairs_first.1 = (bf16[2048,128]{1,0:T(8,128)(2,1)S(1)}, f32[2048,128]{1,0:T(8,128)S(1)}, bf16[2048,128]{1,0:T(8,128)(2,1)S(1)}, bf16[2048,128]{1,0:T(8,128)(2,1...) custom-call(bf16[16,224,128]{2,1,0:T(8,128)(2,1)S(1)} %bitcast.30, bf16[512,128]{1,0:T(8,128)(2,1)S(1)} %copy-done, ...), custom_call_target="tpu_custom_call" | custom-call | flops 1811939328 | bytes 4194304 | tf_op jit(solution)/shard_map/pairs_first/pallas_call | solution.py:237
  48.6 0.0 collective-permute-done.3.a_ref
  48.6 0.0 collective-permute-done.4.b_ref
  48.7 0.0 collective-permute-done.5.c_ref
  48.7 0.0 copy-start.1
  48.7 0.6 copy-done.1
  49.3 17.5 %pairs_last.1 = (f32[2,8,128,128]{3,2,1,0:T(8,128)S(1)}, f32[8,128]{1,0:T(8,128)S(1)}) custom-call(s32[1]{0:T(128)} %bitcast.me_ref, bf16[2048,128]{1,0:T(8,128)(2,1)S(1)} %get-tuple-element.14.ca, f32[2048,128]{1,0:T(8,128)S(1)} %get-tuple-element.15.hc, bf16[2048,128]{1,0:T(8,128)(2,1)S(1)} %get-tuple-element.16.us, ...), custom_call_target="tpu_custom_call" | custom-call | flops 5435817984 | bytes 4194304 | tf_op jit(solution)/shard_map/pairs_last/pallas_call | solution.py:255
  66.8 0.7 broadcast_in_dim.6
  67.5 4.4 %all-to-all-start = ((f32[32,8,128]{2,1,0:T(8,128)}), f32[32,8,128]{2,1,0:T(8,128)S(1)}, u32[]{:S(2)}, u32[]{:S(2)}) async-start(f32[32,8,128]{2,1,0:T(8,128)} %broadcast_in_dim.6), calls=%async_computation | async-start | bytes 262144 | tf_op jit(solution)/shard_map/all_to_all | solution.py:267
  71.9 0.3 collective-permute-start.6
  72.2 7.3 %all-to-all-done = f32[32,8,128]{2,1,0:T(8,128)S(1)} async-done(((f32[32,8,128]{2,1,0:T(8,128)}), f32[32,8,128]{2,1,0:T(8,128)S(1)}, u32[]{:S(2)}, u32[]{:S(2)}) %all-to-all-start) | async-done | bytes 131104 | tf_op jit(solution)/shard_map/all_to_all | solution.py:267
  79.6 0.1 maximum_maximum_fusion
  79.6 0.0 collective-permute-done.6
  79.7 0.1 fusion
  79.8 15.2 %all_to_all.10 = bf16[8,144,128]{2,1,0:T(8,128)(2,1)S(1)} all-to-all(bf16[8,144,128]{2,1,0:T(8,128)(2,1)S(1)} %pad_maximum_fusion.1), channel_id=1, replica_groups=mesh['zh'=4,'y'=4,'core'=2,'zl'=2,'x'=4] {'zh','zl'}, dimensions={0} | all-to-all | bytes 589824 | tf_op jit(solution)/shard_map/all_to_all | solution.py:270
  95.0 0.6 slice.16
  95.7 0.5 div.3
  (9 shorter events, 0.2 us)
Async XLA Ops:
  2.2 6.1 %collective-permute-start = (bf16[512,128]{1,0:T(8,128)(2,1)}, bf16[512,128]{1,0:T(8,128)(2,1)S(1)}, u32[]{:S(2)}, u32[]{:S(2)}) collective-permute-start(bf16[512,128]{1,0:T(8,128)(2,1)} %get-tuple-element.13.a_ref), channel_id=1, source_target_pairs={{0,1},{1,2},{2,3},{3,0},{8,24},{9,25},{10,26},{11,27},{16,17},{17,... | collective-permute-start | bytes 393224 | tf_op jit(solution)/shard_map/ppermute | solution.py:198
  4.3 4.0 %collective-permute-start.1 = (bf16[512,128]{1,0:T(8,128)(2,1)}, bf16[512,128]{1,0:T(8,128)(2,1)S(1)}, u32[]{:S(2)}, u32[]{:S(2)}) collective-permute-start(bf16[512,128]{1,0:T(8,128)(2,1)} %get-tuple-element.13.a_ref), channel_id=1, source_target_pairs={{0,3},{1,0},{2,1},{3,2},{8,56},{9,57},{10,58},{11,59},{16,19},{17,... | collective-permute-start | bytes 393224 | tf_op jit(solution)/shard_map/ppermute | solution.py:198
  5.8 5.5 %collective-permute-start.2 = (bf16[512,128]{1,0:T(8,128)(2,1)}, bf16[512,128]{1,0:T(8,128)(2,1)S(1)}, u32[]{:S(2)}, u32[]{:S(2)}) collective-permute-start(bf16[512,128]{1,0:T(8,128)(2,1)} %get-tuple-element.13.a_ref), channel_id=1, source_target_pairs={{0,2},{1,3},{2,0},{3,1},{8,40},{9,41},{10,42},{11,43},{16,18},{17,... | collective-permute-start | bytes 393224 | tf_op jit(solution)/shard_map/ppermute | solution.py:198
  11.3 5.3 %copy-start.2 = (bf16[224,128]{1,0:T(8,128)(2,1)S(1)}, bf16[224,128]{1,0:T(8,128)(2,1)}, u32[]{:S(2)}) copy-start(bf16[224,128]{1,0:T(8,128)(2,1)} %get-tuple-element.12) | copy-start | bytes 172036
  12.3 36.3 %collective-permute-start.3 = (bf16[4,512,128]{2,1,0:T(8,128)(2,1)S(1)}, bf16[4,512,128]{2,1,0:T(8,128)(2,1)S(1)}, u32[]{:S(2)}, u32[]{:S(2)}) collective-permute-start(bf16[4,512,128]{2,1,0:T(8,128)(2,1)S(1)} %pad_maximum_fusion), channel_id=1, source_target_pairs={{0,16},{1,17},{2,18},{3,19},{8,9},{9,10},{10,11},{11,8},{16,32},{1... | collective-permute-start | bytes 1572872 | tf_op jit(solution)/shard_map/ppermute | solution.py:198
  13.6 35.1 %collective-permute-start.4 = (bf16[4,512,128]{2,1,0:T(8,128)(2,1)S(1)}, bf16[4,512,128]{2,1,0:T(8,128)(2,1)S(1)}, u32[]{:S(2)}, u32[]{:S(2)}) collective-permute-start(bf16[4,512,128]{2,1,0:T(8,128)(2,1)S(1)} %pad_maximum_fusion), channel_id=1, source_target_pairs={{0,48},{1,49},{2,50},{3,51},{8,11},{9,8},{10,9},{11,10},{16,0},{17... | collective-permute-start | bytes 1572872 | tf_op jit(solution)/shard_map/ppermute | solution.py:198
  15.2 33.4 %collective-permute-start.5 = (bf16[4,512,128]{2,1,0:T(8,128)(2,1)S(1)}, bf16[4,512,128]{2,1,0:T(8,128)(2,1)S(1)}, u32[]{:S(2)}, u32[]{:S(2)}) collective-permute-start(bf16[4,512,128]{2,1,0:T(8,128)(2,1)S(1)} %pad_maximum_fusion), channel_id=1, source_target_pairs={{0,32},{1,33},{2,34},{3,35},{8,10},{9,11},{10,8},{11,9},{16,48},{1... | collective-permute-start | bytes 1572872 | tf_op jit(solution)/shard_map/ppermute | solution.py:198
  16.6 25.8 %copy-start = (bf16[512,128]{1,0:T(8,128)(2,1)S(1)}, bf16[512,128]{1,0:T(8,128)(2,1)}, u32[]{:S(2)}) copy-start(bf16[512,128]{1,0:T(8,128)(2,1)} %get-tuple-element.13.a_ref) | copy-start | bytes 393220
  48.7 0.7 copy-start.1
  67.5 12.0 %all-to-all-start = ((f32[32,8,128]{2,1,0:T(8,128)}), f32[32,8,128]{2,1,0:T(8,128)S(1)}, u32[]{:S(2)}, u32[]{:S(2)}) async-start(f32[32,8,128]{2,1,0:T(8,128)} %broadcast_in_dim.6), calls=%async_computation | async-start | bytes 262144 | tf_op jit(solution)/shard_map/all_to_all | solution.py:267
  71.9 7.7 %collective-permute-start.6 = (f32[8,128,128]{2,1,0:T(8,128)S(1)}, f32[8,128,128]{2,1,0:T(8,128)S(1)}, u32[]{:S(2)}, u32[]{:S(2)}) collective-permute-start(f32[8,128,128]{2,1,0:T(8,128)S(1)} %slice_bitcast_fusion), channel_id=1, source_target_pairs={{0,8},{8,0},{1,9},{9,1},{2,10},{10,2},{3,11},{11,3},{4,12},{12,4},... | collective-permute-start | bytes 1572872 | tf_op jit(solution)/shard_map/ppermute | solution.py:265

commit v3 on v2

--- a/solution.py
+++ b/solution.py
@@ -12,7 +12,6 @@
 AXES = ("zh", "y", "core", "zl", "x")
 SIZES = (4, 4, 2, 2, 4)
 CENTER_AXES = ("zh", "zl")
-BLOCK_AXES = ("zh", "zl", "core")
 PLANE_AXES = ("y", "core", "x")
 SCALE_AXES = ("y", "x", "core")
 D = 128
@@ -26,6 +25,7 @@
 NZ = 8
 NB = 2 * NZ
 NSIDE = 4
+SHIFTS = (0, 1, 3, 2)
 M = NB * CTR
 VM = pl.BlockSpec(memory_space=pltpu.VMEM)
 SM = pl.BlockSpec(memory_space=pltpu.SMEM)
@@ -40,24 +40,26 @@
     return jnp.sum(v.reshape(v.shape[0] // 8, 8, v.shape[1]), axis=0)
 
 
-def prep_kernel(x_ref, v_ref, c_ref, s_ref, l_ref, r_ref, ls_ref, pp_ref, cb_ref):
+def prep_kernel(x_ref, v_ref, c_ref, s_ref, l_ref, r_ref, ls_ref, pp_ref, cb_ref, lv_ref):
     ls = ls_ref[...]
     x = (x_ref[...].astype(F32) / ls).astype(BF)
     c = (c_ref[...].astype(F32) / ls).astype(BF)
     lt, rt = l_ref[...], r_ref[...]
     pp_ref[...] = jnp.concatenate([x, c, v_ref[:, 0:CTR], v_ref[:, CTR:PTS], rt, lt], 0)
     cb_ref[...] = jnp.concatenate([c, s_ref[...], lt, rt], 0)
-
-
-def set_centers(cen_ref, ca, hc, us, ul):
+    lv_ref[...] = jnp.broadcast_to(ls, lv_ref.shape)
+
+
+def set_centers(own_ref, oth_ref, ca, hc, us, ul):
     lane = lax.broadcasted_iota(jnp.int32, (CTR, 128), 1)
     for j in range(NB):
         rows = slice(j * CTR, (j + 1) * CTR)
-        c = cen_ref[j, 0:CTR, :]
+        cen_ref, i = (own_ref, j) if j < NZ else (oth_ref, j - NZ)
+        c = cen_ref[i, 0:CTR, :]
         cf = c.astype(F32)
         ca[rows, :] = c
         hc[rows, :] = jnp.broadcast_to(0.5 * jnp.sum(cf * cf, axis=1, keepdims=True), (CTR, 128))
-        ut = jnp.concatenate([cen_ref[j, CTR:CROWS, :], jnp.zeros((R, 128), BF)], 0)
+        ut = jnp.concatenate([cen_ref[i, CTR:CROWS, :], jnp.zeros((R, 128), BF)], 0)
         u = ut.astype(F32).T
         us[rows, :] = jnp.where(lane < R, u, 0.0).astype(BF)
         ul[rows, :] = jnp.where((lane >= R) & (lane < 3 * R), u, 0.0).astype(BF)
@@ -160,8 +162,8 @@
     return t, fold(c * t)
 
 
-def first_kernel(cen_ref, a_ref, b_ref, c_ref, d_ref, ca, hc, us, ul, t_ref, s_ref, g, qa, ell, xt, hx, ct, hy, blocks):
-    set_centers(cen_ref, ca, hc, us, ul)
+def first_kernel(own_ref, oth_ref, a_ref, b_ref, c_ref, d_ref, ca, hc, us, ul, t_ref, s_ref, g, qa, ell, xt, hx, ct, hy, blocks):
+    set_centers(own_ref, oth_ref, ca, hc, us, ul)
     for k, ref in enumerate((a_ref, b_ref, c_ref, d_ref)):
         blocks[k] = ref[...]
     scale = add_pairs(blocks, NSIDE, ca, hc, us, ul, g, qa, ell, xt, hx, ct, hy)
@@ -172,19 +174,25 @@
     s_ref[...] = scale
 
 
-def last_kernel(me_ref, ca, hc, us, ul, t0, s0, ls_ref, a_ref, b_ref, c_ref, t_ref, s_ref, g, qa, ell, xt, hx, ct, hy, blocks):
+def last_kernel(at_ref, ca, hc, us, ul, t0, s0, ls_ref, a_ref, b_ref, c_ref, t_ref, s_ref, g, qa, ell, xt, hx, ct, hy, blocks):
     for k, ref in enumerate((a_ref, b_ref, c_ref)):
         for i in range(NSIDE):
             blocks[NSIDE * k + i] = ref[i]
     scale = s0[...] + add_pairs(blocks, 3 * NSIDE, ca, hc, us, ul, g, qa, ell, xt, hx, ct, hy)
-    ls = ls_ref[...]
-    me = me_ref[0]
+    ls = ls_ref[0:1, :]
+    zh, zl = at_ref[0], at_ref[1]
     for j in range(NB):
         t, s = block_terms(j, ca, g, qa)
-        h = me if j % 2 == 0 else 1 - me
-        t_ref[h, j // 2] = (t0[j] + t) / ls
+        h, i = divmod(j, NZ)
+        place = lax.rem(zh + 4 - SHIFTS[i // 2], 4) * 2 + (zl if i % 2 == 0 else 1 - zl)
+        t_ref[h, place] = (t0[j] + t) / ls
         scale = scale - s
     s_ref[...] = scale
+
+
+def shifted(value, axis, by):
+    n = dict(zip(AXES, SIZES))[axis]
+    return lax.ppermute(value, axis, [(i, (i + by) % n) for i in range(n)])
 
 
 def plane_shift(value, by, swap):
@@ -214,17 +222,19 @@
 def local(points, adjoint_rows, centers, solution_rows, center_left, center_right, lengthscale):
     ls = lengthscale.reshape(1, D)
     shape = jax.ShapeDtypeStruct
-    pp, cb = pl.pallas_call(
+    pp, cb, lv = pl.pallas_call(
         prep_kernel,
-        out_shape=[shape((PROWS, D), BF), shape((CROWS, D), BF)],
+        out_shape=[shape((PROWS, D), BF), shape((CROWS, D), BF), shape((8, D), F32)],
         in_specs=[VM] * 7,
-        out_specs=[VM] * 2,
+        out_specs=[VM] * 3,
         name="prep",
     )(points, adjoint_rows.T, centers, solution_rows.T, center_left.T, center_right.T, ls)
     side = [pp] + [plane_shift(pp, by, False) for by in (1, 3, 2)]
+    two = jnp.stack([cb, shifted(cb, "zl", 1)])
     line = jnp.stack(side)
     rest = [plane_shift(line, by, True) for by in (1, 3, 2)]
-    cen = lax.all_gather(cb, BLOCK_AXES, axis=0, tiled=False)
+    own = jnp.concatenate([two] + [shifted(two, "zh", by) for by in SHIFTS[1:]], 0)
+    oth = shifted(own, "core", 1)
     work = [
         pltpu.VMEM((M, D), F32),
         pltpu.VMEM((M, D), F32),
@@ -244,14 +254,14 @@
             shape((NB, CTR, D), F32),
             shape((8, D), F32),
         ],
-        in_specs=[VM] * 5,
+        in_specs=[VM] * 6,
         out_specs=[VM] * 6,
         scratch_shapes=work + [pltpu.VMEM((NSIDE, PROWS, D), BF)],
         compiler_params=PARAMS,
-        cost_estimate=cost(NSIDE),
+        cost_estimate=pl.CostEstimate(flops=1, bytes_accessed=1, transcendentals=0),
         name="pairs_first",
-    )(cen, *side)
-    me = lax.axis_index("core").astype(jnp.int32).reshape(1)
+    )(own, oth, *side)
+    at = jnp.stack([lax.axis_index("zh"), lax.axis_index("zl")]).astype(jnp.int32)
     terms, scale = pl.pallas_call(
         last_kernel,
         out_shape=[shape((2, NZ, CTR, D), F32), shape((8, D), F32)],
@@ -261,14 +271,15 @@
         compiler_params=PARAMS,
         cost_estimate=cost(3 * NSIDE),
         name="pairs_last",
-    )(me, *state, ls, *rest)
-    swapped = lax.ppermute(terms[1], "core", [(0, 1), (1, 0)])
+    )(at, *state, lv, *rest)
+    swapped = shifted(terms[1], "core", 1)
     tiny = jnp.broadcast_to(scale[None], (32, 8, D))
     scale = jnp.sum(lax.all_to_all(tiny, SCALE_AXES, 0, 0, tiled=True), (0, 1))
     mine = (terms[0] + swapped).astype(BF)
     chunk = jnp.concatenate([mine, jnp.broadcast_to(pieces(scale)[None], (NZ, TAIL, D))], 1)
-    parts = jnp.sum(lax.all_to_all(chunk, CENTER_AXES, 0, 0, tiled=True).astype(F32), 0)
-    return parts[0:CTR], jnp.sum(parts[CTR:], 0) / lengthscale
+    parts = lax.all_to_all(chunk, CENTER_AXES, 0, 0, tiled=True)
+    total = jnp.sum(parts[:, 0:CTR].astype(F32), 0)
+    return total, jnp.sum(parts[:, CTR:].astype(F32), (0, 1)) / lv[0]
 
 
 def solution(mesh):

time: 96.5 us -> 90.2 us (0.935)
  blocking collectives: 41 us -> 14.6 us
  starting transfers between devices: 14.2 us -> 34.4 us
    all_gather x1 -> x0, blocking collectives: 25.8 us -> none  [local(): cen = lax.all_gather(cb, BLOCK_AXES, axis=0, tiled=False)]
    ppermute x1 -> x6, starting transfers between devices: 0.32 us -> 15.9 us  [shifted(): return lax.ppermute(value, axis, [(i, (i + by) % n) for i in range(n)])]
    ppermute x6, waiting for transfers between devices: 3.81 us -> 0.02 us  [plane_shift(): return lax.ppermute(value, PLANE_AXES, perm)]
    ppermute x1 -> x6, waiting for transfers between devices: 0.01 us -> 2.92 us  [shifted(): return lax.ppermute(value, axis, [(i, (i + by) % n) for i in range(n)])]
    all_to_all x1, starting transfers between devices: 4.39 us -> 7.3 us  [local(): scale = jnp.sum(lax.all_to_all(tiny, SCALE_AXES, 0, 0, tiled=True), (0, 1))]
    ppermute x6, starting transfers between devices: 9.5 us -> 11.2 us  [plane_shift(): return lax.ppermute(value, PLANE_AXES, perm)]
  transfers between devices with their start and end apart: 8 -> 13, of which waited for: 3 -> 4; matrix products, arithmetic and copies ran while one was open for 0% -> 1% of each run, Pallas kernels for 7% -> 7%
where the time goes in v3:
time: 90.2 us; the launch traced here: 89.9 us
  starting transfers between devices  34.4 us (38%)
  Pallas kernels  26 us (29%)
  blocking collectives  14.6 us (16%)
  waiting for transfers between devices  10.2 us (11%)
  local copies, waits for them, and re-layouts  2.38 us (3%)
  other arithmetic  1.6 us (2%)
    pallas_call x1, Pallas kernels, local(): pl.pallas_call(last_kernel, out_shape=[shape((2, NZ, CTR, D), F32), shape...  18.1 us
    ppermute x6, starting transfers between devices, shifted(): return lax.ppermute(value, axis, [(i, (i + by) % n) for i in range(n)])  15.9 us
    all_to_all x1, blocking collectives, local(): parts = lax.all_to_all(chunk, CENTER_AXES, 0, 0, tiled=True)  14.6 us
    ppermute x6, starting transfers between devices, plane_shift(): return lax.ppermute(value, PLANE_AXES, perm)  11.2 us
    all_to_all x1, starting transfers between devices, local(): scale = jnp.sum(lax.all_to_all(tiny, SCALE_AXES, 0, 0, tiled=True), (0, 1))  7.3 us
    all_to_all x1, waiting for transfers between devices, local(): scale = jnp.sum(lax.all_to_all(tiny, SCALE_AXES, 0, 0, tiled=True), (0, 1))  7.26 us
    pallas_call x1, Pallas kernels, local(): pl.pallas_call(first_kernel, out_shape=[shape((M, D), BF), shape((M, D),...  6.33 us
    ppermute x6, waiting for transfers between devices, shifted(): return lax.ppermute(value, axis, [(i, (i + by) % n) for i in range(n)])  2.92 us
  transfers between devices with their start and end apart: 13, of which 4 were waited for; matrix products, arithmetic and copies ran while one was open for 1% of the time, Pallas kernels for 7%

profile of v3, /device:TPU:1, one launch (start us, length us, event | category | flops | bytes accessed | tf_op | source)
XLA Modules:
  0.0 89.9 jit_solution(13082001568544120299)
XLA Ops:
  0.6 1.6 %prep.1 = (bf16[512,128]{1,0:T(8,128)(2,1)}, bf16[224,128]{1,0:T(8,128)(2,1)}, f32[8,128]{1,0:T(8,128)}) custom-call(bf16[256,128]{1,0:T(8,128)(2,1)} %x_ref.1, bf16[32,256]{1,0:T(8,128)(2,1)} %bitcast.42, bf16[128,128]{1,0:T(8,128)(2,1)} %c_ref.1, bf16[32,128]{1,0:T(8,128)(2,1)} %bitcast.43, bf16[32,128]{1,0:T(8,128)(2,1)} %bitcast.44, ...), custom_call_target="tpu_custom_call" | custom-call | tf_op jit(solution)/shard_map/prep/pallas_call | solution.py:225
  2.2 2.1 %collective-permute-start.5 = (bf16[512,128]{1,0:T(8,128)(2,1)}, bf16[512,128]{1,0:T(8,128)(2,1)S(1)}, u32[]{:S(2)}, u32[]{:S(2)}) collective-permute-start(bf16[512,128]{1,0:T(8,128)(2,1)} %get-tuple-element.14.a_ref), channel_id=1, source_target_pairs={{0,1},{1,2},{2,3},{3,0},{8,24},{9,25},{10,26},{11,27},{16,17},{17,... | collective-permute-start | bytes 393224 | tf_op jit(solution)/shard_map/ppermute | solution.py:206
  4.3 1.4 %collective-permute-start.6 = (bf16[512,128]{1,0:T(8,128)(2,1)}, bf16[512,128]{1,0:T(8,128)(2,1)S(1)}, u32[]{:S(2)}, u32[]{:S(2)}) collective-permute-start(bf16[512,128]{1,0:T(8,128)(2,1)} %get-tuple-element.14.a_ref), channel_id=1, source_target_pairs={{0,3},{1,0},{2,1},{3,2},{8,56},{9,57},{10,58},{11,59},{16,19},{17,... | collective-permute-start | bytes 393224 | tf_op jit(solution)/shard_map/ppermute | solution.py:206
  5.8 1.6 %collective-permute-start.7 = (bf16[512,128]{1,0:T(8,128)(2,1)}, bf16[512,128]{1,0:T(8,128)(2,1)S(1)}, u32[]{:S(2)}, u32[]{:S(2)}) collective-permute-start(bf16[512,128]{1,0:T(8,128)(2,1)} %get-tuple-element.14.a_ref), channel_id=1, source_target_pairs={{0,2},{1,3},{2,0},{3,1},{8,40},{9,41},{10,42},{11,43},{16,18},{17,... | collective-permute-start | bytes 393224 | tf_op jit(solution)/shard_map/ppermute | solution.py:206
  7.4 0.0 copy-start.2
  7.4 1.6 %collective-permute-start = (bf16[224,128]{1,0:T(8,128)(2,1)}, bf16[224,128]{1,0:T(8,128)(2,1)S(1)}, u32[]{:S(2)}, u32[]{:S(2)}) collective-permute-start(bf16[224,128]{1,0:T(8,128)(2,1)} %get-tuple-element.13), channel_id=1, source_target_pairs={{0,4},{4,0},{1,5},{5,1},{2,6},{6,2},{3,7},{7,3},{8,12},{12,8},{9,1... | collective-permute-start | bytes 172040 | tf_op jit(solution)/shard_map/ppermute | solution.py:195
  9.1 0.9 constant_dynamic-update-slice_fusion.4
  9.9 1.3 %collective-permute-done = bf16[224,128]{1,0:T(8,128)(2,1)S(1)} collective-permute-done((bf16[224,128]{1,0:T(8,128)(2,1)}, bf16[224,128]{1,0:T(8,128)(2,1)S(1)}, u32[]{:S(2)}, u32[]{:S(2)}) %collective-permute-start) | collective-permute-done | bytes 57376 | tf_op jit(solution)/shard_map/ppermute | solution.py:195
  11.2 0.0 copy-done.2
  11.2 0.0 copy-start
  11.2 2.8 %collective-permute-start.1 = (bf16[2,224,128]{2,1,0:T(8,128)(2,1)S(1)}, bf16[2,224,128]{2,1,0:T(8,128)(2,1)S(1)}, u32[]{:S(2)}, u32[]{:S(2)}) collective-permute-start(bf16[2,224,128]{2,1,0:T(8,128)(2,1)S(1)} %pad_maximum_fusion.2), channel_id=1, source_target_pairs={{0,64},{64,128},{128,192},{192,0},{1,65},{65,129},{129,193},{193,1... | collective-permute-start | bytes 344072 | tf_op jit(solution)/shard_map/ppermute | solution.py:195
  14.0 2.9 %collective-permute-start.2 = (bf16[2,224,128]{2,1,0:T(8,128)(2,1)S(1)}, bf16[2,224,128]{2,1,0:T(8,128)(2,1)S(1)}, u32[]{:S(2)}, u32[]{:S(2)}) collective-permute-start(bf16[2,224,128]{2,1,0:T(8,128)(2,1)S(1)} %pad_maximum_fusion.2), channel_id=1, source_target_pairs={{0,192},{64,0},{128,64},{192,128},{1,193},{65,1},{129,65},{193,129... | collective-permute-start | bytes 344072 | tf_op jit(solution)/shard_map/ppermute | solution.py:195
  16.9 0.0 collective-permute-done.5.b_ref
  16.9 4.5 %collective-permute-start.3 = (bf16[2,224,128]{2,1,0:T(8,128)(2,1)S(1)}, bf16[2,224,128]{2,1,0:T(8,128)(2,1)S(1)}, u32[]{:S(2)}, u32[]{:S(2)}) collective-permute-start(bf16[2,224,128]{2,1,0:T(8,128)(2,1)S(1)} %pad_maximum_fusion.2), channel_id=1, source_target_pairs={{0,128},{64,192},{128,0},{192,64},{1,129},{65,193},{129,1},{193,65... | collective-permute-start | bytes 344072 | tf_op jit(solution)/shard_map/ppermute | solution.py:195
  21.4 0.0 collective-permute-done.6.c_ref
  21.4 0.0 collective-permute-done.7.d_ref
  21.4 0.0 copy-done
  21.4 0.1 pad_maximum_fusion
  21.5 3.3 %collective-permute-start.10 = (bf16[4,512,128]{2,1,0:T(8,128)(2,1)S(1)}, bf16[4,512,128]{2,1,0:T(8,128)(2,1)S(1)}, u32[]{:S(2)}, u32[]{:S(2)}) collective-permute-start(bf16[4,512,128]{2,1,0:T(8,128)(2,1)S(1)} %pad_maximum_fusion), channel_id=1, source_target_pairs={{0,32},{1,33},{2,34},{3,35},{8,10},{9,11},{10,8},{11,9},{16,48},{1... | collective-permute-start | bytes 1572872 | tf_op jit(solution)/shard_map/ppermute | solution.py:206
  24.8 0.6 collective-permute-start.8
  25.3 0.0 collective-permute-done.1
  25.3 2.1 %collective-permute-start.9 = (bf16[4,512,128]{2,1,0:T(8,128)(2,1)S(1)}, bf16[4,512,128]{2,1,0:T(8,128)(2,1)S(1)}, u32[]{:S(2)}, u32[]{:S(2)}) collective-permute-start(bf16[4,512,128]{2,1,0:T(8,128)(2,1)S(1)} %pad_maximum_fusion), channel_id=1, source_target_pairs={{0,48},{1,49},{2,50},{3,51},{8,11},{9,8},{10,9},{11,10},{16,0},{17... | collective-permute-start | bytes 1572872 | tf_op jit(solution)/shard_map/ppermute | solution.py:206
  27.5 0.0 collective-permute-done.2
  27.5 0.3 collective-permute-done.3
  27.9 3.8 %collective-permute-start.4 = (bf16[8,224,128]{2,1,0:T(8,128)(2,1)S(1)}, bf16[8,224,128]{2,1,0:T(8,128)(2,1)S(1)}, u32[]{:S(2)}, u32[]{:S(2)}) collective-permute-start(bf16[8,224,128]{2,1,0:T(8,128)(2,1)S(1)} %constant_dynamic-update-slice_fusion.own_ref), channel_id=1, source_target_pairs={{0,8},{8,0},{1,9},{9,1},{2,10},{10,2},{3,11},{11,3},{4,12},{12,4},... | collective-permute-start | bytes 1376264 | tf_op jit(solution)/shard_map/ppermute | solution.py:195
  31.7 0.1 pad.5.clone
  31.8 0.1 pad_add_fusion.at_ref
  31.8 1.3 %collective-permute-done.4.oth_ref = bf16[8,224,128]{2,1,0:T(8,128)(2,1)S(1)} collective-permute-done((bf16[8,224,128]{2,1,0:T(8,128)(2,1)S(1)}, bf16[8,224,128]{2,1,0:T(8,128)(2,1)S(1)}, u32[]{:S(2)}, u32[]{:S(2)}) %collective-permute-start.4) | collective-permute-done | bytes 458784 | tf_op jit(solution)/shard_map/ppermute | solution.py:195
  33.1 6.3 %pairs_first.1 = (bf16[2048,128]{1,0:T(8,128)(2,1)S(1)}, f32[2048,128]{1,0:T(8,128)S(1)}, bf16[2048,128]{1,0:T(8,128)(2,1)S(1)}, bf16[2048,128]{1,0:T(8,128)(2,1...) custom-call(bf16[8,224,128]{2,1,0:T(8,128)(2,1)S(1)} %constant_dynamic-update-slice_fusion.own_ref, ...), custom_call_target="tpu_custom_call" | custom-call | flops 1 | bytes 1 | tf_op jit(solution)/shard_map/pairs_first/pallas_call | solution.py:247
  39.4 0.0 collective-permute-done.10.c_ref
  39.5 0.0 collective-permute-done.8.a_ref
  39.5 0.0 collective-permute-done.9.b_ref
  39.5 0.0 copy-start.1
  39.5 0.7 copy-done.1
  40.2 18.1 %pairs_last.1 = (f32[2,8,128,128]{3,2,1,0:T(8,128)S(1)}, f32[8,128]{1,0:T(8,128)S(1)}) custom-call(s32[2]{0:T(128)S(1)} %pad_add_fusion.at_ref, bf16[2048,128]{1,0:T(8,128)(2,1)S(1)} %get-tuple-element.15.ca, f32[2048,128]{1,0:T(8,128)S(1)} %get-tuple-element.16.hc, bf16[2048,128]{1,0:T(8,128)(2,1)S(1)} %get-tuple-element.17.us, ...), custom_call_target="tpu_custom_call" | custom-call | flops 5435817984 | bytes 4194304 | tf_op jit(solution)/shard_map/pairs_last/pallas_call | solution.py:265
  58.3 0.7 broadcast_in_dim.6
  59.0 7.3 %all-to-all-start = ((f32[32,8,128]{2,1,0:T(8,128)}), f32[32,8,128]{2,1,0:T(8,128)S(1)}, u32[]{:S(2)}, u32[]{:S(2)}) async-start(f32[32,8,128]{2,1,0:T(8,128)} %broadcast_in_dim.6), calls=%async_computation | async-start | bytes 262144 | tf_op jit(solution)/shard_map/all_to_all | solution.py:277
  66.3 0.3 collective-permute-start.11
  66.6 7.3 %all-to-all-done = f32[32,8,128]{2,1,0:T(8,128)S(1)} async-done(((f32[32,8,128]{2,1,0:T(8,128)}), f32[32,8,128]{2,1,0:T(8,128)S(1)}, u32[]{:S(2)}, u32[]{:S(2)}) %all-to-all-start) | async-done | bytes 131104 | tf_op jit(solution)/shard_map/all_to_all | solution.py:277
  74.0 0.1 maximum_maximum_fusion
  74.0 0.0 collective-permute-done.11
  74.0 0.1 fusion
  74.2 14.6 %all_to_all.10 = bf16[8,144,128]{2,1,0:T(8,128)(2,1)S(1)} all-to-all(bf16[8,144,128]{2,1,0:T(8,128)(2,1)S(1)} %pad_maximum_fusion.1), channel_id=1, replica_groups=mesh['zh'=4,'y'=4,'core'=2,'zl'=2,'x'=4] {'zh','zl'}, dimensions={0} | all-to-all | bytes 589824 | tf_op jit(solution)/shard_map/all_to_all | solution.py:280
  88.7 0.5 bitcast_divide_fusion
  89.3 0.7 convert_reduce_fusion
  (13 shorter events, 0.2 us)
Async XLA Ops:
  2.2 14.7 %collective-permute-start.5 = (bf16[512,128]{1,0:T(8,128)(2,1)}, bf16[512,128]{1,0:T(8,128)(2,1)S(1)}, u32[]{:S(2)}, u32[]{:S(2)}) collective-permute-start(bf16[512,128]{1,0:T(8,128)(2,1)} %get-tuple-element.14.a_ref), channel_id=1, source_target_pairs={{0,1},{1,2},{2,3},{3,0},{8,24},{9,25},{10,26},{11,27},{16,17},{17,... | collective-permute-start | bytes 393224 | tf_op jit(solution)/shard_map/ppermute | solution.py:206
  4.3 17.0 %collective-permute-start.6 = (bf16[512,128]{1,0:T(8,128)(2,1)}, bf16[512,128]{1,0:T(8,128)(2,1)S(1)}, u32[]{:S(2)}, u32[]{:S(2)}) collective-permute-start(bf16[512,128]{1,0:T(8,128)(2,1)} %get-tuple-element.14.a_ref), channel_id=1, source_target_pairs={{0,3},{1,0},{2,1},{3,2},{8,56},{9,57},{10,58},{11,59},{16,19},{17,... | collective-permute-start | bytes 393224 | tf_op jit(solution)/shard_map/ppermute | solution.py:206
  5.8 15.6 %collective-permute-start.7 = (bf16[512,128]{1,0:T(8,128)(2,1)}, bf16[512,128]{1,0:T(8,128)(2,1)S(1)}, u32[]{:S(2)}, u32[]{:S(2)}) collective-permute-start(bf16[512,128]{1,0:T(8,128)(2,1)} %get-tuple-element.14.a_ref), channel_id=1, source_target_pairs={{0,2},{1,3},{2,0},{3,1},{8,40},{9,41},{10,42},{11,43},{16,18},{17,... | collective-permute-start | bytes 393224 | tf_op jit(solution)/shard_map/ppermute | solution.py:206
  7.4 3.8 %copy-start.2 = (bf16[224,128]{1,0:T(8,128)(2,1)S(1)}, bf16[224,128]{1,0:T(8,128)(2,1)}, u32[]{:S(2)}) copy-start(bf16[224,128]{1,0:T(8,128)(2,1)} %get-tuple-element.13) | copy-start | bytes 172036
  7.4 3.8 %collective-permute-start = (bf16[224,128]{1,0:T(8,128)(2,1)}, bf16[224,128]{1,0:T(8,128)(2,1)S(1)}, u32[]{:S(2)}, u32[]{:S(2)}) collective-permute-start(bf16[224,128]{1,0:T(8,128)(2,1)} %get-tuple-element.13), channel_id=1, source_target_pairs={{0,4},{4,0},{1,5},{5,1},{2,6},{6,2},{3,7},{7,3},{8,12},{12,8},{9,1... | collective-permute-start | bytes 172040 | tf_op jit(solution)/shard_map/ppermute | solution.py:195
  11.2 10.2 %copy-start = (bf16[512,128]{1,0:T(8,128)(2,1)S(1)}, bf16[512,128]{1,0:T(8,128)(2,1)}, u32[]{:S(2)}) copy-start(bf16[512,128]{1,0:T(8,128)(2,1)} %get-tuple-element.14.a_ref) | copy-start | bytes 393220
  11.2 14.1 %collective-permute-start.1 = (bf16[2,224,128]{2,1,0:T(8,128)(2,1)S(1)}, bf16[2,224,128]{2,1,0:T(8,128)(2,1)S(1)}, u32[]{:S(2)}, u32[]{:S(2)}) collective-permute-start(bf16[2,224,128]{2,1,0:T(8,128)(2,1)S(1)} %pad_maximum_fusion.2), channel_id=1, source_target_pairs={{0,64},{64,128},{128,192},{192,0},{1,65},{65,129},{129,193},{193,1... | collective-permute-start | bytes 344072 | tf_op jit(solution)/shard_map/ppermute | solution.py:195
  14.0 13.5 %collective-permute-start.2 = (bf16[2,224,128]{2,1,0:T(8,128)(2,1)S(1)}, bf16[2,224,128]{2,1,0:T(8,128)(2,1)S(1)}, u32[]{:S(2)}, u32[]{:S(2)}) collective-permute-start(bf16[2,224,128]{2,1,0:T(8,128)(2,1)S(1)} %pad_maximum_fusion.2), channel_id=1, source_target_pairs={{0,192},{64,0},{128,64},{192,128},{1,193},{65,1},{129,65},{193,129... | collective-permute-start | bytes 344072 | tf_op jit(solution)/shard_map/ppermute | solution.py:195
  16.9 10.9 %collective-permute-start.3 = (bf16[2,224,128]{2,1,0:T(8,128)(2,1)S(1)}, bf16[2,224,128]{2,1,0:T(8,128)(2,1)S(1)}, u32[]{:S(2)}, u32[]{:S(2)}) collective-permute-start(bf16[2,224,128]{2,1,0:T(8,128)(2,1)S(1)} %pad_maximum_fusion.2), channel_id=1, source_target_pairs={{0,128},{64,192},{128,0},{192,64},{1,129},{65,193},{129,1},{193,65... | collective-permute-start | bytes 344072 | tf_op jit(solution)/shard_map/ppermute | solution.py:195
  21.5 18.0 %collective-permute-start.10 = (bf16[4,512,128]{2,1,0:T(8,128)(2,1)S(1)}, bf16[4,512,128]{2,1,0:T(8,128)(2,1)S(1)}, u32[]{:S(2)}, u32[]{:S(2)}) collective-permute-start(bf16[4,512,128]{2,1,0:T(8,128)(2,1)S(1)} %pad_maximum_fusion), channel_id=1, source_target_pairs={{0,32},{1,33},{2,34},{3,35},{8,10},{9,11},{10,8},{11,9},{16,48},{1... | collective-permute-start | bytes 1572872 | tf_op jit(solution)/shard_map/ppermute | solution.py:206
  24.8 14.7 %collective-permute-start.8 = (bf16[4,512,128]{2,1,0:T(8,128)(2,1)S(1)}, bf16[4,512,128]{2,1,0:T(8,128)(2,1)S(1)}, u32[]{:S(2)}, u32[]{:S(2)}) collective-permute-start(bf16[4,512,128]{2,1,0:T(8,128)(2,1)S(1)} %pad_maximum_fusion), channel_id=1, source_target_pairs={{0,16},{1,17},{2,18},{3,19},{8,9},{9,10},{10,11},{11,8},{16,32},{1... | collective-permute-start | bytes 1572872 | tf_op jit(solution)/shard_map/ppermute | solution.py:206
  25.3 14.1 %collective-permute-start.9 = (bf16[4,512,128]{2,1,0:T(8,128)(2,1)S(1)}, bf16[4,512,128]{2,1,0:T(8,128)(2,1)S(1)}, u32[]{:S(2)}, u32[]{:S(2)}) collective-permute-start(bf16[4,512,128]{2,1,0:T(8,128)(2,1)S(1)} %pad_maximum_fusion), channel_id=1, source_target_pairs={{0,48},{1,49},{2,50},{3,51},{8,11},{9,8},{10,9},{11,10},{16,0},{17... | collective-permute-start | bytes 1572872 | tf_op jit(solution)/shard_map/ppermute | solution.py:206
  27.9 5.2 %collective-permute-start.4 = (bf16[8,224,128]{2,1,0:T(8,128)(2,1)S(1)}, bf16[8,224,128]{2,1,0:T(8,128)(2,1)S(1)}, u32[]{:S(2)}, u32[]{:S(2)}) collective-permute-start(bf16[8,224,128]{2,1,0:T(8,128)(2,1)S(1)} %constant_dynamic-update-slice_fusion.own_ref), channel_id=1, source_target_pairs={{0,8},{8,0},{1,9},{9,1},{2,10},{10,2},{3,11},{11,3},{4,12},{12,4},... | collective-permute-start | bytes 1376264 | tf_op jit(solution)/shard_map/ppermute | solution.py:195
  39.5 0.7 copy-start.1
  59.0 14.9 %all-to-all-start = ((f32[32,8,128]{2,1,0:T(8,128)}), f32[32,8,128]{2,1,0:T(8,128)S(1)}, u32[]{:S(2)}, u32[]{:S(2)}) async-start(f32[32,8,128]{2,1,0:T(8,128)} %broadcast_in_dim.6), calls=%async_computation | async-start | bytes 262144 | tf_op jit(solution)/shard_map/all_to_all | solution.py:277
  66.3 7.7 %collective-permute-start.11 = (f32[8,128,128]{2,1,0:T(8,128)S(1)}, f32[8,128,128]{2,1,0:T(8,128)S(1)}, u32[]{:S(2)}, u32[]{:S(2)}) collective-permute-start(f32[8,128,128]{2,1,0:T(8,128)S(1)} %slice_bitcast_fusion), channel_id=1, source_target_pairs={{0,8},{8,0},{1,9},{9,1},{2,10},{10,2},{3,11},{11,3},{4,12},{12,4},... | collective-permute-start | bytes 1572872 | tf_op jit(solution)/shard_map/ppermute | solution.py:195

commit v4 on v3

v4 whole, which is shorter than its diff:
```python
import functools

import jax
import jax.numpy as jnp
from jax import lax
from jax.experimental import pallas as pl
from jax.experimental.pallas import tpu as pltpu
from jax.sharding import Mesh, PartitionSpec as P

BF = jnp.bfloat16
F32 = jnp.float32
AXES = ("zh", "y", "core", "zl", "x")
SIZES = (4, 4, 2, 2, 4)
CENTER_AXES = ("zh", "zl")
PLANE_AXES = ("y", "core", "x")
SCALE_AXES = ("y", "x", "core")
D = 128
R = 32
PTS = 256
CTR = 128
CROWS = CTR + 3 * R
BASE = PTS + CTR
PROWS = BASE + 4 * R
TAIL = 16
NZ = 8
NB = 2 * NZ
NSIDE = 4
SHIFTS = (0, 1, 3, 2)
SPAN = 1024
PER = {4: 4, 12: 12}
M = NB * CTR
VM = pl.BlockSpec(memory_space=pltpu.VMEM)
SM = pl.BlockSpec(memory_space=pltpu.SMEM)
PARAMS = pltpu.CompilerParams(vmem_limit_bytes=44 * 2**20)


def dot_nn(a, b):
    return lax.dot_general(a, b, (((1,), (0,)), ((), ())), preferred_element_type=F32)


def fold(v):
    return jnp.sum(v.reshape(v.shape[0] // 8, 8, v.shape[1]), axis=0)


def prep_kernel(x_ref, v_ref, c_ref, s_ref, l_ref, r_ref, ls_ref, pp_ref, cb_ref, lv_ref):
    ls = ls_ref[...]
    x = (x_ref[...].astype(F32) / ls).astype(BF)
    c = (c_ref[...].astype(F32) / ls).astype(BF)
    lt, rt = l_ref[...], r_ref[...]
    pp_ref[...] = jnp.concatenate([x, c, v_ref[:, 0:CTR], v_ref[:, CTR:PTS], rt, lt], 0)
    cb_ref[...] = jnp.concatenate([c, s_ref[...], lt, rt], 0)
    lv_ref[...] = jnp.broadcast_to(ls, lv_ref.shape)


def set_centers(held, ct, hc, ut):
    for j in range(NB):
        h, i = divmod(j, NZ)
        ref, i = (held[2 * h], i) if i < 2 else (held[2 * h + 1], i - 2)
        cols = slice(j * CTR, (j + 1) * CTR)
        t = ref[i, 0:CTR, :].astype(F32).T
        ct[:, cols] = t.astype(BF)
        hc[:, cols] = jnp.broadcast_to(0.5 * jnp.sum(t * t, axis=0, keepdims=True), (8, CTR))
        ut[0 : 3 * R, cols] = ref[i, CTR:CROWS, :]
        ut[3 * R : D, cols] = jnp.zeros((R, CTR), BF)


def turn(rows, vrows, first, xt, hx, vs, slot, at):
    span = slice(at * 128, (at + 1) * 128)
    f = rows.astype(F32)
    xt[slot, :, span] = f.T.astype(BF)
    hx[slot, span, :] = jnp.broadcast_to(0.5 * jnp.sum(f * f, axis=1, keepdims=True), (128, 128))
    above = [jnp.zeros((first, 128), F32)] if first else []
    below = jnp.zeros((128 - first - vrows.shape[0], 128), F32)
    vs[slot, span, :] = jnp.concatenate(above + [vrows.astype(F32), below], 0).T.astype(BF)


def sweep(x, xt, hx, vs, ct, hc, ut, gt, qt, want_rows):
    n = x.shape[0]
    rows = None
    for m in range(0, M, SPAN):
        cols = slice(m, m + SPAN)
        cross = dot_nn(x, ct[:, cols])
        prod = dot_nn(vs, ut[:, cols])
        parts = []
        for k in range(SPAN // 128):
            part = slice(k * 128, (k + 1) * 128)
            h = hc[0:1, m + k * 128 : m + (k + 1) * 128]
            parts.append(jnp.exp((cross[:, part] - hx) - h) * prod[:, part])
        w = jnp.concatenate(parts, 1)
        gt[:, cols] += dot_nn(xt, w.astype(BF))
        qt[:, cols] += fold(w)
        if want_rows:
            for p in parts:
                rows = p if rows is None else rows + p
    return rows


def add_pairs(blocks, count, ct, hc, ut, gt, qt, xt, hx, vs, yt, hy, us):
    gt[...] = jnp.zeros_like(gt)
    qt[...] = jnp.zeros_like(qt)
    per = PER[count]
    steps, csteps = count // NSIDE, count // per

    def turn_points(a, slot):
        for k in range(2 * NSIDE):
            i, h = NSIDE * a + k // 2, k % 2
            vrows = blocks[i, BASE + h * R : BASE + (h + 1) * R, :]
            turn(blocks[i, h * 128 : (h + 1) * 128, :], vrows, 0, xt, hx, vs, slot, k)

    def turn_centers(a, slot):
        for k in range(per):
            i = per * a + k
            turn(blocks[i, PTS:BASE, :], blocks[i, BASE + 2 * R : PROWS, :], R, yt, hy, us, slot, k)

    def points_step(a, ell):
        slot = lax.rem(a, 2)
        x = jnp.concatenate([blocks[NSIDE * a + k, 0:PTS, :] for k in range(NSIDE)], 0)
        rows = sweep(x, xt[slot], hx[slot], vs[slot], ct, hc, ut, gt, qt, True)
        if steps > 1:
            turn_points(lax.min(a + 1, steps - 1), 1 - slot)
        xf = x.astype(F32)
        return ell + fold(jnp.sum(rows, axis=1, keepdims=True) * (xf * xf))

    def centers_step(a, carry):
        slot = lax.rem(a, 2)
        c = jnp.concatenate([blocks[per * a + k, PTS:BASE, :] for k in range(per)], 0)
        sweep(c, yt[slot], hy[slot], us[slot], ct, hc, ut, gt, qt, False)
        if csteps > 1:
            turn_centers(lax.min(a + 1, csteps - 1), 1 - slot)
        return carry

    turn_points(0, 0)
    ell = lax.fori_loop(0, steps, points_step, jnp.zeros((8, D), F32))
    both = jnp.zeros((D, CTR), F32)
    for j in range(NB):
        cols = slice(j * CTR, (j + 1) * CTR)
        both = both + ct[:, cols].astype(F32) * gt[:, cols]
    turn_centers(0, 0)
    lax.fori_loop(0, csteps, centers_step, 0)
    return ell, both


def block_terms(j, ct, gt, qt):
    cols = slice(j * CTR, (j + 1) * CTR)
    c = ct[:, cols].astype(F32)
    q = jnp.sum(qt[:, cols], axis=0, keepdims=True)
    t = gt[:, cols] - q * c
    return t, c * t


def first_kernel(h0, h1, h2, h3, a_ref, b_ref, c_ref, d_ref, lv_ref, ct, hc, ut, t_ref, s_ref, gt, qt, *work):
    set_centers((h0, h1, h2, h3), ct, hc, ut)
    blocks = work[-1]
    for k, ref in enumerate((a_ref, b_ref, c_ref, d_ref)):
        blocks[k] = ref[...]
    ell, both = add_pairs(blocks, NSIDE, ct, hc, ut, gt, qt, *work[:-1])
    for j in range(NB):
        t, s = block_terms(j, ct, gt, qt)
        t_ref[:, j * CTR : (j + 1) * CTR] = t
        both = both + s
    s_ref[0:8, :] = ell - fold(both.T)
    s_ref[8:16, :] = lv_ref[...]


def last_kernel(at_ref, ct, hc, ut, t0, s0, a_ref, b_ref, c_ref, t_ref, s_ref, gt, qt, *work):
    blocks = work[-1]
    for k, ref in enumerate((a_ref, b_ref, c_ref)):
        for i in range(NSIDE):
            blocks[NSIDE * k + i] = ref[i]
    ell, both = add_pairs(blocks, 3 * NSIDE, ct, hc, ut, gt, qt, *work[:-1])
    inv = 1.0 / s0[8:9, :]
    zh, zl = at_ref[0], at_ref[1]
    for j in range(NB):
        t, s = block_terms(j, ct, gt, qt)
        both = both + s
        h, i = divmod(j, NZ)
        place = lax.rem(zh + 4 - SHIFTS[i // 2], 4) * 2 + (zl if i % 2 == 0 else 1 - zl)
        t_ref[h, place] = (t0[:, j * CTR : (j + 1) * CTR] + t).T * inv
    scale = jnp.sum(s0[0:8, :] + ell - fold(both.T), axis=0, keepdims=True)
    s_ref[...] = jnp.broadcast_to(scale[None], s_ref.shape)


def shifted(value, axis, by):
    n = dict(zip(AXES, SIZES))[axis]
    return lax.ppermute(value, axis, [(i, (i + by) % n) for i in range(n)])


def plane_shift(value, by, swap):
    perm = []
    for y in range(4):
        for core in range(2):
            for x in range(4):
                along_x = (core == 0) != swap
                ty, tx = (y, (x + by) % 4) if along_x else ((y + by) % 4, x)
                perm.append(((y * 2 + core) * 4 + x, (ty * 2 + core) * 4 + tx))
    return lax.ppermute(value, PLANE_AXES, perm)


def pieces(s):
    a = s.astype(BF)
    rest = s - a.astype(F32)
    b = rest.astype(BF)
    c = (rest - b.astype(F32)).astype(BF)
    return jnp.concatenate([jnp.stack([a, b, c]), jnp.zeros((TAIL - 3, D), BF)], 0)


def cost(peers):
    rows = peers * BASE
    return pl.CostEstimate(flops=2 * rows * M * 288, bytes_accessed=2**22, transcendentals=rows * M)


def work_space(count):
    n, nc = NSIDE * PTS, PER[count] * CTR
    return [
        pltpu.VMEM((D, M), F32),
        pltpu.VMEM((8, M), F32),
        pltpu.VMEM((2, D, n), BF),
        pltpu.VMEM((2, n, 128), F32),
        pltpu.VMEM((2, n, 128), BF),
        pltpu.VMEM((2, D, nc), BF),
        pltpu.VMEM((2, nc, 128), F32),
        pltpu.VMEM((2, nc, 128), BF),
        pltpu.VMEM((count, PROWS, D), BF),
    ]


def first_call(*args):
    shape = jax.ShapeDtypeStruct
    return pl.pallas_call(
        first_kernel,
        out_shape=[
            shape((D, M), BF),
            shape((8, M), F32),
            shape((D, M), BF),
            shape((D, M), F32),
            shape((16, D), F32),
        ],
        in_specs=[VM] * 9,
        out_specs=[VM] * 5,
        scratch_shapes=work_space(NSIDE),
        compiler_params=PARAMS,
        cost_estimate=pl.CostEstimate(flops=1, bytes_accessed=1, transcendentals=0),
        name="pairs_first",
    )(*args)


def last_call(*args):
    shape = jax.ShapeDtypeStruct
    return pl.pallas_call(
        last_kernel,
        out_shape=[shape((2, NZ, CTR, D), F32), shape((32, 1, D), F32)],
        in_specs=[SM] + [VM] * 8,
        out_specs=[VM] * 2,
        scratch_shapes=work_space(3 * NSIDE),
        compiler_params=PARAMS,
        cost_estimate=cost(3 * NSIDE),
        name="pairs_last",
    )(*args)


def local(points, adjoint_rows, centers, solution_rows, center_left, center_right, lengthscale):
    ls = lengthscale.reshape(1, D)
    shape = jax.ShapeDtypeStruct
    pp, cb, lv = pl.pallas_call(
        prep_kernel,
        out_shape=[shape((PROWS, D), BF), shape((CROWS, D), BF), shape((8, D), F32)],
        in_specs=[VM] * 7,
        out_specs=[VM] * 3,
        name="prep",
    )(points, adjoint_rows.T, centers, solution_rows.T, center_left.T, center_right.T, ls)
    side = [pp] + [plane_shift(pp, by, False) for by in (1, 3, 2)]
    two = jnp.stack([cb, shifted(cb, "zl", 1)])
    line = jnp.stack(side)
    rest = [plane_shift(line, by, True) for by in (1, 3, 2)]
    two_other = shifted(two, "core", 1)
    six = jnp.concatenate([shifted(two, "zh", by) for by in SHIFTS[1:]], 0)
    held = (two, six, two_other, shifted(six, "core", 1))
    at = jnp.stack([lax.axis_index("zh"), lax.axis_index("zl")]).astype(jnp.int32)
    terms, scale = last_call(at, *first_call(*held, *side, lv), *rest)
    swapped = shifted(terms[1], "core", 1)
    scale = jnp.sum(lax.all_to_all(scale, SCALE_AXES, 0, 0, tiled=True), (0, 1))
    mine = (terms[0] + swapped).astype(BF)
    chunk = jnp.concatenate([mine, jnp.broadcast_to(pieces(scale)[None], (NZ, TAIL, D))], 1)
    parts = lax.all_to_all(chunk, CENTER_AXES, 0, 0, tiled=True)
    total = jnp.sum(parts[:, 0:CTR].astype(F32), 0)
    return total, jnp.sum(parts[:, CTR:].astype(F32), (0, 1)) / lv[0]


def solution(mesh):
    grid = Mesh(mesh.devices.reshape(SIZES), AXES)
    rows = P(AXES, None)
    return jax.shard_map(
        local,
        mesh=grid,
        in_specs=(rows,) * 6 + (P(),),
        out_specs=(rows, P()),
        check_vma=False,
    )
```

time: 90.2 us -> 85.3 us (0.946)
  starting transfers between devices: 34.4 us -> 31.7 us
  local copies, waits for them, and re-layouts: 2.38 us -> 0.18 us
  Pallas kernels: 26 us -> 24.2 us
  waiting for transfers between devices: 10.2 us -> 11.2 us
    ppermute x6, starting transfers between devices: 11.2 us -> 8.06 us  [plane_shift(): return lax.ppermute(value, PLANE_AXES, perm)]
    ppermute x6, waiting for transfers between devices: 0.02 us -> 2.29 us  [plane_shift(): return lax.ppermute(value, PLANE_AXES, perm)]
    pallas_call x2, Pallas kernels: 24.5 us -> 22.6 us  [the longest x1 17 us: last_call(): pl.pallas_call(last_kernel, out_shape=[shape((2, NZ, CTR, D), F32), shape...]
    unnamed x10 -> x6, local copies, waits for them, and re-layouts: 1.58 us -> 0.03 us
    ppermute x6 -> x7, waiting for transfers between devices: 2.92 us -> 2.38 us  [shifted(): return lax.ppermute(value, axis, [(i, (i + by) % n) for i in range(n)])]
    ppermute x6 -> x7, starting transfers between devices: 15.9 us -> 16.3 us  [shifted(): return lax.ppermute(value, axis, [(i, (i + by) % n) for i in range(n)])]
  transfers between devices with their start and end apart: 13 -> 14, of which waited for: 4 -> 4; matrix products, arithmetic and copies ran while one was open for 1% -> 2% of each run, Pallas kernels for 7% -> 7%
where the time goes in v4:
time: 85.3 us; the launch traced here: 85 us
  starting transfers between devices  31.7 us (37%)
  Pallas kernels  24.2 us (28%)
  blocking collectives  14.6 us (17%)
  waiting for transfers between devices  11.2 us (13%)
  other arithmetic  2.43 us (3%)
    pallas_call x1, Pallas kernels, last_call(): pl.pallas_call(last_kernel, out_shape=[shape((2, NZ, CTR, D), F32), shape...  17 us
    ppermute x7, starting transfers between devices, shifted(): return lax.ppermute(value, axis, [(i, (i + by) % n) for i in range(n)])  16.3 us
    all_to_all x1, blocking collectives, local(): parts = lax.all_to_all(chunk, CENTER_AXES, 0, 0, tiled=True)  14.6 us
    ppermute x6, starting transfers between devices, plane_shift(): return lax.ppermute(value, PLANE_AXES, perm)  8.06 us
    all_to_all x1, starting transfers between devices, local(): scale = jnp.sum(lax.all_to_all(scale, SCALE_AXES, 0, 0, tiled=True), (0, 1))  7.34 us
    all_to_all x1, waiting for transfers between devices, local(): scale = jnp.sum(lax.all_to_all(scale, SCALE_AXES, 0, 0, tiled=True), (0, 1))  6.5 us
    pallas_call x1, Pallas kernels, first_call(): pl.pallas_call(first_kernel, out_shape=[shape((D, M), BF), shape((8, M),...  5.65 us
    ppermute x7, waiting for transfers between devices, shifted(): return lax.ppermute(value, axis, [(i, (i + by) % n) for i in range(n)])  2.38 us
  transfers between devices with their start and end apart: 14, of which 4 were waited for; matrix products, arithmetic and copies ran while one was open for 2% of the time, Pallas kernels for 7%

profile of v4, /device:TPU:1, one launch (start us, length us, event | category | flops | bytes accessed | tf_op | source)
XLA Modules:
  0.0 85.0 jit_solution(5386852570958841522)
XLA Ops:
  0.6 1.6 %prep.1 = (bf16[512,128]{1,0:T(8,128)(2,1)}, bf16[224,128]{1,0:T(8,128)(2,1)}, f32[8,128]{1,0:T(8,128)}) custom-call(bf16[256,128]{1,0:T(8,128)(2,1)} %x_ref.1, bf16[32,256]{1,0:T(8,128)(2,1)} %bitcast.40, bf16[128,128]{1,0:T(8,128)(2,1)} %c_ref.1, bf16[32,128]{1,0:T(8,128)(2,1)} %bitcast.41, bf16[32,128]{1,0:T(8,128)(2,1)} %bitcast.42, ...), custom_call_target="tpu_custom_call" | custom-call | tf_op jit(solution)/shard_map/prep/pallas_call | solution.py:264
  2.2 0.0 copy-start
  2.2 2.5 %collective-permute-start = (bf16[224,128]{1,0:T(8,128)(2,1)}, bf16[224,128]{1,0:T(8,128)(2,1)S(1)}, u32[]{:S(2)}, u32[]{:S(2)}) collective-permute-start(bf16[224,128]{1,0:T(8,128)(2,1)} %get-tuple-element.12), channel_id=1, source_target_pairs={{0,4},{4,0},{1,5},{5,1},{2,6},{6,2},{3,7},{7,3},{8,12},{12,8},{9,1... | collective-permute-start | bytes 172040 | tf_op jit(solution)/shard_map/ppermute | solution.py:185
  4.7 1.3 %collective-permute-start.6 = (bf16[512,128]{1,0:T(8,128)(2,1)}, bf16[512,128]{1,0:T(8,128)(2,1)S(1)}, u32[]{:S(2)}, u32[]{:S(2)}) collective-permute-start(bf16[512,128]{1,0:T(8,128)(2,1)} %get-tuple-element.13.a_ref), channel_id=1, source_target_pairs={{0,1},{1,2},{2,3},{3,0},{8,24},{9,25},{10,26},{11,27},{16,17},{17,... | collective-permute-start | bytes 393224 | tf_op jit(solution)/shard_map/ppermute | solution.py:196
  6.0 1.4 %collective-permute-start.7 = (bf16[512,128]{1,0:T(8,128)(2,1)}, bf16[512,128]{1,0:T(8,128)(2,1)S(1)}, u32[]{:S(2)}, u32[]{:S(2)}) collective-permute-start(bf16[512,128]{1,0:T(8,128)(2,1)} %get-tuple-element.13.a_ref), channel_id=1, source_target_pairs={{0,3},{1,0},{2,1},{3,2},{8,56},{9,57},{10,58},{11,59},{16,19},{17,... | collective-permute-start | bytes 393224 | tf_op jit(solution)/shard_map/ppermute | solution.py:196
  7.4 1.6 %collective-permute-start.8 = (bf16[512,128]{1,0:T(8,128)(2,1)}, bf16[512,128]{1,0:T(8,128)(2,1)S(1)}, u32[]{:S(2)}, u32[]{:S(2)}) collective-permute-start(bf16[512,128]{1,0:T(8,128)(2,1)} %get-tuple-element.13.a_ref), channel_id=1, source_target_pairs={{0,2},{1,3},{2,0},{3,1},{8,40},{9,41},{10,42},{11,43},{16,18},{17,... | collective-permute-start | bytes 393224 | tf_op jit(solution)/shard_map/ppermute | solution.py:196
  9.1 0.0 collective-permute-done
  9.1 0.8 pad_maximum_fusion.2.h0
  9.9 3.1 %collective-permute-start.1 = (bf16[2,224,128]{2,1,0:T(8,128)(2,1)S(1)}, bf16[2,224,128]{2,1,0:T(8,128)(2,1)S(1)}, u32[]{:S(2)}, u32[]{:S(2)}) collective-permute-start(bf16[2,224,128]{2,1,0:T(8,128)(2,1)S(1)} %pad_maximum_fusion.2.h0), channel_id=1, source_target_pairs={{0,64},{64,128},{128,192},{192,0},{1,65},{65,129},{129,193},{193,1... | collective-permute-start | bytes 344072 | tf_op jit(solution)/shard_map/ppermute | solution.py:185
  13.0 2.2 %collective-permute-start.2 = (bf16[2,224,128]{2,1,0:T(8,128)(2,1)S(1)}, bf16[2,224,128]{2,1,0:T(8,128)(2,1)S(1)}, u32[]{:S(2)}, u32[]{:S(2)}) collective-permute-start(bf16[2,224,128]{2,1,0:T(8,128)(2,1)S(1)} %pad_maximum_fusion.2.h0), channel_id=1, source_target_pairs={{0,192},{64,0},{128,64},{192,128},{1,193},{65,1},{129,65},{193,129... | collective-permute-start | bytes 344072 | tf_op jit(solution)/shard_map/ppermute | solution.py:185
  15.2 0.0 collective-permute-done.6.b_ref
  15.2 4.4 %collective-permute-start.3 = (bf16[2,224,128]{2,1,0:T(8,128)(2,1)S(1)}, bf16[2,224,128]{2,1,0:T(8,128)(2,1)S(1)}, u32[]{:S(2)}, u32[]{:S(2)}) collective-permute-start(bf16[2,224,128]{2,1,0:T(8,128)(2,1)S(1)} %pad_maximum_fusion.2.h0), channel_id=1, source_target_pairs={{0,128},{64,192},{128,0},{192,64},{1,129},{65,193},{129,1},{193,65... | collective-permute-start | bytes 344072 | tf_op jit(solution)/shard_map/ppermute | solution.py:185
  19.6 0.0 collective-permute-done.7.c_ref
  19.6 0.0 collective-permute-done.8.d_ref
  19.6 0.0 copy-done
  19.6 0.1 pad_maximum_fusion
  19.7 2.6 %collective-permute-start.10 = (bf16[4,512,128]{2,1,0:T(8,128)(2,1)S(1)}, bf16[4,512,128]{2,1,0:T(8,128)(2,1)S(1)}, u32[]{:S(2)}, u32[]{:S(2)}) collective-permute-start(bf16[4,512,128]{2,1,0:T(8,128)(2,1)S(1)} %pad_maximum_fusion), channel_id=1, source_target_pairs={{0,48},{1,49},{2,50},{3,51},{8,11},{9,8},{10,9},{11,10},{16,0},{17... | collective-permute-start | bytes 1572872 | tf_op jit(solution)/shard_map/ppermute | solution.py:196
  22.2 0.5 collective-permute-start.11
  22.7 0.0 collective-permute-done.1
  22.7 0.6 collective-permute-start.9
  23.4 0.0 collective-permute-done.2
  23.4 1.4 %collective-permute-done.3 = bf16[2,224,128]{2,1,0:T(8,128)(2,1)S(1)} collective-permute-done((bf16[2,224,128]{2,1,0:T(8,128)(2,1)S(1)}, bf16[2,224,128]{2,1,0:T(8,128)(2,1)S(1)}, u32[]{:S(2)}, u32[]{:S(2)}) %collective-permute-start.3) | collective-permute-done | bytes 114720 | tf_op jit(solution)/shard_map/ppermute | solution.py:185
  24.8 3.5 %collective-permute-start.5 = (bf16[6,224,128]{2,1,0:T(8,128)(2,1)S(1)}, bf16[6,224,128]{2,1,0:T(8,128)(2,1)S(1)}, u32[]{:S(2)}, u32[]{:S(2)}) collective-permute-start(bf16[6,224,128]{2,1,0:T(8,128)(2,1)S(1)} %constant_dynamic-update-slice_fusion.h1), channel_id=1, source_target_pairs={{0,8},{8,0},{1,9},{9,1},{2,10},{10,2},{3,11},{11,3},{4,12},{12,4},... | collective-permute-start | bytes 1032200 | tf_op jit(solution)/shard_map/ppermute | solution.py:185
  28.3 0.3 collective-permute-start.4
  28.6 0.1 pad.5.clone
  28.6 0.0 copy-start.1
  28.6 0.1 pad_add_fusion.at_ref
  28.7 1.0 %collective-permute-done.4.h2 = bf16[2,224,128]{2,1,0:T(8,128)(2,1)S(1)} collective-permute-done((bf16[2,224,128]{2,1,0:T(8,128)(2,1)S(1)}, bf16[2,224,128]{2,1,0:T(8,128)(2,1)S(1)}, u32[]{:S(2)}, u32[]{:S(2)}) %collective-permute-start.4) | collective-permute-done | bytes 114720 | tf_op jit(solution)/shard_map/ppermute | solution.py:185
  29.7 0.0 collective-permute-done.5.h3
  29.7 0.0 copy-done.1
  29.7 5.7 %pairs_first.1 = (bf16[128,2048]{1,0:T(8,128)(2,1)S(1)}, f32[8,2048]{1,0:T(8,128)S(1)}, bf16[128,2048]{1,0:T(8,128)(2,1)S(1)}, f32[128,2048]{1,0:T(8,128)S(1)}, f32[16,128]{1,0:T(8,128)S(1)}) custom-call(bf16[2,224,128]{2,1,0:T(8,128)(2,1)S(1)} %pad_maximum_fusion.2.h0, bf16[6,224,128]{2,1,0:T(8,128)(2,1)S(1)} %constant_dynamic-update-slice_fusion.h1, ...), custom_call_target="tpu_custom_call" | custom-call | flops 1 | bytes 1 | tf_op jit(solution)/shard_map/pairs_first/pallas_call | solution.py:229
  35.4 0.0 collective-permute-done.10.b_ref
  35.4 0.0 collective-permute-done.11.c_ref
  35.4 2.3 %collective-permute-done.9.a_ref = bf16[4,512,128]{2,1,0:T(8,128)(2,1)S(1)} collective-permute-done((bf16[4,512,128]{2,1,0:T(8,128)(2,1)S(1)}, bf16[4,512,128]{2,1,0:T(8,128)(2,1)S(1)}, u32[]{:S(2)}, u32[]{:S(2)}) %collective-permute-start.9) | collective-permute-done | bytes 524320 | tf_op jit(solution)/shard_map/ppermute | solution.py:196
  37.7 17.0 %pairs_last.1 = (f32[2,8,128,128]{3,2,1,0:T(8,128)S(1)}, f32[32,1,128]{2,1,0:T(1,128)}) custom-call(s32[2]{0:T(128)S(1)} %pad_add_fusion.at_ref, bf16[128,2048]{1,0:T(8,128)(2,1)S(1)} %get-tuple-element.15.ct, f32[8,2048]{1,0:T(8,128)S(1)} %get-tuple-element.16.hc, bf16[128,2048]{1,0:T(8,128)(2,1)S(1)} %get-tuple-element.17.ut, ...), custom_call_target="tpu_custom_call" | custom-call | flops 5435817984 | bytes 4194304 | tf_op jit(solution)/shard_map/pairs_last/pallas_call | solution.py:249
  54.6 7.3 %all-to-all-start = ((f32[32,1,128]{2,1,0:T(1,128)}), f32[32,1,128]{2,1,0:T(1,128)S(1)}, u32[]{:S(2)}, u32[]{:S(2)}) async-start(f32[32,1,128]{2,1,0:T(1,128)} %get-tuple-element.21), calls=%async_computation | async-start | bytes 32768 | tf_op jit(solution)/shard_map/all_to_all | solution.py:281
  62.0 0.4 collective-permute-start.12
  62.5 6.5 %all-to-all-done = f32[32,1,128]{2,1,0:T(1,128)S(1)} async-done(((f32[32,1,128]{2,1,0:T(1,128)}), f32[32,1,128]{2,1,0:T(1,128)S(1)}, u32[]{:S(2)}, u32[]{:S(2)}) %all-to-all-start) | async-done | bytes 16416 | tf_op jit(solution)/shard_map/all_to_all | solution.py:281
  69.0 0.1 reduce_sum.29
  69.0 0.1 maximum_maximum_fusion
  69.1 0.0 collective-permute-done.12
  69.1 0.1 fusion
  69.2 14.6 %all_to_all.10 = bf16[8,144,128]{2,1,0:T(8,128)(2,1)S(1)} all-to-all(bf16[8,144,128]{2,1,0:T(8,128)(2,1)S(1)} %pad_maximum_fusion.1), channel_id=1, replica_groups=mesh['zh'=4,'y'=4,'core'=2,'zl'=2,'x'=4] {'zh','zl'}, dimensions={0} | all-to-all | bytes 589824 | tf_op jit(solution)/shard_map/all_to_all | solution.py:284
  83.8 0.5 bitcast_divide_fusion
  84.4 0.7 convert_reduce_fusion
  (10 shorter events, 0.2 us)
Async XLA Ops:
  2.2 17.4 %copy-start = (bf16[512,128]{1,0:T(8,128)(2,1)S(1)}, bf16[512,128]{1,0:T(8,128)(2,1)}, u32[]{:S(2)}) copy-start(bf16[512,128]{1,0:T(8,128)(2,1)} %get-tuple-element.13.a_ref) | copy-start | bytes 393220
  2.2 6.9 %collective-permute-start = (bf16[224,128]{1,0:T(8,128)(2,1)}, bf16[224,128]{1,0:T(8,128)(2,1)S(1)}, u32[]{:S(2)}, u32[]{:S(2)}) collective-permute-start(bf16[224,128]{1,0:T(8,128)(2,1)} %get-tuple-element.12), channel_id=1, source_target_pairs={{0,4},{4,0},{1,5},{5,1},{2,6},{6,2},{3,7},{7,3},{8,12},{12,8},{9,1... | collective-permute-start | bytes 172040 | tf_op jit(solution)/shard_map/ppermute | solution.py:185
  4.7 10.5 %collective-permute-start.6 = (bf16[512,128]{1,0:T(8,128)(2,1)}, bf16[512,128]{1,0:T(8,128)(2,1)S(1)}, u32[]{:S(2)}, u32[]{:S(2)}) collective-permute-start(bf16[512,128]{1,0:T(8,128)(2,1)} %get-tuple-element.13.a_ref), channel_id=1, source_target_pairs={{0,1},{1,2},{2,3},{3,0},{8,24},{9,25},{10,26},{11,27},{16,17},{17,... | collective-permute-start | bytes 393224 | tf_op jit(solution)/shard_map/ppermute | solution.py:196
  6.0 13.6 %collective-permute-start.7 = (bf16[512,128]{1,0:T(8,128)(2,1)}, bf16[512,128]{1,0:T(8,128)(2,1)S(1)}, u32[]{:S(2)}, u32[]{:S(2)}) collective-permute-start(bf16[512,128]{1,0:T(8,128)(2,1)} %get-tuple-element.13.a_ref), channel_id=1, source_target_pairs={{0,3},{1,0},{2,1},{3,2},{8,56},{9,57},{10,58},{11,59},{16,19},{17,... | collective-permute-start | bytes 393224 | tf_op jit(solution)/shard_map/ppermute | solution.py:196
  7.4 12.2 %collective-permute-start.8 = (bf16[512,128]{1,0:T(8,128)(2,1)}, bf16[512,128]{1,0:T(8,128)(2,1)S(1)}, u32[]{:S(2)}, u32[]{:S(2)}) collective-permute-start(bf16[512,128]{1,0:T(8,128)(2,1)} %get-tuple-element.13.a_ref), channel_id=1, source_target_pairs={{0,2},{1,3},{2,0},{3,1},{8,40},{9,41},{10,42},{11,43},{16,18},{17,... | collective-permute-start | bytes 393224 | tf_op jit(solution)/shard_map/ppermute | solution.py:196
  9.9 12.8 %collective-permute-start.1 = (bf16[2,224,128]{2,1,0:T(8,128)(2,1)S(1)}, bf16[2,224,128]{2,1,0:T(8,128)(2,1)S(1)}, u32[]{:S(2)}, u32[]{:S(2)}) collective-permute-start(bf16[2,224,128]{2,1,0:T(8,128)(2,1)S(1)} %pad_maximum_fusion.2.h0), channel_id=1, source_target_pairs={{0,64},{64,128},{128,192},{192,0},{1,65},{65,129},{129,193},{193,1... | collective-permute-start | bytes 344072 | tf_op jit(solution)/shard_map/ppermute | solution.py:185
  13.0 10.4 %collective-permute-start.2 = (bf16[2,224,128]{2,1,0:T(8,128)(2,1)S(1)}, bf16[2,224,128]{2,1,0:T(8,128)(2,1)S(1)}, u32[]{:S(2)}, u32[]{:S(2)}) collective-permute-start(bf16[2,224,128]{2,1,0:T(8,128)(2,1)S(1)} %pad_maximum_fusion.2.h0), channel_id=1, source_target_pairs={{0,192},{64,0},{128,64},{192,128},{1,193},{65,1},{129,65},{193,129... | collective-permute-start | bytes 344072 | tf_op jit(solution)/shard_map/ppermute | solution.py:185
  15.2 9.6 %collective-permute-start.3 = (bf16[2,224,128]{2,1,0:T(8,128)(2,1)S(1)}, bf16[2,224,128]{2,1,0:T(8,128)(2,1)S(1)}, u32[]{:S(2)}, u32[]{:S(2)}) collective-permute-start(bf16[2,224,128]{2,1,0:T(8,128)(2,1)S(1)} %pad_maximum_fusion.2.h0), channel_id=1, source_target_pairs={{0,128},{64,192},{128,0},{192,64},{1,129},{65,193},{129,1},{193,65... | collective-permute-start | bytes 344072 | tf_op jit(solution)/shard_map/ppermute | solution.py:185
  19.7 15.7 %collective-permute-start.10 = (bf16[4,512,128]{2,1,0:T(8,128)(2,1)S(1)}, bf16[4,512,128]{2,1,0:T(8,128)(2,1)S(1)}, u32[]{:S(2)}, u32[]{:S(2)}) collective-permute-start(bf16[4,512,128]{2,1,0:T(8,128)(2,1)S(1)} %pad_maximum_fusion), channel_id=1, source_target_pairs={{0,48},{1,49},{2,50},{3,51},{8,11},{9,8},{10,9},{11,10},{16,0},{17... | collective-permute-start | bytes 1572872 | tf_op jit(solution)/shard_map/ppermute | solution.py:196
  22.2 13.2 %collective-permute-start.11 = (bf16[4,512,128]{2,1,0:T(8,128)(2,1)S(1)}, bf16[4,512,128]{2,1,0:T(8,128)(2,1)S(1)}, u32[]{:S(2)}, u32[]{:S(2)}) collective-permute-start(bf16[4,512,128]{2,1,0:T(8,128)(2,1)S(1)} %pad_maximum_fusion), channel_id=1, source_target_pairs={{0,32},{1,33},{2,34},{3,35},{8,10},{9,11},{10,8},{11,9},{16,48},{1... | collective-permute-start | bytes 1572872 | tf_op jit(solution)/shard_map/ppermute | solution.py:196
  22.7 14.9 %collective-permute-start.9 = (bf16[4,512,128]{2,1,0:T(8,128)(2,1)S(1)}, bf16[4,512,128]{2,1,0:T(8,128)(2,1)S(1)}, u32[]{:S(2)}, u32[]{:S(2)}) collective-permute-start(bf16[4,512,128]{2,1,0:T(8,128)(2,1)S(1)} %pad_maximum_fusion), channel_id=1, source_target_pairs={{0,16},{1,17},{2,18},{3,19},{8,9},{9,10},{10,11},{11,8},{16,32},{1... | collective-permute-start | bytes 1572872 | tf_op jit(solution)/shard_map/ppermute | solution.py:196
  24.8 4.9 %collective-permute-start.5 = (bf16[6,224,128]{2,1,0:T(8,128)(2,1)S(1)}, bf16[6,224,128]{2,1,0:T(8,128)(2,1)S(1)}, u32[]{:S(2)}, u32[]{:S(2)}) collective-permute-start(bf16[6,224,128]{2,1,0:T(8,128)(2,1)S(1)} %constant_dynamic-update-slice_fusion.h1), channel_id=1, source_target_pairs={{0,8},{8,0},{1,9},{9,1},{2,10},{10,2},{3,11},{11,3},{4,12},{12,4},... | collective-permute-start | bytes 1032200 | tf_op jit(solution)/shard_map/ppermute | solution.py:185
  28.3 1.4 %collective-permute-start.4 = (bf16[2,224,128]{2,1,0:T(8,128)(2,1)S(1)}, bf16[2,224,128]{2,1,0:T(8,128)(2,1)S(1)}, u32[]{:S(2)}, u32[]{:S(2)}) collective-permute-start(bf16[2,224,128]{2,1,0:T(8,128)(2,1)S(1)} %pad_maximum_fusion.2.h0), channel_id=1, source_target_pairs={{0,8},{8,0},{1,9},{9,1},{2,10},{10,2},{3,11},{11,3},{4,12},{12,4},... | collective-permute-start | bytes 344072 | tf_op jit(solution)/shard_map/ppermute | solution.py:185
  28.6 1.1 %copy-start.1 = (f32[8,128]{1,0:T(8,128)S(1)}, f32[8,128]{1,0:T(8,128)}, u32[]{:S(2)}) copy-start(f32[8,128]{1,0:T(8,128)} %get-tuple-element.14.lv_ref) | copy-start | bytes 12292
  54.6 14.3 %all-to-all-start = ((f32[32,1,128]{2,1,0:T(1,128)}), f32[32,1,128]{2,1,0:T(1,128)S(1)}, u32[]{:S(2)}, u32[]{:S(2)}) async-start(f32[32,1,128]{2,1,0:T(1,128)} %get-tuple-element.21), calls=%async_computation | async-start | bytes 32768 | tf_op jit(solution)/shard_map/all_to_all | solution.py:281
  62.0 7.1 %collective-permute-start.12 = (f32[8,128,128]{2,1,0:T(8,128)S(1)}, f32[8,128,128]{2,1,0:T(8,128)S(1)}, u32[]{:S(2)}, u32[]{:S(2)}) collective-permute-start(f32[8,128,128]{2,1,0:T(8,128)S(1)} %slice_bitcast_fusion), channel_id=1, source_target_pairs={{0,8},{8,0},{1,9},{9,1},{2,10},{10,2},{3,11},{11,3},{4,12},{12,4},... | collective-permute-start | bytes 1572872 | tf_op jit(solution)/shard_map/ppermute | solution.py:185

commit v5 on v4

--- a/solution.py
+++ b/solution.py
@@ -27,7 +27,6 @@
 NSIDE = 4
 SHIFTS = (0, 1, 3, 2)
 SPAN = 1024
-PER = {4: 4, 12: 12}
 M = NB * CTR
 VM = pl.BlockSpec(memory_space=pltpu.VMEM)
 SM = pl.BlockSpec(memory_space=pltpu.SMEM)
@@ -98,8 +97,7 @@
 def add_pairs(blocks, count, ct, hc, ut, gt, qt, xt, hx, vs, yt, hy, us):
     gt[...] = jnp.zeros_like(gt)
     qt[...] = jnp.zeros_like(qt)
-    per = PER[count]
-    steps, csteps = count // NSIDE, count // per
+    steps = count // NSIDE
 
     def turn_points(a, slot):
         for k in range(2 * NSIDE):
@@ -107,10 +105,10 @@
             vrows = blocks[i, BASE + h * R : BASE + (h + 1) * R, :]
             turn(blocks[i, h * 128 : (h + 1) * 128, :], vrows, 0, xt, hx, vs, slot, k)
 
-    def turn_centers(a, slot):
-        for k in range(per):
-            i = per * a + k
-            turn(blocks[i, PTS:BASE, :], blocks[i, BASE + 2 * R : PROWS, :], R, yt, hy, us, slot, k)
+    def turn_centers(a):
+        for k in range(NSIDE):
+            i = NSIDE * a + k
+            turn(blocks[i, PTS:BASE, :], blocks[i, BASE + 2 * R : PROWS, :], R, yt, hy, us, a, k)
 
     def points_step(a, ell):
         slot = lax.rem(a, 2)
@@ -118,16 +116,9 @@
         rows = sweep(x, xt[slot], hx[slot], vs[slot], ct, hc, ut, gt, qt, True)
         if steps > 1:
             turn_points(lax.min(a + 1, steps - 1), 1 - slot)
+        turn_centers(a)
         xf = x.astype(F32)
         return ell + fold(jnp.sum(rows, axis=1, keepdims=True) * (xf * xf))
-
-    def centers_step(a, carry):
-        slot = lax.rem(a, 2)
-        c = jnp.concatenate([blocks[per * a + k, PTS:BASE, :] for k in range(per)], 0)
-        sweep(c, yt[slot], hy[slot], us[slot], ct, hc, ut, gt, qt, False)
-        if csteps > 1:
-            turn_centers(lax.min(a + 1, csteps - 1), 1 - slot)
-        return carry
 
     turn_points(0, 0)
     ell = lax.fori_loop(0, steps, points_step, jnp.zeros((8, D), F32))
@@ -135,8 +126,11 @@
     for j in range(NB):
         cols = slice(j * CTR, (j + 1) * CTR)
         both = both + ct[:, cols].astype(F32) * gt[:, cols]
-    turn_centers(0, 0)
-    lax.fori_loop(0, csteps, centers_step, 0)
+    c = jnp.concatenate([blocks[i, PTS:BASE, :] for i in range(count)], 0)
+    yts, hys, uss = (
+        jnp.concatenate([ref[a] for a in range(steps)], axis) for ref, axis in ((yt, 1), (hy, 0), (us, 0))
+    )
+    sweep(c, yts, hys, uss, ct, hc, ut, gt, qt, False)
     return ell, both
 
 
@@ -162,12 +156,26 @@
     s_ref[8:16, :] = lv_ref[...]
 
 
-def last_kernel(at_ref, ct, hc, ut, t0, s0, a_ref, b_ref, c_ref, t_ref, s_ref, gt, qt, *work):
+def middle_kernel(ct, hc, ut, t0, s0, a_ref, b_ref, t_ref, s_ref, gt, qt, *work):
     blocks = work[-1]
-    for k, ref in enumerate((a_ref, b_ref, c_ref)):
+    for k, ref in enumerate((a_ref, b_ref)):
         for i in range(NSIDE):
             blocks[NSIDE * k + i] = ref[i]
-    ell, both = add_pairs(blocks, 3 * NSIDE, ct, hc, ut, gt, qt, *work[:-1])
+    ell, both = add_pairs(blocks, 2 * NSIDE, ct, hc, ut, gt, qt, *work[:-1])
+    for j in range(NB):
+        cols = slice(j * CTR, (j + 1) * CTR)
+        t, s = block_terms(j, ct, gt, qt)
+        t_ref[:, cols] = t0[:, cols] + t
+        both = both + s
+    s_ref[0:8, :] = s0[0:8, :] + ell - fold(both.T)
+    s_ref[8:16, :] = s0[8:16, :]
+
+
+def last_kernel(at_ref, ct, hc, ut, t0, s0, a_ref, t_ref, s_ref, gt, qt, *work):
+    blocks = work[-1]
+    for i in range(NSIDE):
+        blocks[i] = a_ref[i]
+    ell, both = add_pairs(blocks, NSIDE, ct, hc, ut, gt, qt, *work[:-1])
     inv = 1.0 / s0[8:9, :]
     zh, zl = at_ref[0], at_ref[1]
     for j in range(NB):
@@ -210,16 +218,16 @@
 
 
 def work_space(count):
-    n, nc = NSIDE * PTS, PER[count] * CTR
+    n, nc, steps = NSIDE * PTS, NSIDE * CTR, count // NSIDE
     return [
         pltpu.VMEM((D, M), F32),
         pltpu.VMEM((8, M), F32),
         pltpu.VMEM((2, D, n), BF),
         pltpu.VMEM((2, n, 128), F32),
         pltpu.VMEM((2, n, 128), BF),
-        pltpu.VMEM((2, D, nc), BF),
-        pltpu.VMEM((2, nc, 128), F32),
-        pltpu.VMEM((2, nc, 128), BF),
+        pltpu.VMEM((steps, D, nc), BF),
+        pltpu.VMEM((steps, nc, 128), F32),
+        pltpu.VMEM((steps, nc, 128), BF),
         pltpu.VMEM((count, PROWS, D), BF),
     ]
 
@@ -244,16 +252,30 @@
     )(*args)
 
 
+def middle_call(*args):
+    shape = jax.ShapeDtypeStruct
+    return pl.pallas_call(
+        middle_kernel,
+        out_shape=[shape((D, M), F32), shape((16, D), F32)],
+        in_specs=[VM] * 7,
+        out_specs=[VM] * 2,
+        scratch_shapes=work_space(2 * NSIDE),
+        compiler_params=PARAMS,
+        cost_estimate=pl.CostEstimate(flops=1, bytes_accessed=1, transcendentals=0),
+        name="pairs_middle",
+    )(*args)
+
+
 def last_call(*args):
     shape = jax.ShapeDtypeStruct
     return pl.pallas_call(
         last_kernel,
         out_shape=[shape((2, NZ, CTR, D), F32), shape((32, 1, D), F32)],
-        in_specs=[SM] + [VM] * 8,
+        in_specs=[SM] + [VM] * 6,
         out_specs=[VM] * 2,
-        scratch_shapes=work_space(3 * NSIDE),
+        scratch_shapes=work_space(NSIDE),
         compiler_params=PARAMS,
-        cost_estimate=cost(3 * NSIDE),
+        cost_estimate=cost(NSIDE),
         name="pairs_last",
     )(*args)
 
@@ -276,7 +298,9 @@
     six = jnp.concatenate([shifted(two, "zh", by) for by in SHIFTS[1:]], 0)
     held = (two, six, two_other, shifted(six, "core", 1))
     at = jnp.stack([lax.axis_index("zh"), lax.axis_index("zl")]).astype(jnp.int32)
-    terms, scale = last_call(at, *first_call(*held, *side, lv), *rest)
+    state = list(first_call(*held, *side, lv))
+    state[3:5] = middle_call(*state, *rest[1:])
+    terms, scale = last_call(at, *state, rest[0])
     swapped = shifted(terms[1], "core", 1)
     scale = jnp.sum(lax.all_to_all(scale, SCALE_AXES, 0, 0, tiled=True), (0, 1))
     mine = (terms[0] + swapped).astype(BF)

time: 85.3 us -> 83.9 us (0.984)
  waiting for transfers between devices: 11.2 us -> 8.27 us
  starting transfers between devices: 31.7 us -> 33.6 us
  blocking collectives: 14.6 us -> 13.4 us
    pallas_call x0 -> x1, Pallas kernels: none -> 10.9 us  [middle_call(): pl.pallas_call(middle_kernel, out_shape=[shape((D, M), F32), shape((16, D...]
    pallas_call x1, Pallas kernels: 17 us -> 6.76 us  [last_call(): pl.pallas_call(last_kernel, out_shape=[shape((2, NZ, CTR, D), F32), shape...]
    ppermute x6, waiting for transfers between devices: 2.29 us -> 0.02 us  [plane_shift(): return lax.ppermute(value, PLANE_AXES, perm)]
    all_to_all x1, starting transfers between devices: 7.34 us -> 8.73 us  [local(): scale = jnp.sum(lax.all_to_all(scale, SCALE_AXES, 0, 0, tiled=True), (0, 1))]
    all_to_all x1, blocking collectives: 14.6 us -> 13.4 us  [local(): parts = lax.all_to_all(chunk, CENTER_AXES, 0, 0, tiled=True)]
  transfers between devices with their start and end apart: 14 -> 14, of which waited for: 4 -> 3; matrix products, arithmetic and copies ran while one was open for 2% -> 2% of each run, Pallas kernels for 7% -> 20%
where the time goes in v5:
time: 83.9 us; the launch traced here: 83.6 us
  starting transfers between devices  33.6 us (40%)
  Pallas kernels  24.9 us (30%)
  blocking collectives  13.4 us (16%)
  waiting for transfers between devices  8.27 us (10%)
  other arithmetic  2.41 us (3%)
    ppermute x7, starting transfers between devices, shifted(): return lax.ppermute(value, axis, [(i, (i + by) % n) for i in range(n)])  16.2 us
    all_to_all x1, blocking collectives, local(): parts = lax.all_to_all(chunk, CENTER_AXES, 0, 0, tiled=True)  13.4 us
    pallas_call x1, Pallas kernels, middle_call(): pl.pallas_call(middle_kernel, out_shape=[shape((D, M), F32), shape((16, D...  10.9 us
    all_to_all x1, starting transfers between devices, local(): scale = jnp.sum(lax.all_to_all(scale, SCALE_AXES, 0, 0, tiled=True), (0, 1))  8.73 us
    ppermute x6, starting transfers between devices, plane_shift(): return lax.ppermute(value, PLANE_AXES, perm)  8.68 us
    pallas_call x1, Pallas kernels, last_call(): pl.pallas_call(last_kernel, out_shape=[shape((2, NZ, CTR, D), F32), shape...  6.76 us
    all_to_all x1, waiting for transfers between devices, local(): scale = jnp.sum(lax.all_to_all(scale, SCALE_AXES, 0, 0, tiled=True), (0, 1))  6.5 us
    pallas_call x1, Pallas kernels, first_call(): pl.pallas_call(first_kernel, out_shape=[shape((D, M), BF), shape((8, M),...  5.64 us
  transfers between devices with their start and end apart: 14, of which 3 were waited for; matrix products, arithmetic and copies ran while one was open for 2% of the time, Pallas kernels for 20%

profile of v5, /device:TPU:1, one launch (start us, length us, event | category | flops | bytes accessed | tf_op | source)
XLA Modules:
  0.0 83.6 jit_solution(16415125578891700046)
XLA Ops:
  0.6 1.6 %prep.1 = (bf16[512,128]{1,0:T(8,128)(2,1)}, bf16[224,128]{1,0:T(8,128)(2,1)}, f32[8,128]{1,0:T(8,128)}) custom-call(bf16[256,128]{1,0:T(8,128)(2,1)} %x_ref.1, bf16[32,256]{1,0:T(8,128)(2,1)} %bitcast.40, bf16[128,128]{1,0:T(8,128)(2,1)} %c_ref.1, bf16[32,128]{1,0:T(8,128)(2,1)} %bitcast.41, bf16[32,128]{1,0:T(8,128)(2,1)} %bitcast.42, ...), custom_call_target="tpu_custom_call" | custom-call | tf_op jit(solution)/shard_map/prep/pallas_call | solution.py:286
  2.2 0.0 copy-start
  2.2 2.5 %collective-permute-start = (bf16[224,128]{1,0:T(8,128)(2,1)}, bf16[224,128]{1,0:T(8,128)(2,1)S(1)}, u32[]{:S(2)}, u32[]{:S(2)}) collective-permute-start(bf16[224,128]{1,0:T(8,128)(2,1)} %get-tuple-element.14), channel_id=1, source_target_pairs={{0,4},{4,0},{1,5},{5,1},{2,6},{6,2},{3,7},{7,3},{8,12},{12,8},{9,1... | collective-permute-start | bytes 172040 | tf_op jit(solution)/shard_map/ppermute | solution.py:193
  4.7 1.3 %collective-permute-start.6 = (bf16[512,128]{1,0:T(8,128)(2,1)}, bf16[512,128]{1,0:T(8,128)(2,1)S(1)}, u32[]{:S(2)}, u32[]{:S(2)}) collective-permute-start(bf16[512,128]{1,0:T(8,128)(2,1)} %get-tuple-element.15.a_ref), channel_id=1, source_target_pairs={{0,1},{1,2},{2,3},{3,0},{8,24},{9,25},{10,26},{11,27},{16,17},{17,... | collective-permute-start | bytes 393224 | tf_op jit(solution)/shard_map/ppermute | solution.py:204
  6.0 1.4 %collective-permute-start.7 = (bf16[512,128]{1,0:T(8,128)(2,1)}, bf16[512,128]{1,0:T(8,128)(2,1)S(1)}, u32[]{:S(2)}, u32[]{:S(2)}) collective-permute-start(bf16[512,128]{1,0:T(8,128)(2,1)} %get-tuple-element.15.a_ref), channel_id=1, source_target_pairs={{0,3},{1,0},{2,1},{3,2},{8,56},{9,57},{10,58},{11,59},{16,19},{17,... | collective-permute-start | bytes 393224 | tf_op jit(solution)/shard_map/ppermute | solution.py:204
  7.4 1.6 %collective-permute-start.8 = (bf16[512,128]{1,0:T(8,128)(2,1)}, bf16[512,128]{1,0:T(8,128)(2,1)S(1)}, u32[]{:S(2)}, u32[]{:S(2)}) collective-permute-start(bf16[512,128]{1,0:T(8,128)(2,1)} %get-tuple-element.15.a_ref), channel_id=1, source_target_pairs={{0,2},{1,3},{2,0},{3,1},{8,40},{9,41},{10,42},{11,43},{16,18},{17,... | collective-permute-start | bytes 393224 | tf_op jit(solution)/shard_map/ppermute | solution.py:204
  9.1 0.0 collective-permute-done
  9.1 0.8 pad_maximum_fusion.2.h0
  9.9 3.1 %collective-permute-start.1 = (bf16[2,224,128]{2,1,0:T(8,128)(2,1)S(1)}, bf16[2,224,128]{2,1,0:T(8,128)(2,1)S(1)}, u32[]{:S(2)}, u32[]{:S(2)}) collective-permute-start(bf16[2,224,128]{2,1,0:T(8,128)(2,1)S(1)} %pad_maximum_fusion.2.h0), channel_id=1, source_target_pairs={{0,64},{64,128},{128,192},{192,0},{1,65},{65,129},{129,193},{193,1... | collective-permute-start | bytes 344072 | tf_op jit(solution)/shard_map/ppermute | solution.py:193
  13.0 2.2 %collective-permute-start.2 = (bf16[2,224,128]{2,1,0:T(8,128)(2,1)S(1)}, bf16[2,224,128]{2,1,0:T(8,128)(2,1)S(1)}, u32[]{:S(2)}, u32[]{:S(2)}) collective-permute-start(bf16[2,224,128]{2,1,0:T(8,128)(2,1)S(1)} %pad_maximum_fusion.2.h0), channel_id=1, source_target_pairs={{0,192},{64,0},{128,64},{192,128},{1,193},{65,1},{129,65},{193,129... | collective-permute-start | bytes 344072 | tf_op jit(solution)/shard_map/ppermute | solution.py:193
  15.2 0.0 collective-permute-done.6.b_ref
  15.2 4.4 %collective-permute-start.3 = (bf16[2,224,128]{2,1,0:T(8,128)(2,1)S(1)}, bf16[2,224,128]{2,1,0:T(8,128)(2,1)S(1)}, u32[]{:S(2)}, u32[]{:S(2)}) collective-permute-start(bf16[2,224,128]{2,1,0:T(8,128)(2,1)S(1)} %pad_maximum_fusion.2.h0), channel_id=1, source_target_pairs={{0,128},{64,192},{128,0},{192,64},{1,129},{65,193},{129,1},{193,65... | collective-permute-start | bytes 344072 | tf_op jit(solution)/shard_map/ppermute | solution.py:193
  19.6 0.0 collective-permute-done.7.c_ref
  19.6 0.0 collective-permute-done.8.d_ref
  19.6 0.0 copy-done
  19.6 0.1 pad_maximum_fusion
  19.7 2.8 %collective-permute-start.10 = (bf16[4,512,128]{2,1,0:T(8,128)(2,1)S(1)}, bf16[4,512,128]{2,1,0:T(8,128)(2,1)S(1)}, u32[]{:S(2)}, u32[]{:S(2)}) collective-permute-start(bf16[4,512,128]{2,1,0:T(8,128)(2,1)S(1)} %pad_maximum_fusion), channel_id=1, source_target_pairs={{0,32},{1,33},{2,34},{3,35},{8,10},{9,11},{10,8},{11,9},{16,48},{1... | collective-permute-start | bytes 1572872 | tf_op jit(solution)/shard_map/ppermute | solution.py:204
  22.5 0.9 %collective-permute-start.9 = (bf16[4,512,128]{2,1,0:T(8,128)(2,1)S(1)}, bf16[4,512,128]{2,1,0:T(8,128)(2,1)S(1)}, u32[]{:S(2)}, u32[]{:S(2)}) collective-permute-start(bf16[4,512,128]{2,1,0:T(8,128)(2,1)S(1)} %pad_maximum_fusion), channel_id=1, source_target_pairs={{0,48},{1,49},{2,50},{3,51},{8,11},{9,8},{10,9},{11,10},{16,0},{17... | collective-permute-start | bytes 1572872 | tf_op jit(solution)/shard_map/ppermute | solution.py:204
  23.4 0.0 collective-permute-done.1
  23.4 0.6 collective-permute-start.11
  24.0 0.0 collective-permute-done.2
  24.0 0.7 collective-permute-done.3
  24.8 3.5 %collective-permute-start.5 = (bf16[6,224,128]{2,1,0:T(8,128)(2,1)S(1)}, bf16[6,224,128]{2,1,0:T(8,128)(2,1)S(1)}, u32[]{:S(2)}, u32[]{:S(2)}) collective-permute-start(bf16[6,224,128]{2,1,0:T(8,128)(2,1)S(1)} %constant_dynamic-update-slice_fusion.h1), channel_id=1, source_target_pairs={{0,8},{8,0},{1,9},{9,1},{2,10},{10,2},{3,11},{11,3},{4,12},{12,4},... | collective-permute-start | bytes 1032200 | tf_op jit(solution)/shard_map/ppermute | solution.py:193
  28.3 0.3 collective-permute-start.4
  28.6 0.1 pad.5.clone
  28.6 0.0 copy-start.1
  28.6 0.1 pad_add_fusion.at_ref
  28.7 1.0 %collective-permute-done.4.h2 = bf16[2,224,128]{2,1,0:T(8,128)(2,1)S(1)} collective-permute-done((bf16[2,224,128]{2,1,0:T(8,128)(2,1)S(1)}, bf16[2,224,128]{2,1,0:T(8,128)(2,1)S(1)}, u32[]{:S(2)}, u32[]{:S(2)}) %collective-permute-start.4) | collective-permute-done | bytes 114720 | tf_op jit(solution)/shard_map/ppermute | solution.py:193
  29.7 0.0 collective-permute-done.5.h3
  29.7 0.0 copy-done.1
  29.7 5.6 %pairs_first.1 = (bf16[128,2048]{1,0:T(8,128)(2,1)S(1)}, f32[8,2048]{1,0:T(8,128)S(1)}, bf16[128,2048]{1,0:T(8,128)(2,1)S(1)}, f32[128,2048]{1,0:T(8,128)S(1)}, f32[16,128]{1,0:T(8,128)S(1)}) custom-call(bf16[2,224,128]{2,1,0:T(8,128)(2,1)S(1)} %pad_maximum_fusion.2.h0, bf16[6,224,128]{2,1,0:T(8,128)(2,1)S(1)} %constant_dynamic-update-slice_fusion.h1, ...), custom_call_target="tpu_custom_call" | custom-call | flops 1 | bytes 1 | tf_op jit(solution)/shard_map/pairs_first/pallas_call | solution.py:237
  35.4 0.0 collective-permute-done.10.b_ref
  35.4 0.0 collective-permute-done.9.a_ref
  35.4 10.9 %pairs_middle.1 = (f32[128,2048]{1,0:T(8,128)S(1)}, f32[16,128]{1,0:T(8,128)S(1)}) custom-call(bf16[128,2048]{1,0:T(8,128)(2,1)S(1)} %get-tuple-element.17.ct, f32[8,2048]{1,0:T(8,128)S(1)} %get-tuple-element.18.hc, bf16[128,2048]{1,0:T(8,128)(2,1)S(1)} %get-tuple-element.19.ut, f32[128,2048]{1,0:T(8,128)S(1)} %get-tuple-element.20.t0, ...), custom_call_target="tpu_custom_call" | custom-call | flops 1 | bytes 1 | tf_op jit(solution)/shard_map/pairs_middle/pallas_call | solution.py:257
  46.3 0.0 collective-permute-done.11.a_ref
  46.3 6.8 %pairs_last.1 = (f32[2,8,128,128]{3,2,1,0:T(8,128)S(1)}, f32[32,1,128]{2,1,0:T(1,128)}) custom-call(s32[2]{0:T(128)S(1)} %pad_add_fusion.at_ref, bf16[128,2048]{1,0:T(8,128)(2,1)S(1)} %get-tuple-element.17.ct, f32[8,2048]{1,0:T(8,128)S(1)} %get-tuple-element.18.hc, bf16[128,2048]{1,0:T(8,128)(2,1)S(1)} %get-tuple-element.19.ut, ...), custom_call_target="tpu_custom_call" | custom-call | flops 1811939328 | bytes 4194304 | tf_op jit(solution)/shard_map/pairs_last/pallas_call | solution.py:271
  53.1 8.7 %all-to-all-start = ((f32[32,1,128]{2,1,0:T(1,128)}), f32[32,1,128]{2,1,0:T(1,128)S(1)}, u32[]{:S(2)}, u32[]{:S(2)}) async-start(f32[32,1,128]{2,1,0:T(1,128)} %get-tuple-element.25), calls=%async_computation | async-start | bytes 32768 | tf_op jit(solution)/shard_map/all_to_all | solution.py:305
  61.9 0.3 collective-permute-start.12
  62.2 6.5 %all-to-all-done = f32[32,1,128]{2,1,0:T(1,128)S(1)} async-done(((f32[32,1,128]{2,1,0:T(1,128)}), f32[32,1,128]{2,1,0:T(1,128)S(1)}, u32[]{:S(2)}, u32[]{:S(2)}) %all-to-all-start) | async-done | bytes 16416 | tf_op jit(solution)/shard_map/all_to_all | solution.py:305
  68.7 0.1 reduce_sum.29
  68.7 0.1 maximum_maximum_fusion
  68.8 0.0 collective-permute-done.12
  68.8 0.1 fusion
  68.9 13.4 %all_to_all.10 = bf16[8,144,128]{2,1,0:T(8,128)(2,1)S(1)} all-to-all(bf16[8,144,128]{2,1,0:T(8,128)(2,1)S(1)} %pad_maximum_fusion.1), channel_id=1, replica_groups=mesh['zh'=4,'y'=4,'core'=2,'zl'=2,'x'=4] {'zh','zl'}, dimensions={0} | all-to-all | bytes 589824 | tf_op jit(solution)/shard_map/all_to_all | solution.py:308
  82.4 0.5 bitcast_divide_fusion
  82.9 0.7 convert_reduce_fusion
  (10 shorter events, 0.2 us)
Async XLA Ops:
  2.2 17.4 %copy-start = (bf16[512,128]{1,0:T(8,128)(2,1)S(1)}, bf16[512,128]{1,0:T(8,128)(2,1)}, u32[]{:S(2)}) copy-start(bf16[512,128]{1,0:T(8,128)(2,1)} %get-tuple-element.15.a_ref) | copy-start | bytes 393220
  2.2 6.9 %collective-permute-start = (bf16[224,128]{1,0:T(8,128)(2,1)}, bf16[224,128]{1,0:T(8,128)(2,1)S(1)}, u32[]{:S(2)}, u32[]{:S(2)}) collective-permute-start(bf16[224,128]{1,0:T(8,128)(2,1)} %get-tuple-element.14), channel_id=1, source_target_pairs={{0,4},{4,0},{1,5},{5,1},{2,6},{6,2},{3,7},{7,3},{8,12},{12,8},{9,1... | collective-permute-start | bytes 172040 | tf_op jit(solution)/shard_map/ppermute | solution.py:193
  4.7 10.5 %collective-permute-start.6 = (bf16[512,128]{1,0:T(8,128)(2,1)}, bf16[512,128]{1,0:T(8,128)(2,1)S(1)}, u32[]{:S(2)}, u32[]{:S(2)}) collective-permute-start(bf16[512,128]{1,0:T(8,128)(2,1)} %get-tuple-element.15.a_ref), channel_id=1, source_target_pairs={{0,1},{1,2},{2,3},{3,0},{8,24},{9,25},{10,26},{11,27},{16,17},{17,... | collective-permute-start | bytes 393224 | tf_op jit(solution)/shard_map/ppermute | solution.py:204
  6.0 13.6 %collective-permute-start.7 = (bf16[512,128]{1,0:T(8,128)(2,1)}, bf16[512,128]{1,0:T(8,128)(2,1)S(1)}, u32[]{:S(2)}, u32[]{:S(2)}) collective-permute-start(bf16[512,128]{1,0:T(8,128)(2,1)} %get-tuple-element.15.a_ref), channel_id=1, source_target_pairs={{0,3},{1,0},{2,1},{3,2},{8,56},{9,57},{10,58},{11,59},{16,19},{17,... | collective-permute-start | bytes 393224 | tf_op jit(solution)/shard_map/ppermute | solution.py:204
  7.4 12.2 %collective-permute-start.8 = (bf16[512,128]{1,0:T(8,128)(2,1)}, bf16[512,128]{1,0:T(8,128)(2,1)S(1)}, u32[]{:S(2)}, u32[]{:S(2)}) collective-permute-start(bf16[512,128]{1,0:T(8,128)(2,1)} %get-tuple-element.15.a_ref), channel_id=1, source_target_pairs={{0,2},{1,3},{2,0},{3,1},{8,40},{9,41},{10,42},{11,43},{16,18},{17,... | collective-permute-start | bytes 393224 | tf_op jit(solution)/shard_map/ppermute | solution.py:204
  9.9 13.5 %collective-permute-start.1 = (bf16[2,224,128]{2,1,0:T(8,128)(2,1)S(1)}, bf16[2,224,128]{2,1,0:T(8,128)(2,1)S(1)}, u32[]{:S(2)}, u32[]{:S(2)}) collective-permute-start(bf16[2,224,128]{2,1,0:T(8,128)(2,1)S(1)} %pad_maximum_fusion.2.h0), channel_id=1, source_target_pairs={{0,64},{64,128},{128,192},{192,0},{1,65},{65,129},{129,193},{193,1... | collective-permute-start | bytes 344072 | tf_op jit(solution)/shard_map/ppermute | solution.py:193
  13.0 11.0 %collective-permute-start.2 = (bf16[2,224,128]{2,1,0:T(8,128)(2,1)S(1)}, bf16[2,224,128]{2,1,0:T(8,128)(2,1)S(1)}, u32[]{:S(2)}, u32[]{:S(2)}) collective-permute-start(bf16[2,224,128]{2,1,0:T(8,128)(2,1)S(1)} %pad_maximum_fusion.2.h0), channel_id=1, source_target_pairs={{0,192},{64,0},{128,64},{192,128},{1,193},{65,1},{129,65},{193,129... | collective-permute-start | bytes 344072 | tf_op jit(solution)/shard_map/ppermute | solution.py:193
  15.2 9.6 %collective-permute-start.3 = (bf16[2,224,128]{2,1,0:T(8,128)(2,1)S(1)}, bf16[2,224,128]{2,1,0:T(8,128)(2,1)S(1)}, u32[]{:S(2)}, u32[]{:S(2)}) collective-permute-start(bf16[2,224,128]{2,1,0:T(8,128)(2,1)S(1)} %pad_maximum_fusion.2.h0), channel_id=1, source_target_pairs={{0,128},{64,192},{128,0},{192,64},{1,129},{65,193},{129,1},{193,65... | collective-permute-start | bytes 344072 | tf_op jit(solution)/shard_map/ppermute | solution.py:193
  19.7 15.7 %collective-permute-start.10 = (bf16[4,512,128]{2,1,0:T(8,128)(2,1)S(1)}, bf16[4,512,128]{2,1,0:T(8,128)(2,1)S(1)}, u32[]{:S(2)}, u32[]{:S(2)}) collective-permute-start(bf16[4,512,128]{2,1,0:T(8,128)(2,1)S(1)} %pad_maximum_fusion), channel_id=1, source_target_pairs={{0,32},{1,33},{2,34},{3,35},{8,10},{9,11},{10,8},{11,9},{16,48},{1... | collective-permute-start | bytes 1572872 | tf_op jit(solution)/shard_map/ppermute | solution.py:204
  22.5 12.9 %collective-permute-start.9 = (bf16[4,512,128]{2,1,0:T(8,128)(2,1)S(1)}, bf16[4,512,128]{2,1,0:T(8,128)(2,1)S(1)}, u32[]{:S(2)}, u32[]{:S(2)}) collective-permute-start(bf16[4,512,128]{2,1,0:T(8,128)(2,1)S(1)} %pad_maximum_fusion), channel_id=1, source_target_pairs={{0,48},{1,49},{2,50},{3,51},{8,11},{9,8},{10,9},{11,10},{16,0},{17... | collective-permute-start | bytes 1572872 | tf_op jit(solution)/shard_map/ppermute | solution.py:204
  23.4 23.0 %collective-permute-start.11 = (bf16[4,512,128]{2,1,0:T(8,128)(2,1)S(1)}, bf16[4,512,128]{2,1,0:T(8,128)(2,1)S(1)}, u32[]{:S(2)}, u32[]{:S(2)}) collective-permute-start(bf16[4,512,128]{2,1,0:T(8,128)(2,1)S(1)} %pad_maximum_fusion), channel_id=1, source_target_pairs={{0,16},{1,17},{2,18},{3,19},{8,9},{9,10},{10,11},{11,8},{16,32},{1... | collective-permute-start | bytes 1572872 | tf_op jit(solution)/shard_map/ppermute | solution.py:204
  24.8 4.9 %collective-permute-start.5 = (bf16[6,224,128]{2,1,0:T(8,128)(2,1)S(1)}, bf16[6,224,128]{2,1,0:T(8,128)(2,1)S(1)}, u32[]{:S(2)}, u32[]{:S(2)}) collective-permute-start(bf16[6,224,128]{2,1,0:T(8,128)(2,1)S(1)} %constant_dynamic-update-slice_fusion.h1), channel_id=1, source_target_pairs={{0,8},{8,0},{1,9},{9,1},{2,10},{10,2},{3,11},{11,3},{4,12},{12,4},... | collective-permute-start | bytes 1032200 | tf_op jit(solution)/shard_map/ppermute | solution.py:193
  28.3 1.4 %collective-permute-start.4 = (bf16[2,224,128]{2,1,0:T(8,128)(2,1)S(1)}, bf16[2,224,128]{2,1,0:T(8,128)(2,1)S(1)}, u32[]{:S(2)}, u32[]{:S(2)}) collective-permute-start(bf16[2,224,128]{2,1,0:T(8,128)(2,1)S(1)} %pad_maximum_fusion.2.h0), channel_id=1, source_target_pairs={{0,8},{8,0},{1,9},{9,1},{2,10},{10,2},{3,11},{11,3},{4,12},{12,4},... | collective-permute-start | bytes 344072 | tf_op jit(solution)/shard_map/ppermute | solution.py:193
  28.6 1.1 %copy-start.1 = (f32[8,128]{1,0:T(8,128)S(1)}, f32[8,128]{1,0:T(8,128)}, u32[]{:S(2)}) copy-start(f32[8,128]{1,0:T(8,128)} %get-tuple-element.16.lv_ref) | copy-start | bytes 12292
  53.1 15.6 %all-to-all-start = ((f32[32,1,128]{2,1,0:T(1,128)}), f32[32,1,128]{2,1,0:T(1,128)S(1)}, u32[]{:S(2)}, u32[]{:S(2)}) async-start(f32[32,1,128]{2,1,0:T(1,128)} %get-tuple-element.25), calls=%async_computation | async-start | bytes 32768 | tf_op jit(solution)/shard_map/all_to_all | solution.py:305
  61.9 7.0 %collective-permute-start.12 = (f32[8,128,128]{2,1,0:T(8,128)S(1)}, f32[8,128,128]{2,1,0:T(8,128)S(1)}, u32[]{:S(2)}, u32[]{:S(2)}) collective-permute-start(f32[8,128,128]{2,1,0:T(8,128)S(1)} %slice_bitcast_fusion), channel_id=1, source_target_pairs={{0,8},{8,0},{1,9},{9,1},{2,10},{10,2},{3,11},{11,3},{4,12},{12,4},... | collective-permute-start | bytes 1572872 | tf_op jit(solution)/shard_map/ppermute | solution.py:193

commit v6 on v5

--- a/solution.py
+++ b/solution.py
@@ -11,9 +11,8 @@
 F32 = jnp.float32
 AXES = ("zh", "y", "core", "zl", "x")
 SIZES = (4, 4, 2, 2, 4)
-CENTER_AXES = ("zh", "zl")
 PLANE_AXES = ("y", "core", "x")
-SCALE_AXES = ("y", "x", "core")
+SCALE_AXES = ("y", "x", "core", "zl")
 D = 128
 R = 32
 PTS = 256
@@ -177,13 +176,12 @@
         blocks[i] = a_ref[i]
     ell, both = add_pairs(blocks, NSIDE, ct, hc, ut, gt, qt, *work[:-1])
     inv = 1.0 / s0[8:9, :]
-    zh, zl = at_ref[0], at_ref[1]
+    zh = at_ref[0]
     for j in range(NB):
         t, s = block_terms(j, ct, gt, qt)
         both = both + s
         h, i = divmod(j, NZ)
-        place = lax.rem(zh + 4 - SHIFTS[i // 2], 4) * 2 + (zl if i % 2 == 0 else 1 - zl)
-        t_ref[h, place] = (t0[:, j * CTR : (j + 1) * CTR] + t).T * inv
+        t_ref[h, i % 2, lax.rem(zh + 4 - SHIFTS[i // 2], 4)] = (t0[:, j * CTR : (j + 1) * CTR] + t).T * inv
     scale = jnp.sum(s0[0:8, :] + ell - fold(both.T), axis=0, keepdims=True)
     s_ref[...] = jnp.broadcast_to(scale[None], s_ref.shape)
 
@@ -270,7 +268,7 @@
     shape = jax.ShapeDtypeStruct
     return pl.pallas_call(
         last_kernel,
-        out_shape=[shape((2, NZ, CTR, D), F32), shape((32, 1, D), F32)],
+        out_shape=[shape((2, 2, NZ // 2, CTR, D), F32), shape((64, 1, D), F32)],
         in_specs=[SM] + [VM] * 6,
         out_specs=[VM] * 2,
         scratch_shapes=work_space(NSIDE),
@@ -297,15 +295,17 @@
     two_other = shifted(two, "core", 1)
     six = jnp.concatenate([shifted(two, "zh", by) for by in SHIFTS[1:]], 0)
     held = (two, six, two_other, shifted(six, "core", 1))
-    at = jnp.stack([lax.axis_index("zh"), lax.axis_index("zl")]).astype(jnp.int32)
+    at = lax.axis_index("zh").astype(jnp.int32).reshape(1)
     state = list(first_call(*held, *side, lv))
     state[3:5] = middle_call(*state, *rest[1:])
     terms, scale = last_call(at, *state, rest[0])
-    swapped = shifted(terms[1], "core", 1)
+    half = terms[0, 0] + shifted(terms[1, 0], "core", 1)
+    half = half + shifted(terms[0, 1].astype(BF), "zl", 1).astype(F32)
+    cross = [(2 * a + b, 2 * (1 - a) + 1 - b) for a in range(2) for b in range(2)]
+    half = half + lax.ppermute(terms[1, 1].astype(BF), ("core", "zl"), cross).astype(F32)
     scale = jnp.sum(lax.all_to_all(scale, SCALE_AXES, 0, 0, tiled=True), (0, 1))
-    mine = (terms[0] + swapped).astype(BF)
-    chunk = jnp.concatenate([mine, jnp.broadcast_to(pieces(scale)[None], (NZ, TAIL, D))], 1)
-    parts = lax.all_to_all(chunk, CENTER_AXES, 0, 0, tiled=True)
+    tail = jnp.broadcast_to(pieces(scale)[None], (NZ // 2, TAIL, D))
+    parts = lax.all_to_all(jnp.concatenate([half.astype(BF), tail], 1), "zh", 0, 0, tiled=True)
     total = jnp.sum(parts[:, 0:CTR].astype(F32), 0)
     return total, jnp.sum(parts[:, CTR:].astype(F32), (0, 1)) / lv[0]
 

time: 83.9 us -> 83.8 us (level); the launches traced: 83.6 us -> 82.1 us
  blocking collectives: 13.4 us -> 10.2 us
  starting transfers between devices: 33.6 us -> 36.3 us
    all_to_all x1, blocking collectives: 13.4 us -> 10.2 us  [local(): lax.all_to_all(jnp.concatenate([half.astype(BF), tail], 1), 'zh', 0, 0, t...]
    ppermute x7 -> x8, starting transfers between devices: 16.2 us -> 17.4 us  [shifted(): return lax.ppermute(value, axis, [(i, (i + by) % n) for i in range(n)])]
    all_to_all x1, waiting for transfers between devices: 6.5 us -> 5.47 us  [local(): scale = jnp.sum(lax.all_to_all(scale, SCALE_AXES, 0, 0, tiled=True), (0, 1))]
    all_to_all x1, starting transfers between devices: 8.73 us -> 9.58 us  [local(): scale = jnp.sum(lax.all_to_all(scale, SCALE_AXES, 0, 0, tiled=True), (0, 1))]
    ppermute x7 -> x8, waiting for transfers between devices: 1.76 us -> 1.84 us  [shifted(): return lax.ppermute(value, axis, [(i, (i + by) % n) for i in range(n)])]
  transfers between devices with their start and end apart: 14 -> 16, of which waited for: 3 -> 4; matrix products, arithmetic and copies ran while one was open for 2% -> 1% of each run, Pallas kernels for 20% -> 20%
where the time goes in v6:
time: 83.8 us; the launch traced here: 82.1 us
  starting transfers between devices  36.3 us (43%)
  Pallas kernels  24.4 us (29%)
  blocking collectives  10.2 us (12%)
  waiting for transfers between devices  7.79 us (9%)
  other arithmetic  2.42 us (3%)
    ppermute x8, starting transfers between devices, shifted(): return lax.ppermute(value, axis, [(i, (i + by) % n) for i in range(n)])  17.4 us
    pallas_call x1, Pallas kernels, middle_call(): pl.pallas_call(middle_kernel, out_shape=[shape((D, M), F32), shape((16, D...  10.9 us
    all_to_all x1, blocking collectives, local(): lax.all_to_all(jnp.concatenate([half.astype(BF), tail], 1), 'zh', 0, 0, t...  10.2 us
    all_to_all x1, starting transfers between devices, local(): scale = jnp.sum(lax.all_to_all(scale, SCALE_AXES, 0, 0, tiled=True), (0, 1))  9.58 us
    ppermute x6, starting transfers between devices, plane_shift(): return lax.ppermute(value, PLANE_AXES, perm)  8.68 us
    pallas_call x1, Pallas kernels, last_call(): pl.pallas_call(last_kernel, out_shape=[shape((2, 2, NZ // 2, CTR, D), F32...  6.27 us
    pallas_call x1, Pallas kernels, first_call(): pl.pallas_call(first_kernel, out_shape=[shape((D, M), BF), shape((8, M),...  5.64 us
    all_to_all x1, waiting for transfers between devices, local(): scale = jnp.sum(lax.all_to_all(scale, SCALE_AXES, 0, 0, tiled=True), (0, 1))  5.47 us
  transfers between devices with their start and end apart: 16, of which 4 were waited for; matrix products, arithmetic and copies ran while one was open for 1% of the time, Pallas kernels for 20%

profile of v6, /device:TPU:1, one launch (start us, length us, event | category | flops | bytes accessed | tf_op | source)
XLA Modules:
  0.0 82.1 jit_solution(8433906880449384594)
XLA Ops:
  0.6 1.6 %prep.1 = (bf16[512,128]{1,0:T(8,128)(2,1)}, bf16[224,128]{1,0:T(8,128)(2,1)}, f32[8,128]{1,0:T(8,128)}) custom-call(bf16[256,128]{1,0:T(8,128)(2,1)} %x_ref.1, bf16[32,256]{1,0:T(8,128)(2,1)} %bitcast.47, bf16[128,128]{1,0:T(8,128)(2,1)} %c_ref.1, bf16[32,128]{1,0:T(8,128)(2,1)} %bitcast.48, bf16[32,128]{1,0:T(8,128)(2,1)} %bitcast.49, ...), custom_call_target="tpu_custom_call" | custom-call | tf_op jit(solution)/shard_map/prep/pallas_call | solution.py:284
  2.2 0.0 copy-start
  2.2 2.5 %collective-permute-start = (bf16[224,128]{1,0:T(8,128)(2,1)}, bf16[224,128]{1,0:T(8,128)(2,1)S(1)}, u32[]{:S(2)}, u32[]{:S(2)}) collective-permute-start(bf16[224,128]{1,0:T(8,128)(2,1)} %get-tuple-element.14), channel_id=1, source_target_pairs={{0,4},{4,0},{1,5},{5,1},{2,6},{6,2},{3,7},{7,3},{8,12},{12,8},{9,1... | collective-permute-start | bytes 172040 | tf_op jit(solution)/shard_map/ppermute | solution.py:191
  4.7 1.3 %collective-permute-start.6 = (bf16[512,128]{1,0:T(8,128)(2,1)}, bf16[512,128]{1,0:T(8,128)(2,1)S(1)}, u32[]{:S(2)}, u32[]{:S(2)}) collective-permute-start(bf16[512,128]{1,0:T(8,128)(2,1)} %get-tuple-element.15.a_ref), channel_id=1, source_target_pairs={{0,1},{1,2},{2,3},{3,0},{8,24},{9,25},{10,26},{11,27},{16,17},{17,... | collective-permute-start | bytes 393224 | tf_op jit(solution)/shard_map/ppermute | solution.py:202
  6.0 1.4 %collective-permute-start.7 = (bf16[512,128]{1,0:T(8,128)(2,1)}, bf16[512,128]{1,0:T(8,128)(2,1)S(1)}, u32[]{:S(2)}, u32[]{:S(2)}) collective-permute-start(bf16[512,128]{1,0:T(8,128)(2,1)} %get-tuple-element.15.a_ref), channel_id=1, source_target_pairs={{0,3},{1,0},{2,1},{3,2},{8,56},{9,57},{10,58},{11,59},{16,19},{17,... | collective-permute-start | bytes 393224 | tf_op jit(solution)/shard_map/ppermute | solution.py:202
  7.4 1.6 %collective-permute-start.8 = (bf16[512,128]{1,0:T(8,128)(2,1)}, bf16[512,128]{1,0:T(8,128)(2,1)S(1)}, u32[]{:S(2)}, u32[]{:S(2)}) collective-permute-start(bf16[512,128]{1,0:T(8,128)(2,1)} %get-tuple-element.15.a_ref), channel_id=1, source_target_pairs={{0,2},{1,3},{2,0},{3,1},{8,40},{9,41},{10,42},{11,43},{16,18},{17,... | collective-permute-start | bytes 393224 | tf_op jit(solution)/shard_map/ppermute | solution.py:202
  9.1 0.0 collective-permute-done
  9.1 0.8 %pad_maximum_fusion.2.h0 = bf16[2,224,128]{2,1,0:T(8,128)(2,1)S(1)} fusion(bf16[1,224,128]{2,1,0:T(8,128)(2,1)S(1)} %bitcast.46, bf16[1,224,128]{2,1,0:T(8,128)(2,1)} %bitcast.45), kind=kLoop, calls=%fused_computation.10 | loop fusion | flops 57344 | bytes 229376 | tf_op jit(solution)/shard_map/stack | solution.py:292
  9.9 3.1 %collective-permute-start.1 = (bf16[2,224,128]{2,1,0:T(8,128)(2,1)S(1)}, bf16[2,224,128]{2,1,0:T(8,128)(2,1)S(1)}, u32[]{:S(2)}, u32[]{:S(2)}) collective-permute-start(bf16[2,224,128]{2,1,0:T(8,128)(2,1)S(1)} %pad_maximum_fusion.2.h0), channel_id=1, source_target_pairs={{0,64},{64,128},{128,192},{192,0},{1,65},{65,129},{129,193},{193,1... | collective-permute-start | bytes 344072 | tf_op jit(solution)/shard_map/ppermute | solution.py:191
  13.0 2.2 %collective-permute-start.2 = (bf16[2,224,128]{2,1,0:T(8,128)(2,1)S(1)}, bf16[2,224,128]{2,1,0:T(8,128)(2,1)S(1)}, u32[]{:S(2)}, u32[]{:S(2)}) collective-permute-start(bf16[2,224,128]{2,1,0:T(8,128)(2,1)S(1)} %pad_maximum_fusion.2.h0), channel_id=1, source_target_pairs={{0,192},{64,0},{128,64},{192,128},{1,193},{65,1},{129,65},{193,129... | collective-permute-start | bytes 344072 | tf_op jit(solution)/shard_map/ppermute | solution.py:191
  15.2 0.0 collective-permute-done.6.b_ref
  15.2 4.4 %collective-permute-start.3 = (bf16[2,224,128]{2,1,0:T(8,128)(2,1)S(1)}, bf16[2,224,128]{2,1,0:T(8,128)(2,1)S(1)}, u32[]{:S(2)}, u32[]{:S(2)}) collective-permute-start(bf16[2,224,128]{2,1,0:T(8,128)(2,1)S(1)} %pad_maximum_fusion.2.h0), channel_id=1, source_target_pairs={{0,128},{64,192},{128,0},{192,64},{1,129},{65,193},{129,1},{193,65... | collective-permute-start | bytes 344072 | tf_op jit(solution)/shard_map/ppermute | solution.py:191
  19.6 0.0 collective-permute-done.7.c_ref
  19.6 0.0 collective-permute-done.8.d_ref
  19.6 0.0 copy-done
  19.6 0.1 pad_maximum_fusion
  19.7 2.8 %collective-permute-start.10 = (bf16[4,512,128]{2,1,0:T(8,128)(2,1)S(1)}, bf16[4,512,128]{2,1,0:T(8,128)(2,1)S(1)}, u32[]{:S(2)}, u32[]{:S(2)}) collective-permute-start(bf16[4,512,128]{2,1,0:T(8,128)(2,1)S(1)} %pad_maximum_fusion), channel_id=1, source_target_pairs={{0,32},{1,33},{2,34},{3,35},{8,10},{9,11},{10,8},{11,9},{16,48},{1... | collective-permute-start | bytes 1572872 | tf_op jit(solution)/shard_map/ppermute | solution.py:202
  22.5 0.9 %collective-permute-start.9 = (bf16[4,512,128]{2,1,0:T(8,128)(2,1)S(1)}, bf16[4,512,128]{2,1,0:T(8,128)(2,1)S(1)}, u32[]{:S(2)}, u32[]{:S(2)}) collective-permute-start(bf16[4,512,128]{2,1,0:T(8,128)(2,1)S(1)} %pad_maximum_fusion), channel_id=1, source_target_pairs={{0,48},{1,49},{2,50},{3,51},{8,11},{9,8},{10,9},{11,10},{16,0},{17... | collective-permute-start | bytes 1572872 | tf_op jit(solution)/shard_map/ppermute | solution.py:202
  23.4 0.0 collective-permute-done.1
  23.4 0.6 collective-permute-start.11
  24.0 0.0 collective-permute-done.2
  24.0 0.7 collective-permute-done.3
  24.8 3.5 %collective-permute-start.5 = (bf16[6,224,128]{2,1,0:T(8,128)(2,1)S(1)}, bf16[6,224,128]{2,1,0:T(8,128)(2,1)S(1)}, u32[]{:S(2)}, u32[]{:S(2)}) collective-permute-start(bf16[6,224,128]{2,1,0:T(8,128)(2,1)S(1)} %constant_dynamic-update-slice_fusion.h1), channel_id=1, source_target_pairs={{0,8},{8,0},{1,9},{9,1},{2,10},{10,2},{3,11},{11,3},{4,12},{12,4},... | collective-permute-start | bytes 1032200 | tf_op jit(solution)/shard_map/ppermute | solution.py:191
  28.3 0.3 collective-permute-start.4
  28.6 0.0 copy-start.1
  28.6 0.1 pad.5.clone
  28.6 1.1 %collective-permute-done.4.h2 = bf16[2,224,128]{2,1,0:T(8,128)(2,1)S(1)} collective-permute-done((bf16[2,224,128]{2,1,0:T(8,128)(2,1)S(1)}, bf16[2,224,128]{2,1,0:T(8,128)(2,1)S(1)}, u32[]{:S(2)}, u32[]{:S(2)}) %collective-permute-start.4) | collective-permute-done | bytes 114720 | tf_op jit(solution)/shard_map/ppermute | solution.py:191
  29.7 0.0 collective-permute-done.5.h3
  29.7 0.0 copy-done.1
  29.7 5.6 %pairs_first.1 = (bf16[128,2048]{1,0:T(8,128)(2,1)S(1)}, f32[8,2048]{1,0:T(8,128)S(1)}, bf16[128,2048]{1,0:T(8,128)(2,1)S(1)}, f32[128,2048]{1,0:T(8,128)S(1)}, f32[16,128]{1,0:T(8,128)S(1)}) custom-call(bf16[2,224,128]{2,1,0:T(8,128)(2,1)S(1)} %pad_maximum_fusion.2.h0, bf16[6,224,128]{2,1,0:T(8,128)(2,1)S(1)} %constant_dynamic-update-slice_fusion.h1, ...), custom_call_target="tpu_custom_call" | custom-call | flops 1 | bytes 1 | tf_op jit(solution)/shard_map/pairs_first/pallas_call | solution.py:235
  35.4 0.0 collective-permute-done.10.b_ref
  35.4 0.0 collective-permute-done.9.a_ref
  35.4 10.9 %pairs_middle.1 = (f32[128,2048]{1,0:T(8,128)S(1)}, f32[16,128]{1,0:T(8,128)S(1)}) custom-call(bf16[128,2048]{1,0:T(8,128)(2,1)S(1)} %get-tuple-element.17.ct, f32[8,2048]{1,0:T(8,128)S(1)} %get-tuple-element.18.hc, bf16[128,2048]{1,0:T(8,128)(2,1)S(1)} %get-tuple-element.19.ut, f32[128,2048]{1,0:T(8,128)S(1)} %get-tuple-element.20.t0, ...), custom_call_target="tpu_custom_call" | custom-call | flops 1 | bytes 1 | tf_op jit(solution)/shard_map/pairs_middle/pallas_call | solution.py:255
  46.3 0.0 collective-permute-done.11.a_ref
  46.3 6.3 %pairs_last.1 = (f32[2,2,4,128,128]{4,3,2,1,0:T(8,128)S(1)}, f32[64,1,128]{2,1,0:T(1,128)}) custom-call(s32[1]{0:T(128)} %bitcast.at_ref, bf16[128,2048]{1,0:T(8,128)(2,1)S(1)} %get-tuple-element.17.ct, f32[8,2048]{1,0:T(8,128)S(1)} %get-tuple-element.18.hc, bf16[128,2048]{1,0:T(8,128)(2,1)S(1)} %get-tuple-element.19.ut, ...), custom_call_target="tpu_custom_call" | custom-call | flops 1811939328 | bytes 4194304 | tf_op jit(solution)/shard_map/pairs_last/pallas_call | solution.py:269
  52.6 0.1 convert.4
  52.7 9.6 %all-to-all-start = ((f32[64,1,128]{2,1,0:T(1,128)}), f32[64,1,128]{2,1,0:T(1,128)S(1)}, u32[]{:S(2)}, u32[]{:S(2)}) async-start(f32[64,1,128]{2,1,0:T(1,128)} %get-tuple-element.25), calls=%async_computation | async-start | bytes 65536 | tf_op jit(solution)/shard_map/all_to_all | solution.py:306
  62.3 1.5 %collective-permute-start.13 = (bf16[4,128,128]{2,1,0:T(8,128)(2,1)S(1)}, bf16[4,128,128]{2,1,0:T(8,128)(2,1)S(1)}, u32[]{:S(2)}, u32[]{:S(2)}) collective-permute-start(bf16[4,128,128]{2,1,0:T(8,128)(2,1)S(1)} %get-tuple-element.26), channel_id=1, source_target_pairs={{0,4},{4,0},{1,5},{5,1},{2,6},{6,2},{3,7},{7,3},{8,12},{12,8},{9,1... | collective-permute-start | bytes 393224 | tf_op jit(solution)/shard_map/ppermute | solution.py:191
  63.8 0.7 collective-permute-start.14
  64.5 0.0 collective-permute-start.12
  64.5 5.5 %all-to-all-done = f32[64,1,128]{2,1,0:T(1,128)S(1)} async-done(((f32[64,1,128]{2,1,0:T(1,128)}), f32[64,1,128]{2,1,0:T(1,128)S(1)}, u32[]{:S(2)}, u32[]{:S(2)}) %all-to-all-start) | async-done | bytes 32800 | tf_op jit(solution)/shard_map/all_to_all | solution.py:306
  70.0 0.1 reduce_sum.29
  70.1 0.1 maximum_maximum_fusion
  70.2 0.0 collective-permute-done.13
  70.2 0.5 collective-permute-done.14
  70.6 0.0 collective-permute-done.12
  70.6 0.1 fusion.2
  70.7 10.2 %all_to_all.10 = bf16[4,144,128]{2,1,0:T(8,128)(2,1)S(1)} all-to-all(bf16[4,144,128]{2,1,0:T(8,128)(2,1)S(1)} %pad_maximum_fusion.1), channel_id=1, replica_groups=mesh['zh'=4,'y'=4,'core'=2,'zl'=2,'x'=4] {'zh'}, dimensions={0} | all-to-all | bytes 294912 | tf_op jit(solution)/shard_map/all_to_all | solution.py:308
  81.0 0.5 bitcast_divide_fusion
  81.5 0.6 convert_reduce_fusion
  (11 shorter events, 0.1 us)
Async XLA Ops:
  2.2 17.4 %copy-start = (bf16[512,128]{1,0:T(8,128)(2,1)S(1)}, bf16[512,128]{1,0:T(8,128)(2,1)}, u32[]{:S(2)}) copy-start(bf16[512,128]{1,0:T(8,128)(2,1)} %get-tuple-element.15.a_ref) | copy-start | bytes 393220
  2.2 6.9 %collective-permute-start = (bf16[224,128]{1,0:T(8,128)(2,1)}, bf16[224,128]{1,0:T(8,128)(2,1)S(1)}, u32[]{:S(2)}, u32[]{:S(2)}) collective-permute-start(bf16[224,128]{1,0:T(8,128)(2,1)} %get-tuple-element.14), channel_id=1, source_target_pairs={{0,4},{4,0},{1,5},{5,1},{2,6},{6,2},{3,7},{7,3},{8,12},{12,8},{9,1... | collective-permute-start | bytes 172040 | tf_op jit(solution)/shard_map/ppermute | solution.py:191
  4.7 10.5 %collective-permute-start.6 = (bf16[512,128]{1,0:T(8,128)(2,1)}, bf16[512,128]{1,0:T(8,128)(2,1)S(1)}, u32[]{:S(2)}, u32[]{:S(2)}) collective-permute-start(bf16[512,128]{1,0:T(8,128)(2,1)} %get-tuple-element.15.a_ref), channel_id=1, source_target_pairs={{0,1},{1,2},{2,3},{3,0},{8,24},{9,25},{10,26},{11,27},{16,17},{17,... | collective-permute-start | bytes 393224 | tf_op jit(solution)/shard_map/ppermute | solution.py:202
  6.0 13.6 %collective-permute-start.7 = (bf16[512,128]{1,0:T(8,128)(2,1)}, bf16[512,128]{1,0:T(8,128)(2,1)S(1)}, u32[]{:S(2)}, u32[]{:S(2)}) collective-permute-start(bf16[512,128]{1,0:T(8,128)(2,1)} %get-tuple-element.15.a_ref), channel_id=1, source_target_pairs={{0,3},{1,0},{2,1},{3,2},{8,56},{9,57},{10,58},{11,59},{16,19},{17,... | collective-permute-start | bytes 393224 | tf_op jit(solution)/shard_map/ppermute | solution.py:202
  7.4 12.2 %collective-permute-start.8 = (bf16[512,128]{1,0:T(8,128)(2,1)}, bf16[512,128]{1,0:T(8,128)(2,1)S(1)}, u32[]{:S(2)}, u32[]{:S(2)}) collective-permute-start(bf16[512,128]{1,0:T(8,128)(2,1)} %get-tuple-element.15.a_ref), channel_id=1, source_target_pairs={{0,2},{1,3},{2,0},{3,1},{8,40},{9,41},{10,42},{11,43},{16,18},{17,... | collective-permute-start | bytes 393224 | tf_op jit(solution)/shard_map/ppermute | solution.py:202
  9.9 13.5 %collective-permute-start.1 = (bf16[2,224,128]{2,1,0:T(8,128)(2,1)S(1)}, bf16[2,224,128]{2,1,0:T(8,128)(2,1)S(1)}, u32[]{:S(2)}, u32[]{:S(2)}) collective-permute-start(bf16[2,224,128]{2,1,0:T(8,128)(2,1)S(1)} %pad_maximum_fusion.2.h0), channel_id=1, source_target_pairs={{0,64},{64,128},{128,192},{192,0},{1,65},{65,129},{129,193},{193,1... | collective-permute-start | bytes 344072 | tf_op jit(solution)/shard_map/ppermute | solution.py:191
  13.0 11.0 %collective-permute-start.2 = (bf16[2,224,128]{2,1,0:T(8,128)(2,1)S(1)}, bf16[2,224,128]{2,1,0:T(8,128)(2,1)S(1)}, u32[]{:S(2)}, u32[]{:S(2)}) collective-permute-start(bf16[2,224,128]{2,1,0:T(8,128)(2,1)S(1)} %pad_maximum_fusion.2.h0), channel_id=1, source_target_pairs={{0,192},{64,0},{128,64},{192,128},{1,193},{65,1},{129,65},{193,129... | collective-permute-start | bytes 344072 | tf_op jit(solution)/shard_map/ppermute | solution.py:191
  15.2 9.6 %collective-permute-start.3 = (bf16[2,224,128]{2,1,0:T(8,128)(2,1)S(1)}, bf16[2,224,128]{2,1,0:T(8,128)(2,1)S(1)}, u32[]{:S(2)}, u32[]{:S(2)}) collective-permute-start(bf16[2,224,128]{2,1,0:T(8,128)(2,1)S(1)} %pad_maximum_fusion.2.h0), channel_id=1, source_target_pairs={{0,128},{64,192},{128,0},{192,64},{1,129},{65,193},{129,1},{193,65... | collective-permute-start | bytes 344072 | tf_op jit(solution)/shard_map/ppermute | solution.py:191
  19.7 15.7 %collective-permute-start.10 = (bf16[4,512,128]{2,1,0:T(8,128)(2,1)S(1)}, bf16[4,512,128]{2,1,0:T(8,128)(2,1)S(1)}, u32[]{:S(2)}, u32[]{:S(2)}) collective-permute-start(bf16[4,512,128]{2,1,0:T(8,128)(2,1)S(1)} %pad_maximum_fusion), channel_id=1, source_target_pairs={{0,32},{1,33},{2,34},{3,35},{8,10},{9,11},{10,8},{11,9},{16,48},{1... | collective-permute-start | bytes 1572872 | tf_op jit(solution)/shard_map/ppermute | solution.py:202
  22.5 12.9 %collective-permute-start.9 = (bf16[4,512,128]{2,1,0:T(8,128)(2,1)S(1)}, bf16[4,512,128]{2,1,0:T(8,128)(2,1)S(1)}, u32[]{:S(2)}, u32[]{:S(2)}) collective-permute-start(bf16[4,512,128]{2,1,0:T(8,128)(2,1)S(1)} %pad_maximum_fusion), channel_id=1, source_target_pairs={{0,48},{1,49},{2,50},{3,51},{8,11},{9,8},{10,9},{11,10},{16,0},{17... | collective-permute-start | bytes 1572872 | tf_op jit(solution)/shard_map/ppermute | solution.py:202
  23.4 23.0 %collective-permute-start.11 = (bf16[4,512,128]{2,1,0:T(8,128)(2,1)S(1)}, bf16[4,512,128]{2,1,0:T(8,128)(2,1)S(1)}, u32[]{:S(2)}, u32[]{:S(2)}) collective-permute-start(bf16[4,512,128]{2,1,0:T(8,128)(2,1)S(1)} %pad_maximum_fusion), channel_id=1, source_target_pairs={{0,16},{1,17},{2,18},{3,19},{8,9},{9,10},{10,11},{11,8},{16,32},{1... | collective-permute-start | bytes 1572872 | tf_op jit(solution)/shard_map/ppermute | solution.py:202
  24.8 4.9 %collective-permute-start.5 = (bf16[6,224,128]{2,1,0:T(8,128)(2,1)S(1)}, bf16[6,224,128]{2,1,0:T(8,128)(2,1)S(1)}, u32[]{:S(2)}, u32[]{:S(2)}) collective-permute-start(bf16[6,224,128]{2,1,0:T(8,128)(2,1)S(1)} %constant_dynamic-update-slice_fusion.h1), channel_id=1, source_target_pairs={{0,8},{8,0},{1,9},{9,1},{2,10},{10,2},{3,11},{11,3},{4,12},{12,4},... | collective-permute-start | bytes 1032200 | tf_op jit(solution)/shard_map/ppermute | solution.py:191
  28.3 1.4 %collective-permute-start.4 = (bf16[2,224,128]{2,1,0:T(8,128)(2,1)S(1)}, bf16[2,224,128]{2,1,0:T(8,128)(2,1)S(1)}, u32[]{:S(2)}, u32[]{:S(2)}) collective-permute-start(bf16[2,224,128]{2,1,0:T(8,128)(2,1)S(1)} %pad_maximum_fusion.2.h0), channel_id=1, source_target_pairs={{0,8},{8,0},{1,9},{9,1},{2,10},{10,2},{3,11},{11,3},{4,12},{12,4},... | collective-permute-start | bytes 344072 | tf_op jit(solution)/shard_map/ppermute | solution.py:191
  28.6 1.2 %copy-start.1 = (f32[8,128]{1,0:T(8,128)S(1)}, f32[8,128]{1,0:T(8,128)}, u32[]{:S(2)}) copy-start(f32[8,128]{1,0:T(8,128)} %get-tuple-element.16.lv_ref) | copy-start | bytes 12292
  52.7 17.3 %all-to-all-start = ((f32[64,1,128]{2,1,0:T(1,128)}), f32[64,1,128]{2,1,0:T(1,128)S(1)}, u32[]{:S(2)}, u32[]{:S(2)}) async-start(f32[64,1,128]{2,1,0:T(1,128)} %get-tuple-element.25), calls=%async_computation | async-start | bytes 65536 | tf_op jit(solution)/shard_map/all_to_all | solution.py:306
  62.3 7.8 %collective-permute-start.13 = (bf16[4,128,128]{2,1,0:T(8,128)(2,1)S(1)}, bf16[4,128,128]{2,1,0:T(8,128)(2,1)S(1)}, u32[]{:S(2)}, u32[]{:S(2)}) collective-permute-start(bf16[4,128,128]{2,1,0:T(8,128)(2,1)S(1)} %get-tuple-element.26), channel_id=1, source_target_pairs={{0,4},{4,0},{1,5},{5,1},{2,6},{6,2},{3,7},{7,3},{8,12},{12,8},{9,1... | collective-permute-start | bytes 393224 | tf_op jit(solution)/shard_map/ppermute | solution.py:191
  63.8 6.8 %collective-permute-start.14 = (bf16[4,128,128]{2,1,0:T(8,128)(2,1)S(1)}, bf16[4,128,128]{2,1,0:T(8,128)(2,1)S(1)}, u32[]{:S(2)}, u32[]{:S(2)}) collective-permute-start(bf16[4,128,128]{2,1,0:T(8,128)(2,1)S(1)} %get-tuple-element.27), channel_id=1, source_target_pairs={{0,12},{4,8},{8,4},{12,0},{1,13},{5,9},{9,5},{13,1},{2,14},{6,10},... | collective-permute-start | bytes 393224 | tf_op jit(solution)/shard_map/ppermute | solution.py:305
  64.5 6.1 %collective-permute-start.12 = (f32[4,128,128]{2,1,0:T(8,128)S(1)}, f32[4,128,128]{2,1,0:T(8,128)S(1)}, u32[]{:S(2)}, u32[]{:S(2)}) collective-permute-start(f32[4,128,128]{2,1,0:T(8,128)S(1)} %slice_bitcast_fusion), channel_id=1, source_target_pairs={{0,8},{8,0},{1,9},{9,1},{2,10},{10,2},{3,11},{11,3},{4,12},{12,4},... | collective-permute-start | bytes 786440 | tf_op jit(solution)/shard_map/ppermute | solution.py:191

commit v7 on v5

--- a/solution.py
+++ b/solution.py
@@ -293,7 +293,7 @@
     side = [pp] + [plane_shift(pp, by, False) for by in (1, 3, 2)]
     two = jnp.stack([cb, shifted(cb, "zl", 1)])
     line = jnp.stack(side)
-    rest = [plane_shift(line, by, True) for by in (1, 3, 2)]
+    rest = [plane_shift(line, by, True) for by in (2, 1, 3)]
     two_other = shifted(two, "core", 1)
     six = jnp.concatenate([shifted(two, "zh", by) for by in SHIFTS[1:]], 0)
     held = (two, six, two_other, shifted(six, "core", 1))

time: 83.9 us -> 85.7 us (1.021)
  waiting for transfers between devices: 8.27 us -> 10.3 us
  starting transfers between devices: 33.6 us -> 32.3 us
  blocking collectives: 13.4 us -> 14.6 us
    ppermute x6, waiting for transfers between devices: 0.02 us -> 2.01 us  [plane_shift(): return lax.ppermute(value, PLANE_AXES, perm)]
    all_to_all x1, starting transfers between devices: 8.73 us -> 7.34 us  [local(): scale = jnp.sum(lax.all_to_all(scale, SCALE_AXES, 0, 0, tiled=True), (0, 1))]
    all_to_all x1, blocking collectives: 13.4 us -> 14.6 us  [local(): parts = lax.all_to_all(chunk, CENTER_AXES, 0, 0, tiled=True)]
  transfers between devices with their start and end apart: 14 -> 14, of which waited for: 3 -> 4; matrix products, arithmetic and copies ran while one was open for 2% -> 1% of each run, Pallas kernels for 20% -> 19%
where the time goes in v7:
time: 85.7 us; the launch traced here: 85.4 us
  starting transfers between devices  32.3 us (38%)
  Pallas kernels  24.9 us (29%)
  blocking collectives  14.6 us (17%)
  waiting for transfers between devices  10.3 us (12%)
  other arithmetic  2.41 us (3%)
    ppermute x7, starting transfers between devices, shifted(): return lax.ppermute(value, axis, [(i, (i + by) % n) for i in range(n)])  16.3 us
    all_to_all x1, blocking collectives, local(): parts = lax.all_to_all(chunk, CENTER_AXES, 0, 0, tiled=True)  14.6 us
    pallas_call x1, Pallas kernels, middle_call(): pl.pallas_call(middle_kernel, out_shape=[shape((D, M), F32), shape((16, D...  10.9 us
    ppermute x6, starting transfers between devices, plane_shift(): return lax.ppermute(value, PLANE_AXES, perm)  8.67 us
    all_to_all x1, starting transfers between devices, local(): scale = jnp.sum(lax.all_to_all(scale, SCALE_AXES, 0, 0, tiled=True), (0, 1))  7.34 us
    pallas_call x1, Pallas kernels, last_call(): pl.pallas_call(last_kernel, out_shape=[shape((2, NZ, CTR, D), F32), shape...  6.76 us
    all_to_all x1, waiting for transfers between devices, local(): scale = jnp.sum(lax.all_to_all(scale, SCALE_AXES, 0, 0, tiled=True), (0, 1))  6.5 us
    pallas_call x1, Pallas kernels, first_call(): pl.pallas_call(first_kernel, out_shape=[shape((D, M), BF), shape((8, M),...  5.64 us
  transfers between devices with their start and end apart: 14, of which 4 were waited for; matrix products, arithmetic and copies ran while one was open for 1% of the time, Pallas kernels for 19%

profile of v7, /device:TPU:1, one launch (start us, length us, event | category | flops | bytes accessed | tf_op | source)
XLA Modules:
  0.0 85.4 jit_solution(1555601857294417733)
XLA Ops:
  0.6 1.6 %prep.1 = (bf16[512,128]{1,0:T(8,128)(2,1)}, bf16[224,128]{1,0:T(8,128)(2,1)}, f32[8,128]{1,0:T(8,128)}) custom-call(bf16[256,128]{1,0:T(8,128)(2,1)} %x_ref.1, bf16[32,256]{1,0:T(8,128)(2,1)} %bitcast.40, bf16[128,128]{1,0:T(8,128)(2,1)} %c_ref.1, bf16[32,128]{1,0:T(8,128)(2,1)} %bitcast.41, bf16[32,128]{1,0:T(8,128)(2,1)} %bitcast.42, ...), custom_call_target="tpu_custom_call" | custom-call | tf_op jit(solution)/shard_map/prep/pallas_call | solution.py:286
  2.2 0.0 copy-start
  2.2 2.5 %collective-permute-start = (bf16[224,128]{1,0:T(8,128)(2,1)}, bf16[224,128]{1,0:T(8,128)(2,1)S(1)}, u32[]{:S(2)}, u32[]{:S(2)}) collective-permute-start(bf16[224,128]{1,0:T(8,128)(2,1)} %get-tuple-element.14), channel_id=1, source_target_pairs={{0,4},{4,0},{1,5},{5,1},{2,6},{6,2},{3,7},{7,3},{8,12},{12,8},{9,1... | collective-permute-start | bytes 172040 | tf_op jit(solution)/shard_map/ppermute | solution.py:193
  4.7 1.3 %collective-permute-start.6 = (bf16[512,128]{1,0:T(8,128)(2,1)}, bf16[512,128]{1,0:T(8,128)(2,1)S(1)}, u32[]{:S(2)}, u32[]{:S(2)}) collective-permute-start(bf16[512,128]{1,0:T(8,128)(2,1)} %get-tuple-element.15.a_ref), channel_id=1, source_target_pairs={{0,1},{1,2},{2,3},{3,0},{8,24},{9,25},{10,26},{11,27},{16,17},{17,... | collective-permute-start | bytes 393224 | tf_op jit(solution)/shard_map/ppermute | solution.py:204
  6.0 1.4 %collective-permute-start.7 = (bf16[512,128]{1,0:T(8,128)(2,1)}, bf16[512,128]{1,0:T(8,128)(2,1)S(1)}, u32[]{:S(2)}, u32[]{:S(2)}) collective-permute-start(bf16[512,128]{1,0:T(8,128)(2,1)} %get-tuple-element.15.a_ref), channel_id=1, source_target_pairs={{0,3},{1,0},{2,1},{3,2},{8,56},{9,57},{10,58},{11,59},{16,19},{17,... | collective-permute-start | bytes 393224 | tf_op jit(solution)/shard_map/ppermute | solution.py:204
  7.4 1.6 %collective-permute-start.8 = (bf16[512,128]{1,0:T(8,128)(2,1)}, bf16[512,128]{1,0:T(8,128)(2,1)S(1)}, u32[]{:S(2)}, u32[]{:S(2)}) collective-permute-start(bf16[512,128]{1,0:T(8,128)(2,1)} %get-tuple-element.15.a_ref), channel_id=1, source_target_pairs={{0,2},{1,3},{2,0},{3,1},{8,40},{9,41},{10,42},{11,43},{16,18},{17,... | collective-permute-start | bytes 393224 | tf_op jit(solution)/shard_map/ppermute | solution.py:204
  9.1 0.0 collective-permute-done
  9.1 0.8 pad_maximum_fusion.2.h0
  9.9 3.1 %collective-permute-start.1 = (bf16[2,224,128]{2,1,0:T(8,128)(2,1)S(1)}, bf16[2,224,128]{2,1,0:T(8,128)(2,1)S(1)}, u32[]{:S(2)}, u32[]{:S(2)}) collective-permute-start(bf16[2,224,128]{2,1,0:T(8,128)(2,1)S(1)} %pad_maximum_fusion.2.h0), channel_id=1, source_target_pairs={{0,64},{64,128},{128,192},{192,0},{1,65},{65,129},{129,193},{193,1... | collective-permute-start | bytes 344072 | tf_op jit(solution)/shard_map/ppermute | solution.py:193
  13.0 2.2 %collective-permute-start.2 = (bf16[2,224,128]{2,1,0:T(8,128)(2,1)S(1)}, bf16[2,224,128]{2,1,0:T(8,128)(2,1)S(1)}, u32[]{:S(2)}, u32[]{:S(2)}) collective-permute-start(bf16[2,224,128]{2,1,0:T(8,128)(2,1)S(1)} %pad_maximum_fusion.2.h0), channel_id=1, source_target_pairs={{0,192},{64,0},{128,64},{192,128},{1,193},{65,1},{129,65},{193,129... | collective-permute-start | bytes 344072 | tf_op jit(solution)/shard_map/ppermute | solution.py:193
  15.2 0.0 collective-permute-done.6.b_ref
  15.2 4.4 %collective-permute-start.3 = (bf16[2,224,128]{2,1,0:T(8,128)(2,1)S(1)}, bf16[2,224,128]{2,1,0:T(8,128)(2,1)S(1)}, u32[]{:S(2)}, u32[]{:S(2)}) collective-permute-start(bf16[2,224,128]{2,1,0:T(8,128)(2,1)S(1)} %pad_maximum_fusion.2.h0), channel_id=1, source_target_pairs={{0,128},{64,192},{128,0},{192,64},{1,129},{65,193},{129,1},{193,65... | collective-permute-start | bytes 344072 | tf_op jit(solution)/shard_map/ppermute | solution.py:193
  19.6 0.0 collective-permute-done.7.c_ref
  19.6 0.0 collective-permute-done.8.d_ref
  19.6 0.0 copy-done
  19.6 0.1 pad_maximum_fusion
  19.7 2.6 %collective-permute-start.10 = (bf16[4,512,128]{2,1,0:T(8,128)(2,1)S(1)}, bf16[4,512,128]{2,1,0:T(8,128)(2,1)S(1)}, u32[]{:S(2)}, u32[]{:S(2)}) collective-permute-start(bf16[4,512,128]{2,1,0:T(8,128)(2,1)S(1)} %pad_maximum_fusion), channel_id=1, source_target_pairs={{0,48},{1,49},{2,50},{3,51},{8,11},{9,8},{10,9},{11,10},{16,0},{17... | collective-permute-start | bytes 1572872 | tf_op jit(solution)/shard_map/ppermute | solution.py:204
  22.2 0.0 collective-permute-start.9
  22.2 0.0 collective-permute-done.1
  22.2 1.7 %collective-permute-start.11 = (bf16[4,512,128]{2,1,0:T(8,128)(2,1)S(1)}, bf16[4,512,128]{2,1,0:T(8,128)(2,1)S(1)}, u32[]{:S(2)}, u32[]{:S(2)}) collective-permute-start(bf16[4,512,128]{2,1,0:T(8,128)(2,1)S(1)} %pad_maximum_fusion), channel_id=1, source_target_pairs={{0,32},{1,33},{2,34},{3,35},{8,10},{9,11},{10,8},{11,9},{16,48},{1... | collective-permute-start | bytes 1572872 | tf_op jit(solution)/shard_map/ppermute | solution.py:204
  24.0 0.0 collective-permute-done.2
  24.0 0.8 collective-permute-done.3
  24.8 3.5 %collective-permute-start.5 = (bf16[6,224,128]{2,1,0:T(8,128)(2,1)S(1)}, bf16[6,224,128]{2,1,0:T(8,128)(2,1)S(1)}, u32[]{:S(2)}, u32[]{:S(2)}) collective-permute-start(bf16[6,224,128]{2,1,0:T(8,128)(2,1)S(1)} %constant_dynamic-update-slice_fusion.h1), channel_id=1, source_target_pairs={{0,8},{8,0},{1,9},{9,1},{2,10},{10,2},{3,11},{11,3},{4,12},{12,4},... | collective-permute-start | bytes 1032200 | tf_op jit(solution)/shard_map/ppermute | solution.py:193
  28.3 0.3 collective-permute-start.4
  28.6 0.1 pad.5.clone
  28.6 0.0 copy-start.1
  28.6 0.1 pad_add_fusion.at_ref
  28.7 1.0 %collective-permute-done.4.h2 = bf16[2,224,128]{2,1,0:T(8,128)(2,1)S(1)} collective-permute-done((bf16[2,224,128]{2,1,0:T(8,128)(2,1)S(1)}, bf16[2,224,128]{2,1,0:T(8,128)(2,1)S(1)}, u32[]{:S(2)}, u32[]{:S(2)}) %collective-permute-start.4) | collective-permute-done | bytes 114720 | tf_op jit(solution)/shard_map/ppermute | solution.py:193
  29.7 0.0 collective-permute-done.5.h3
  29.7 0.0 copy-done.1
  29.7 5.6 %pairs_first.1 = (bf16[128,2048]{1,0:T(8,128)(2,1)S(1)}, f32[8,2048]{1,0:T(8,128)S(1)}, bf16[128,2048]{1,0:T(8,128)(2,1)S(1)}, f32[128,2048]{1,0:T(8,128)S(1)}, f32[16,128]{1,0:T(8,128)S(1)}) custom-call(bf16[2,224,128]{2,1,0:T(8,128)(2,1)S(1)} %pad_maximum_fusion.2.h0, bf16[6,224,128]{2,1,0:T(8,128)(2,1)S(1)} %constant_dynamic-update-slice_fusion.h1, ...), custom_call_target="tpu_custom_call" | custom-call | flops 1 | bytes 1 | tf_op jit(solution)/shard_map/pairs_first/pallas_call | solution.py:237
  35.4 0.0 collective-permute-done.10.b_ref
  35.4 2.0 %collective-permute-done.9.a_ref = bf16[4,512,128]{2,1,0:T(8,128)(2,1)S(1)} collective-permute-done((bf16[4,512,128]{2,1,0:T(8,128)(2,1)S(1)}, bf16[4,512,128]{2,1,0:T(8,128)(2,1)S(1)}, u32[]{:S(2)}, u32[]{:S(2)}) %collective-permute-start.9) | collective-permute-done | bytes 524320 | tf_op jit(solution)/shard_map/ppermute | solution.py:204
  37.4 10.9 %pairs_middle.1 = (f32[128,2048]{1,0:T(8,128)S(1)}, f32[16,128]{1,0:T(8,128)S(1)}) custom-call(bf16[128,2048]{1,0:T(8,128)(2,1)S(1)} %get-tuple-element.17.ct, f32[8,2048]{1,0:T(8,128)S(1)} %get-tuple-element.18.hc, bf16[128,2048]{1,0:T(8,128)(2,1)S(1)} %get-tuple-element.19.ut, f32[128,2048]{1,0:T(8,128)S(1)} %get-tuple-element.20.t0, ...), custom_call_target="tpu_custom_call" | custom-call | flops 1 | bytes 1 | tf_op jit(solution)/shard_map/pairs_middle/pallas_call | solution.py:257
  48.3 0.0 collective-permute-done.11.a_ref
  48.3 6.8 %pairs_last.1 = (f32[2,8,128,128]{3,2,1,0:T(8,128)S(1)}, f32[32,1,128]{2,1,0:T(1,128)}) custom-call(s32[2]{0:T(128)S(1)} %pad_add_fusion.at_ref, bf16[128,2048]{1,0:T(8,128)(2,1)S(1)} %get-tuple-element.17.ct, f32[8,2048]{1,0:T(8,128)S(1)} %get-tuple-element.18.hc, bf16[128,2048]{1,0:T(8,128)(2,1)S(1)} %get-tuple-element.19.ut, ...), custom_call_target="tpu_custom_call" | custom-call | flops 1811939328 | bytes 4194304 | tf_op jit(solution)/shard_map/pairs_last/pallas_call | solution.py:271
  55.1 7.3 %all-to-all-start = ((f32[32,1,128]{2,1,0:T(1,128)}), f32[32,1,128]{2,1,0:T(1,128)S(1)}, u32[]{:S(2)}, u32[]{:S(2)}) async-start(f32[32,1,128]{2,1,0:T(1,128)} %get-tuple-element.25), calls=%async_computation | async-start | bytes 32768 | tf_op jit(solution)/shard_map/all_to_all | solution.py:305
  62.5 0.4 collective-permute-start.12
  62.9 6.5 %all-to-all-done = f32[32,1,128]{2,1,0:T(1,128)S(1)} async-done(((f32[32,1,128]{2,1,0:T(1,128)}), f32[32,1,128]{2,1,0:T(1,128)S(1)}, u32[]{:S(2)}, u32[]{:S(2)}) %all-to-all-start) | async-done | bytes 16416 | tf_op jit(solution)/shard_map/all_to_all | solution.py:305
  69.4 0.1 reduce_sum.29
  69.5 0.1 maximum_maximum_fusion
  69.5 0.0 collective-permute-done.12
  69.5 0.1 fusion
  69.6 14.6 %all_to_all.10 = bf16[8,144,128]{2,1,0:T(8,128)(2,1)S(1)} all-to-all(bf16[8,144,128]{2,1,0:T(8,128)(2,1)S(1)} %pad_maximum_fusion.1), channel_id=1, replica_groups=mesh['zh'=4,'y'=4,'core'=2,'zl'=2,'x'=4] {'zh','zl'}, dimensions={0} | all-to-all | bytes 589824 | tf_op jit(solution)/shard_map/all_to_all | solution.py:308
  84.3 0.5 bitcast_divide_fusion
  84.8 0.7 convert_reduce_fusion
  (10 shorter events, 0.2 us)
Async XLA Ops:
  2.2 17.4 %copy-start = (bf16[512,128]{1,0:T(8,128)(2,1)S(1)}, bf16[512,128]{1,0:T(8,128)(2,1)}, u32[]{:S(2)}) copy-start(bf16[512,128]{1,0:T(8,128)(2,1)} %get-tuple-element.15.a_ref) | copy-start | bytes 393220
  2.2 6.9 %collective-permute-start = (bf16[224,128]{1,0:T(8,128)(2,1)}, bf16[224,128]{1,0:T(8,128)(2,1)S(1)}, u32[]{:S(2)}, u32[]{:S(2)}) collective-permute-start(bf16[224,128]{1,0:T(8,128)(2,1)} %get-tuple-element.14), channel_id=1, source_target_pairs={{0,4},{4,0},{1,5},{5,1},{2,6},{6,2},{3,7},{7,3},{8,12},{12,8},{9,1... | collective-permute-start | bytes 172040 | tf_op jit(solution)/shard_map/ppermute | solution.py:193
  4.7 10.5 %collective-permute-start.6 = (bf16[512,128]{1,0:T(8,128)(2,1)}, bf16[512,128]{1,0:T(8,128)(2,1)S(1)}, u32[]{:S(2)}, u32[]{:S(2)}) collective-permute-start(bf16[512,128]{1,0:T(8,128)(2,1)} %get-tuple-element.15.a_ref), channel_id=1, source_target_pairs={{0,1},{1,2},{2,3},{3,0},{8,24},{9,25},{10,26},{11,27},{16,17},{17,... | collective-permute-start | bytes 393224 | tf_op jit(solution)/shard_map/ppermute | solution.py:204
  6.0 13.6 %collective-permute-start.7 = (bf16[512,128]{1,0:T(8,128)(2,1)}, bf16[512,128]{1,0:T(8,128)(2,1)S(1)}, u32[]{:S(2)}, u32[]{:S(2)}) collective-permute-start(bf16[512,128]{1,0:T(8,128)(2,1)} %get-tuple-element.15.a_ref), channel_id=1, source_target_pairs={{0,3},{1,0},{2,1},{3,2},{8,56},{9,57},{10,58},{11,59},{16,19},{17,... | collective-permute-start | bytes 393224 | tf_op jit(solution)/shard_map/ppermute | solution.py:204
  7.4 12.2 %collective-permute-start.8 = (bf16[512,128]{1,0:T(8,128)(2,1)}, bf16[512,128]{1,0:T(8,128)(2,1)S(1)}, u32[]{:S(2)}, u32[]{:S(2)}) collective-permute-start(bf16[512,128]{1,0:T(8,128)(2,1)} %get-tuple-element.15.a_ref), channel_id=1, source_target_pairs={{0,2},{1,3},{2,0},{3,1},{8,40},{9,41},{10,42},{11,43},{16,18},{17,... | collective-permute-start | bytes 393224 | tf_op jit(solution)/shard_map/ppermute | solution.py:204
  9.9 12.3 %collective-permute-start.1 = (bf16[2,224,128]{2,1,0:T(8,128)(2,1)S(1)}, bf16[2,224,128]{2,1,0:T(8,128)(2,1)S(1)}, u32[]{:S(2)}, u32[]{:S(2)}) collective-permute-start(bf16[2,224,128]{2,1,0:T(8,128)(2,1)S(1)} %pad_maximum_fusion.2.h0), channel_id=1, source_target_pairs={{0,64},{64,128},{128,192},{192,0},{1,65},{65,129},{129,193},{193,1... | collective-permute-start | bytes 344072 | tf_op jit(solution)/shard_map/ppermute | solution.py:193
  13.0 11.0 %collective-permute-start.2 = (bf16[2,224,128]{2,1,0:T(8,128)(2,1)S(1)}, bf16[2,224,128]{2,1,0:T(8,128)(2,1)S(1)}, u32[]{:S(2)}, u32[]{:S(2)}) collective-permute-start(bf16[2,224,128]{2,1,0:T(8,128)(2,1)S(1)} %pad_maximum_fusion.2.h0), channel_id=1, source_target_pairs={{0,192},{64,0},{128,64},{192,128},{1,193},{65,1},{129,65},{193,129... | collective-permute-start | bytes 344072 | tf_op jit(solution)/shard_map/ppermute | solution.py:193
  15.2 9.6 %collective-permute-start.3 = (bf16[2,224,128]{2,1,0:T(8,128)(2,1)S(1)}, bf16[2,224,128]{2,1,0:T(8,128)(2,1)S(1)}, u32[]{:S(2)}, u32[]{:S(2)}) collective-permute-start(bf16[2,224,128]{2,1,0:T(8,128)(2,1)S(1)} %pad_maximum_fusion.2.h0), channel_id=1, source_target_pairs={{0,128},{64,192},{128,0},{192,64},{1,129},{65,193},{129,1},{193,65... | collective-permute-start | bytes 344072 | tf_op jit(solution)/shard_map/ppermute | solution.py:193
  19.7 15.7 %collective-permute-start.10 = (bf16[4,512,128]{2,1,0:T(8,128)(2,1)S(1)}, bf16[4,512,128]{2,1,0:T(8,128)(2,1)S(1)}, u32[]{:S(2)}, u32[]{:S(2)}) collective-permute-start(bf16[4,512,128]{2,1,0:T(8,128)(2,1)S(1)} %pad_maximum_fusion), channel_id=1, source_target_pairs={{0,48},{1,49},{2,50},{3,51},{8,11},{9,8},{10,9},{11,10},{16,0},{17... | collective-permute-start | bytes 1572872 | tf_op jit(solution)/shard_map/ppermute | solution.py:204
  22.2 15.2 %collective-permute-start.9 = (bf16[4,512,128]{2,1,0:T(8,128)(2,1)S(1)}, bf16[4,512,128]{2,1,0:T(8,128)(2,1)S(1)}, u32[]{:S(2)}, u32[]{:S(2)}) collective-permute-start(bf16[4,512,128]{2,1,0:T(8,128)(2,1)S(1)} %pad_maximum_fusion), channel_id=1, source_target_pairs={{0,16},{1,17},{2,18},{3,19},{8,9},{9,10},{10,11},{11,8},{16,32},{1... | collective-permute-start | bytes 1572872 | tf_op jit(solution)/shard_map/ppermute | solution.py:204
  22.2 26.1 %collective-permute-start.11 = (bf16[4,512,128]{2,1,0:T(8,128)(2,1)S(1)}, bf16[4,512,128]{2,1,0:T(8,128)(2,1)S(1)}, u32[]{:S(2)}, u32[]{:S(2)}) collective-permute-start(bf16[4,512,128]{2,1,0:T(8,128)(2,1)S(1)} %pad_maximum_fusion), channel_id=1, source_target_pairs={{0,32},{1,33},{2,34},{3,35},{8,10},{9,11},{10,8},{11,9},{16,48},{1... | collective-permute-start | bytes 1572872 | tf_op jit(solution)/shard_map/ppermute | solution.py:204
  24.8 4.9 %collective-permute-start.5 = (bf16[6,224,128]{2,1,0:T(8,128)(2,1)S(1)}, bf16[6,224,128]{2,1,0:T(8,128)(2,1)S(1)}, u32[]{:S(2)}, u32[]{:S(2)}) collective-permute-start(bf16[6,224,128]{2,1,0:T(8,128)(2,1)S(1)} %constant_dynamic-update-slice_fusion.h1), channel_id=1, source_target_pairs={{0,8},{8,0},{1,9},{9,1},{2,10},{10,2},{3,11},{11,3},{4,12},{12,4},... | collective-permute-start | bytes 1032200 | tf_op jit(solution)/shard_map/ppermute | solution.py:193
  28.3 1.4 %collective-permute-start.4 = (bf16[2,224,128]{2,1,0:T(8,128)(2,1)S(1)}, bf16[2,224,128]{2,1,0:T(8,128)(2,1)S(1)}, u32[]{:S(2)}, u32[]{:S(2)}) collective-permute-start(bf16[2,224,128]{2,1,0:T(8,128)(2,1)S(1)} %pad_maximum_fusion.2.h0), channel_id=1, source_target_pairs={{0,8},{8,0},{1,9},{9,1},{2,10},{10,2},{3,11},{11,3},{4,12},{12,4},... | collective-permute-start | bytes 344072 | tf_op jit(solution)/shard_map/ppermute | solution.py:193
  28.6 1.1 %copy-start.1 = (f32[8,128]{1,0:T(8,128)S(1)}, f32[8,128]{1,0:T(8,128)}, u32[]{:S(2)}) copy-start(f32[8,128]{1,0:T(8,128)} %get-tuple-element.16.lv_ref) | copy-start | bytes 12292
  55.1 14.3 %all-to-all-start = ((f32[32,1,128]{2,1,0:T(1,128)}), f32[32,1,128]{2,1,0:T(1,128)S(1)}, u32[]{:S(2)}, u32[]{:S(2)}) async-start(f32[32,1,128]{2,1,0:T(1,128)} %get-tuple-element.25), calls=%async_computation | async-start | bytes 32768 | tf_op jit(solution)/shard_map/all_to_all | solution.py:305
  62.5 7.1 %collective-permute-start.12 = (f32[8,128,128]{2,1,0:T(8,128)S(1)}, f32[8,128,128]{2,1,0:T(8,128)S(1)}, u32[]{:S(2)}, u32[]{:S(2)}) collective-permute-start(f32[8,128,128]{2,1,0:T(8,128)S(1)} %slice_bitcast_fusion), channel_id=1, source_target_pairs={{0,8},{8,0},{1,9},{9,1},{2,10},{10,2},{3,11},{11,3},{4,12},{12,4},... | collective-permute-start | bytes 1572872 | tf_op jit(solution)/shard_map/ppermute | solution.py:193

commit v8 on v5

--- a/solution.py
+++ b/solution.py
@@ -47,7 +47,8 @@
     c = (c_ref[...].astype(F32) / ls).astype(BF)
     lt, rt = l_ref[...], r_ref[...]
     pp_ref[...] = jnp.concatenate([x, c, v_ref[:, 0:CTR], v_ref[:, CTR:PTS], rt, lt], 0)
-    cb_ref[...] = jnp.concatenate([c, s_ref[...], lt, rt], 0)
+    cb_ref[0] = jnp.concatenate([c, s_ref[...], lt, rt], 0)
+    cb_ref[1] = jnp.zeros((CROWS, D), BF)
     lv_ref[...] = jnp.broadcast_to(ls, lv_ref.shape)
 
 
@@ -285,13 +286,13 @@
     shape = jax.ShapeDtypeStruct
     pp, cb, lv = pl.pallas_call(
         prep_kernel,
-        out_shape=[shape((PROWS, D), BF), shape((CROWS, D), BF), shape((8, D), F32)],
+        out_shape=[shape((PROWS, D), BF), shape((2, CROWS, D), BF), shape((8, D), F32)],
         in_specs=[VM] * 7,
         out_specs=[VM] * 3,
         name="prep",
     )(points, adjoint_rows.T, centers, solution_rows.T, center_left.T, center_right.T, ls)
     side = [pp] + [plane_shift(pp, by, False) for by in (1, 3, 2)]
-    two = jnp.stack([cb, shifted(cb, "zl", 1)])
+    two = cb.at[1].set(shifted(cb[0], "zl", 1))
     line = jnp.stack(side)
     rest = [plane_shift(line, by, True) for by in (1, 3, 2)]
     two_other = shifted(two, "core", 1)

time: 83.9 us -> 84.9 us (1.012)
  local copies, waits for them, and re-layouts: 0.18 us -> 1.66 us
    squeeze x0 -> x1, local copies, waits for them, and re-layouts: none -> 0.86 us  [local(): two = cb.at[1].set(shifted(cb[0], 'zl', 1))]
  transfers between devices with their start and end apart: 14 -> 14, of which waited for: 3 -> 3; matrix products, arithmetic and copies ran while one was open for 2% -> 1% of each run, Pallas kernels for 20% -> 20%
where the time goes in v8:
time: 84.9 us; the launch traced here: 84.4 us
  starting transfers between devices  33.6 us (40%)
  Pallas kernels  24.9 us (29%)
  blocking collectives  13.7 us (16%)
  waiting for transfers between devices  8.26 us (10%)
  local copies, waits for them, and re-layouts  1.66 us (2%)
  other arithmetic  1.58 us (2%)
    ppermute x7, starting transfers between devices, shifted(): return lax.ppermute(value, axis, [(i, (i + by) % n) for i in range(n)])  16.3 us
    all_to_all x1, blocking collectives, local(): parts = lax.all_to_all(chunk, CENTER_AXES, 0, 0, tiled=True)  13.7 us
    pallas_call x1, Pallas kernels, middle_call(): pl.pallas_call(middle_kernel, out_shape=[shape((D, M), F32), shape((16, D...  10.9 us
    ppermute x6, starting transfers between devices, plane_shift(): return lax.ppermute(value, PLANE_AXES, perm)  8.68 us
    all_to_all x1, starting transfers between devices, local(): scale = jnp.sum(lax.all_to_all(scale, SCALE_AXES, 0, 0, tiled=True), (0, 1))  8.57 us
    pallas_call x1, Pallas kernels, last_call(): pl.pallas_call(last_kernel, out_shape=[shape((2, NZ, CTR, D), F32), shape...  6.7 us
    all_to_all x1, waiting for transfers between devices, local(): scale = jnp.sum(lax.all_to_all(scale, SCALE_AXES, 0, 0, tiled=True), (0, 1))  6.5 us
    pallas_call x1, Pallas kernels, first_call(): pl.pallas_call(first_kernel, out_shape=[shape((D, M), BF), shape((8, M),...  5.64 us
  transfers between devices with their start and end apart: 14, of which 3 were waited for; matrix products, arithmetic and copies ran while one was open for 1% of the time, Pallas kernels for 20%

profile of v8, /device:TPU:1, one launch (start us, length us, event | category | flops | bytes accessed | tf_op | source)
XLA Modules:
  0.0 84.4 jit_solution(4490312001393316957)
XLA Ops:
  0.6 1.6 %prep.1 = (bf16[512,128]{1,0:T(8,128)(2,1)}, bf16[2,224,128]{2,1,0:T(8,128)(2,1)}, f32[8,128]{1,0:T(8,128)}) custom-call(bf16[256,128]{1,0:T(8,128)(2,1)} %x_ref.1, bf16[32,256]{1,0:T(8,128)(2,1)} %bitcast.40, bf16[128,128]{1,0:T(8,128)(2,1)} %c_ref.1, bf16[32,128]{1,0:T(8,128)(2,1)} %bitcast.41, bf16[32,128]{1,0:T(8,128)(2,1)} %bitcast.42, ...), custom_call_target="tpu_custom_call" | custom-call | tf_op jit(solution)/shard_map/prep/pallas_call | solution.py:287
  2.2 0.0 copy-start
  2.2 0.9 %slice_bitcast_fusion.1 = bf16[224,128]{1,0:T(8,128)(2,1)S(1)} fusion(bf16[2,224,128]{2,1,0:T(8,128)(2,1)} %get-tuple-element.26), kind=kLoop, calls=%fused_computation.8 | loop fusion | bytes 114688 | tf_op jit(solution)/shard_map/squeeze | solution.py:295
  3.1 2.5 %collective-permute-start = (bf16[224,128]{1,0:T(8,128)(2,1)S(1)}, bf16[224,128]{1,0:T(8,128)(2,1)S(1)}, u32[]{:S(2)}, u32[]{:S(2)}) collective-permute-start(bf16[224,128]{1,0:T(8,128)(2,1)S(1)} %slice_bitcast_fusion.1), channel_id=1, source_target_pairs={{0,4},{4,0},{1,5},{5,1},{2,6},{6,2},{3,7},{7,3},{8,12},{12,8},{9,1... | collective-permute-start | bytes 172040 | tf_op jit(solution)/shard_map/ppermute | solution.py:194
  5.6 1.3 %collective-permute-start.6 = (bf16[512,128]{1,0:T(8,128)(2,1)}, bf16[512,128]{1,0:T(8,128)(2,1)S(1)}, u32[]{:S(2)}, u32[]{:S(2)}) collective-permute-start(bf16[512,128]{1,0:T(8,128)(2,1)} %get-tuple-element.27.a_ref), channel_id=1, source_target_pairs={{0,1},{1,2},{2,3},{3,0},{8,24},{9,25},{10,26},{11,27},{16,17},{17,... | collective-permute-start | bytes 393224 | tf_op jit(solution)/shard_map/ppermute | solution.py:205
  6.9 1.4 %collective-permute-start.7 = (bf16[512,128]{1,0:T(8,128)(2,1)}, bf16[512,128]{1,0:T(8,128)(2,1)S(1)}, u32[]{:S(2)}, u32[]{:S(2)}) collective-permute-start(bf16[512,128]{1,0:T(8,128)(2,1)} %get-tuple-element.27.a_ref), channel_id=1, source_target_pairs={{0,3},{1,0},{2,1},{3,2},{8,56},{9,57},{10,58},{11,59},{16,19},{17,... | collective-permute-start | bytes 393224 | tf_op jit(solution)/shard_map/ppermute | solution.py:205
  8.3 1.6 %collective-permute-start.8 = (bf16[512,128]{1,0:T(8,128)(2,1)}, bf16[512,128]{1,0:T(8,128)(2,1)S(1)}, u32[]{:S(2)}, u32[]{:S(2)}) collective-permute-start(bf16[512,128]{1,0:T(8,128)(2,1)} %get-tuple-element.27.a_ref), channel_id=1, source_target_pairs={{0,2},{1,3},{2,0},{3,1},{8,40},{9,41},{10,42},{11,43},{16,18},{17,... | collective-permute-start | bytes 393224 | tf_op jit(solution)/shard_map/ppermute | solution.py:205
  10.0 0.0 collective-permute-done
  10.0 0.6 bitcast_dynamic-update-slice_fusion.h0
  10.6 3.0 %collective-permute-start.1 = (bf16[2,224,128]{2,1,0:T(8,128)(2,1)}, bf16[2,224,128]{2,1,0:T(8,128)(2,1)S(1)}, u32[]{:S(2)}, u32[]{:S(2)}) collective-permute-start(bf16[2,224,128]{2,1,0:T(8,128)(2,1)} %bitcast_dynamic-update-slice_fusion.h0), channel_id=1, source_target_pairs={{0,64},{64,128},{128,192},{192,0},{1,65},{65,129},{129,193},{193,1... | collective-permute-start | bytes 344072 | tf_op jit(solution)/shard_map/ppermute | solution.py:194
  13.6 2.1 %collective-permute-start.2 = (bf16[2,224,128]{2,1,0:T(8,128)(2,1)}, bf16[2,224,128]{2,1,0:T(8,128)(2,1)S(1)}, u32[]{:S(2)}, u32[]{:S(2)}) collective-permute-start(bf16[2,224,128]{2,1,0:T(8,128)(2,1)} %bitcast_dynamic-update-slice_fusion.h0), channel_id=1, source_target_pairs={{0,192},{64,0},{128,64},{192,128},{1,193},{65,1},{129,65},{193,129... | collective-permute-start | bytes 344072 | tf_op jit(solution)/shard_map/ppermute | solution.py:194
  15.7 0.0 collective-permute-done.6.b_ref
  15.7 4.5 %collective-permute-start.3 = (bf16[2,224,128]{2,1,0:T(8,128)(2,1)}, bf16[2,224,128]{2,1,0:T(8,128)(2,1)S(1)}, u32[]{:S(2)}, u32[]{:S(2)}) collective-permute-start(bf16[2,224,128]{2,1,0:T(8,128)(2,1)} %bitcast_dynamic-update-slice_fusion.h0), channel_id=1, source_target_pairs={{0,128},{64,192},{128,0},{192,64},{1,129},{65,193},{129,1},{193,65... | collective-permute-start | bytes 344072 | tf_op jit(solution)/shard_map/ppermute | solution.py:194
  20.2 0.0 collective-permute-done.7.c_ref
  20.2 0.0 collective-permute-done.8.d_ref
  20.2 0.0 copy-done
  20.2 0.1 pad_maximum_fusion
  20.3 2.8 %collective-permute-start.10 = (bf16[4,512,128]{2,1,0:T(8,128)(2,1)S(1)}, bf16[4,512,128]{2,1,0:T(8,128)(2,1)S(1)}, u32[]{:S(2)}, u32[]{:S(2)}) collective-permute-start(bf16[4,512,128]{2,1,0:T(8,128)(2,1)S(1)} %pad_maximum_fusion), channel_id=1, source_target_pairs={{0,32},{1,33},{2,34},{3,35},{8,10},{9,11},{10,8},{11,9},{16,48},{1... | collective-permute-start | bytes 1572872 | tf_op jit(solution)/shard_map/ppermute | solution.py:205
  23.1 0.9 %collective-permute-start.9 = (bf16[4,512,128]{2,1,0:T(8,128)(2,1)S(1)}, bf16[4,512,128]{2,1,0:T(8,128)(2,1)S(1)}, u32[]{:S(2)}, u32[]{:S(2)}) collective-permute-start(bf16[4,512,128]{2,1,0:T(8,128)(2,1)S(1)} %pad_maximum_fusion), channel_id=1, source_target_pairs={{0,48},{1,49},{2,50},{3,51},{8,11},{9,8},{10,9},{11,10},{16,0},{17... | collective-permute-start | bytes 1572872 | tf_op jit(solution)/shard_map/ppermute | solution.py:205
  23.9 0.0 collective-permute-done.1
  23.9 0.6 collective-permute-start.11
  24.6 0.0 collective-permute-done.2
  24.6 0.0 copy-start.1
  24.6 0.7 collective-permute-done.3
  25.4 3.6 %collective-permute-start.5 = (bf16[6,224,128]{2,1,0:T(8,128)(2,1)S(1)}, bf16[6,224,128]{2,1,0:T(8,128)(2,1)S(1)}, u32[]{:S(2)}, u32[]{:S(2)}) collective-permute-start(bf16[6,224,128]{2,1,0:T(8,128)(2,1)S(1)} %constant_dynamic-update-slice_fusion.h1), channel_id=1, source_target_pairs={{0,8},{8,0},{1,9},{9,1},{2,10},{10,2},{3,11},{11,3},{4,12},{12,4},... | collective-permute-start | bytes 1032200 | tf_op jit(solution)/shard_map/ppermute | solution.py:194
  29.0 0.0 copy-done.1
  29.0 0.3 collective-permute-start.4
  29.3 0.1 pad.7.clone
  29.4 0.0 copy-start.2
  29.4 0.1 pad_add_fusion.at_ref
  29.5 1.0 %collective-permute-done.4.h2 = bf16[2,224,128]{2,1,0:T(8,128)(2,1)S(1)} collective-permute-done((bf16[2,224,128]{2,1,0:T(8,128)(2,1)S(1)}, bf16[2,224,128]{2,1,0:T(8,128)(2,1)S(1)}, u32[]{:S(2)}, u32[]{:S(2)}) %collective-permute-start.4) | collective-permute-done | bytes 114720 | tf_op jit(solution)/shard_map/ppermute | solution.py:194
  30.5 0.0 collective-permute-done.5.h3
  30.5 0.0 copy-done.2
  30.5 5.6 %pairs_first.1 = (bf16[128,2048]{1,0:T(8,128)(2,1)S(1)}, f32[8,2048]{1,0:T(8,128)S(1)}, bf16[128,2048]{1,0:T(8,128)(2,1)S(1)}, f32[128,2048]{1,0:T(8,128)S(1)}, f32[16,128]{1,0:T(8,128)S(1)}) custom-call(bf16[2,224,128]{2,1,0:T(8,128)(2,1)S(1)} %copy-done.1, bf16[6,224,128]{2,1,0:T(8,128)(2,1)S(1)} %constant_dynamic-update-slice_fusion.h1, ...), custom_call_target="tpu_custom_call" | custom-call | flops 1 | bytes 1 | tf_op jit(solution)/shard_map/pairs_first/pallas_call | solution.py:238
  36.1 0.0 collective-permute-done.10.b_ref
  36.1 0.0 collective-permute-done.9.a_ref
  36.1 10.9 %pairs_middle.1 = (f32[128,2048]{1,0:T(8,128)S(1)}, f32[16,128]{1,0:T(8,128)S(1)}) custom-call(bf16[128,2048]{1,0:T(8,128)(2,1)S(1)} %get-tuple-element.29.ct, f32[8,2048]{1,0:T(8,128)S(1)} %get-tuple-element.30.hc, bf16[128,2048]{1,0:T(8,128)(2,1)S(1)} %get-tuple-element.31.ut, f32[128,2048]{1,0:T(8,128)S(1)} %get-tuple-element.32.t0, ...), custom_call_target="tpu_custom_call" | custom-call | flops 1 | bytes 1 | tf_op jit(solution)/shard_map/pairs_middle/pallas_call | solution.py:258
  47.1 0.0 collective-permute-done.11.a_ref
  47.1 6.7 %pairs_last.1 = (f32[2,8,128,128]{3,2,1,0:T(8,128)S(1)}, f32[32,1,128]{2,1,0:T(1,128)}) custom-call(s32[2]{0:T(128)S(1)} %pad_add_fusion.at_ref, bf16[128,2048]{1,0:T(8,128)(2,1)S(1)} %get-tuple-element.29.ct, f32[8,2048]{1,0:T(8,128)S(1)} %get-tuple-element.30.hc, bf16[128,2048]{1,0:T(8,128)(2,1)S(1)} %get-tuple-element.31.ut, ...), custom_call_target="tpu_custom_call" | custom-call | flops 1811939328 | bytes 4194304 | tf_op jit(solution)/shard_map/pairs_last/pallas_call | solution.py:272
  53.8 8.6 %all-to-all-start = ((f32[32,1,128]{2,1,0:T(1,128)}), f32[32,1,128]{2,1,0:T(1,128)S(1)}, u32[]{:S(2)}, u32[]{:S(2)}) async-start(f32[32,1,128]{2,1,0:T(1,128)} %get-tuple-element.37), calls=%async_computation | async-start | bytes 32768 | tf_op jit(solution)/shard_map/all_to_all | solution.py:306
  62.4 0.3 collective-permute-start.12
  62.7 6.5 %all-to-all-done = f32[32,1,128]{2,1,0:T(1,128)S(1)} async-done(((f32[32,1,128]{2,1,0:T(1,128)}), f32[32,1,128]{2,1,0:T(1,128)S(1)}, u32[]{:S(2)}, u32[]{:S(2)}) %all-to-all-start) | async-done | bytes 16416 | tf_op jit(solution)/shard_map/all_to_all | solution.py:306
  69.2 0.1 reduce_sum.29
  69.3 0.1 maximum_maximum_fusion
  69.4 0.0 collective-permute-done.12
  69.4 0.1 fusion
  69.5 13.7 %all_to_all.10 = bf16[8,144,128]{2,1,0:T(8,128)(2,1)S(1)} all-to-all(bf16[8,144,128]{2,1,0:T(8,128)(2,1)S(1)} %pad_maximum_fusion.1), channel_id=1, replica_groups=mesh['zh'=4,'y'=4,'core'=2,'zl'=2,'x'=4] {'zh','zl'}, dimensions={0} | all-to-all | bytes 589824 | tf_op jit(solution)/shard_map/all_to_all | solution.py:309
  83.2 0.5 bitcast_divide_fusion
  83.7 0.7 convert_reduce_fusion
  (10 shorter events, 0.2 us)
Async XLA Ops:
  2.2 17.9 %copy-start = (bf16[512,128]{1,0:T(8,128)(2,1)S(1)}, bf16[512,128]{1,0:T(8,128)(2,1)}, u32[]{:S(2)}) copy-start(bf16[512,128]{1,0:T(8,128)(2,1)} %get-tuple-element.27.a_ref) | copy-start | bytes 393220
  3.1 6.9 %collective-permute-start = (bf16[224,128]{1,0:T(8,128)(2,1)S(1)}, bf16[224,128]{1,0:T(8,128)(2,1)S(1)}, u32[]{:S(2)}, u32[]{:S(2)}) collective-permute-start(bf16[224,128]{1,0:T(8,128)(2,1)S(1)} %slice_bitcast_fusion.1), channel_id=1, source_target_pairs={{0,4},{4,0},{1,5},{5,1},{2,6},{6,2},{3,7},{7,3},{8,12},{12,8},{9,1... | collective-permute-start | bytes 172040 | tf_op jit(solution)/shard_map/ppermute | solution.py:194
  5.6 10.1 %collective-permute-start.6 = (bf16[512,128]{1,0:T(8,128)(2,1)}, bf16[512,128]{1,0:T(8,128)(2,1)S(1)}, u32[]{:S(2)}, u32[]{:S(2)}) collective-permute-start(bf16[512,128]{1,0:T(8,128)(2,1)} %get-tuple-element.27.a_ref), channel_id=1, source_target_pairs={{0,1},{1,2},{2,3},{3,0},{8,24},{9,25},{10,26},{11,27},{16,17},{17,... | collective-permute-start | bytes 393224 | tf_op jit(solution)/shard_map/ppermute | solution.py:205
  6.9 13.3 %collective-permute-start.7 = (bf16[512,128]{1,0:T(8,128)(2,1)}, bf16[512,128]{1,0:T(8,128)(2,1)S(1)}, u32[]{:S(2)}, u32[]{:S(2)}) collective-permute-start(bf16[512,128]{1,0:T(8,128)(2,1)} %get-tuple-element.27.a_ref), channel_id=1, source_target_pairs={{0,3},{1,0},{2,1},{3,2},{8,56},{9,57},{10,58},{11,59},{16,19},{17,... | collective-permute-start | bytes 393224 | tf_op jit(solution)/shard_map/ppermute | solution.py:205
  8.3 11.9 %collective-permute-start.8 = (bf16[512,128]{1,0:T(8,128)(2,1)}, bf16[512,128]{1,0:T(8,128)(2,1)S(1)}, u32[]{:S(2)}, u32[]{:S(2)}) collective-permute-start(bf16[512,128]{1,0:T(8,128)(2,1)} %get-tuple-element.27.a_ref), channel_id=1, source_target_pairs={{0,2},{1,3},{2,0},{3,1},{8,40},{9,41},{10,42},{11,43},{16,18},{17,... | collective-permute-start | bytes 393224 | tf_op jit(solution)/shard_map/ppermute | solution.py:205
  10.6 13.4 %collective-permute-start.1 = (bf16[2,224,128]{2,1,0:T(8,128)(2,1)}, bf16[2,224,128]{2,1,0:T(8,128)(2,1)S(1)}, u32[]{:S(2)}, u32[]{:S(2)}) collective-permute-start(bf16[2,224,128]{2,1,0:T(8,128)(2,1)} %bitcast_dynamic-update-slice_fusion.h0), channel_id=1, source_target_pairs={{0,64},{64,128},{128,192},{192,0},{1,65},{65,129},{129,193},{193,1... | collective-permute-start | bytes 344072 | tf_op jit(solution)/shard_map/ppermute | solution.py:194
  13.6 11.0 %collective-permute-start.2 = (bf16[2,224,128]{2,1,0:T(8,128)(2,1)}, bf16[2,224,128]{2,1,0:T(8,128)(2,1)S(1)}, u32[]{:S(2)}, u32[]{:S(2)}) collective-permute-start(bf16[2,224,128]{2,1,0:T(8,128)(2,1)} %bitcast_dynamic-update-slice_fusion.h0), channel_id=1, source_target_pairs={{0,192},{64,0},{128,64},{192,128},{1,193},{65,1},{129,65},{193,129... | collective-permute-start | bytes 344072 | tf_op jit(solution)/shard_map/ppermute | solution.py:194
  15.7 9.7 %collective-permute-start.3 = (bf16[2,224,128]{2,1,0:T(8,128)(2,1)}, bf16[2,224,128]{2,1,0:T(8,128)(2,1)S(1)}, u32[]{:S(2)}, u32[]{:S(2)}) collective-permute-start(bf16[2,224,128]{2,1,0:T(8,128)(2,1)} %bitcast_dynamic-update-slice_fusion.h0), channel_id=1, source_target_pairs={{0,128},{64,192},{128,0},{192,64},{1,129},{65,193},{129,1},{193,65... | collective-permute-start | bytes 344072 | tf_op jit(solution)/shard_map/ppermute | solution.py:194
  20.3 15.9 %collective-permute-start.10 = (bf16[4,512,128]{2,1,0:T(8,128)(2,1)S(1)}, bf16[4,512,128]{2,1,0:T(8,128)(2,1)S(1)}, u32[]{:S(2)}, u32[]{:S(2)}) collective-permute-start(bf16[4,512,128]{2,1,0:T(8,128)(2,1)S(1)} %pad_maximum_fusion), channel_id=1, source_target_pairs={{0,32},{1,33},{2,34},{3,35},{8,10},{9,11},{10,8},{11,9},{16,48},{1... | collective-permute-start | bytes 1572872 | tf_op jit(solution)/shard_map/ppermute | solution.py:205
  23.1 13.0 %collective-permute-start.9 = (bf16[4,512,128]{2,1,0:T(8,128)(2,1)S(1)}, bf16[4,512,128]{2,1,0:T(8,128)(2,1)S(1)}, u32[]{:S(2)}, u32[]{:S(2)}) collective-permute-start(bf16[4,512,128]{2,1,0:T(8,128)(2,1)S(1)} %pad_maximum_fusion), channel_id=1, source_target_pairs={{0,48},{1,49},{2,50},{3,51},{8,11},{9,8},{10,9},{11,10},{16,0},{17... | collective-permute-start | bytes 1572872 | tf_op jit(solution)/shard_map/ppermute | solution.py:205
  23.9 23.1 %collective-permute-start.11 = (bf16[4,512,128]{2,1,0:T(8,128)(2,1)S(1)}, bf16[4,512,128]{2,1,0:T(8,128)(2,1)S(1)}, u32[]{:S(2)}, u32[]{:S(2)}) collective-permute-start(bf16[4,512,128]{2,1,0:T(8,128)(2,1)S(1)} %pad_maximum_fusion), channel_id=1, source_target_pairs={{0,16},{1,17},{2,18},{3,19},{8,9},{9,10},{10,11},{11,8},{16,32},{1... | collective-permute-start | bytes 1572872 | tf_op jit(solution)/shard_map/ppermute | solution.py:205
  24.6 4.4 %copy-start.1 = (bf16[2,224,128]{2,1,0:T(8,128)(2,1)S(1)}, bf16[2,224,128]{2,1,0:T(8,128)(2,1)}, u32[]{:S(2)}) copy-start(bf16[2,224,128]{2,1,0:T(8,128)(2,1)} %bitcast_dynamic-update-slice_fusion.h0) | copy-start | bytes 344068
  25.4 5.1 %collective-permute-start.5 = (bf16[6,224,128]{2,1,0:T(8,128)(2,1)S(1)}, bf16[6,224,128]{2,1,0:T(8,128)(2,1)S(1)}, u32[]{:S(2)}, u32[]{:S(2)}) collective-permute-start(bf16[6,224,128]{2,1,0:T(8,128)(2,1)S(1)} %constant_dynamic-update-slice_fusion.h1), channel_id=1, source_target_pairs={{0,8},{8,0},{1,9},{9,1},{2,10},{10,2},{3,11},{11,3},{4,12},{12,4},... | collective-permute-start | bytes 1032200 | tf_op jit(solution)/shard_map/ppermute | solution.py:194
  29.0 1.4 %collective-permute-start.4 = (bf16[2,224,128]{2,1,0:T(8,128)(2,1)S(1)}, bf16[2,224,128]{2,1,0:T(8,128)(2,1)S(1)}, u32[]{:S(2)}, u32[]{:S(2)}) collective-permute-start(bf16[2,224,128]{2,1,0:T(8,128)(2,1)S(1)} %copy-done.1), channel_id=1, source_target_pairs={{0,8},{8,0},{1,9},{9,1},{2,10},{10,2},{3,11},{11,3},{4,12},{12,4},... | collective-permute-start | bytes 344072 | tf_op jit(solution)/shard_map/ppermute | solution.py:194
  29.4 1.1 %copy-start.2 = (f32[8,128]{1,0:T(8,128)S(1)}, f32[8,128]{1,0:T(8,128)}, u32[]{:S(2)}) copy-start(f32[8,128]{1,0:T(8,128)} %get-tuple-element.28.lv_ref) | copy-start | bytes 12292
  53.8 15.4 %all-to-all-start = ((f32[32,1,128]{2,1,0:T(1,128)}), f32[32,1,128]{2,1,0:T(1,128)S(1)}, u32[]{:S(2)}, u32[]{:S(2)}) async-start(f32[32,1,128]{2,1,0:T(1,128)} %get-tuple-element.37), calls=%async_computation | async-start | bytes 32768 | tf_op jit(solution)/shard_map/all_to_all | solution.py:306
  62.4 7.0 %collective-permute-start.12 = (f32[8,128,128]{2,1,0:T(8,128)S(1)}, f32[8,128,128]{2,1,0:T(8,128)S(1)}, u32[]{:S(2)}, u32[]{:S(2)}) collective-permute-start(f32[8,128,128]{2,1,0:T(8,128)S(1)} %slice_bitcast_fusion), channel_id=1, source_target_pairs={{0,8},{8,0},{1,9},{9,1},{2,10},{10,2},{3,11},{11,3},{4,12},{12,4},... | collective-permute-start | bytes 1572872 | tf_op jit(solution)/shard_map/ppermute | solution.py:194
